TPU v7x, 128 devices: a whole 4x4x4 slice. The times are simulated.
128 devices in a mesh: item: 128 (over y, x, z, core).
Axes of the slice: x: 4, y: 4, z: 4, core: 2. Of those that a mesh axis runs over, the one named last changes fastest.
Arguments:
- target_sums: float32 [64, 1572864], P(None, 'item'), may hold values from -700 to 700
- counts: int32 [1572864], P('item'), may hold values from 1 to 30
- band_offsets: int32 [12288, 4], P('item'), may hold values from -48 to 48
- band_weights: bfloat16 [12288, 4, 128, 128], P('item'), may hold values from 0 to 0.0625
- send_tiles: int32 [128, 128], P('item'), may hold values from 0 to 95
- landing_tiles: int32 [128, 128], P('item'), may hold values from 0 to 95
- remote_weights: bfloat16 [16384, 128, 128], P('item'), may hold values from 0 to 0.0625
Outputs:
- encoding: float32 [64, 1572864], P(None, 'item')
All inputs are finite; a program needn't handle non-finite values.
Results may differ from a plain program's by a relative error of at most 0.0003.
Values may be sent and summed in bfloat16 or wider, within the bound.
No kernel may reach another device: no remote copies, remote signals or barrier semaphores. Data moves between devices by JAX's collectives and lax.ppermute only.
A program may use at most 128 MiB of HBM per device.

v0:
```python
import jax
import jax.numpy as jnp
from jax import lax
from jax.sharding import PartitionSpec as P

ROUNDS = 2


prior_strength = 20.0


def shifted(shard, axis, by):
    length = lax.axis_size(axis)
    pairs = [(i, i + by) for i in range(length) if 0 <= i + by < length]
    return lax.ppermute(shard, axis, pairs)


def encode(totals, weight, mean):
    return (totals + prior_strength * mean[:, None]) / (weight[None, :] + prior_strength)


def global_sums(parts):
    return lax.psum((parts[0], parts[1]), "item")


def propagate(state, band_offsets, band_weights, send_tiles, placing, remote_weights):
    channels, columns = state.shape
    tiles_dev, band_count, tile_size = (
        band_weights.shape[0],
        band_weights.shape[1],
        band_weights.shape[2],
    )
    reach = tiles_dev // 2
    tiled = state.reshape(channels, tiles_dev, tile_size)
    below = shifted(tiled, "item", 1)
    above = shifted(tiled, "item", -1)
    window = jnp.concatenate([below[:, tiles_dev - reach :], tiled, above[:, :reach]], axis=1)
    position = band_offsets + jnp.arange(tiles_dev, dtype=jnp.int32)[:, None] + reach
    gathered = jnp.take(window, position, axis=1)
    summed = jnp.einsum(
        "cdbt,dbut->cdu", gathered, band_weights, preferred_element_type=jnp.float32
    )
    outgoing = jnp.take(tiled, send_tiles[0], axis=1)
    incoming = lax.all_to_all(outgoing, "item", split_axis=1, concat_axis=1, tiled=True)
    partial_terms = jnp.einsum(
        "cpt,put->cpu", incoming, remote_weights, preferred_element_type=jnp.float32
    )
    summed = summed + jnp.einsum(
        "cpu,pd->cdu", partial_terms, placing, precision=lax.Precision.HIGHEST
    )
    return summed.reshape(channels, columns)


def on_device(
    target_sums, counts, band_offsets, band_weights, send_tiles, landing_tiles, remote_weights
):
    tiles_dev = band_weights.shape[0]
    counts_float = counts.astype(jnp.float32)
    placing = (landing_tiles[0][:, None] == jnp.arange(tiles_dev, dtype=jnp.int32)[None, :]).astype(
        jnp.float32
    )
    band_rows = jnp.sum(band_weights, axis=(1, 3), dtype=jnp.float32)
    remote_rows = jnp.sum(remote_weights, axis=2, dtype=jnp.float32)
    landed_rows = jnp.einsum("pu,pd->du", remote_rows, placing, precision=lax.Precision.HIGHEST)
    weight = counts_float + (band_rows + landed_rows).reshape(-1)
    source_total, count_total = global_sums((jnp.sum(target_sums, axis=1), jnp.sum(counts_float)))
    state = encode(target_sums, counts_float, source_total / count_total).astype(jnp.bfloat16)
    result = None
    for round_number in range(ROUNDS):
        mixed = propagate(state, band_offsets, band_weights, send_tiles, placing, remote_weights)
        totals = target_sums + mixed
        channel_total, weight_total = global_sums((jnp.sum(totals, axis=1), jnp.sum(weight)))
        result = encode(totals, weight, channel_total / weight_total)
        state = result.astype(jnp.bfloat16)
    return result


def solution(mesh):
    return jax.shard_map(
        on_device,
        mesh=mesh,
        in_specs=(
            P(None, "item"),
            P("item"),
            P("item", None),
            P("item", None, None, None),
            P("item", None),
            P("item", None),
            P("item", None, None),
        ),
        out_specs=P(None, "item"),
        check_vma=False,
    )
```

profile of v0, /device:TPU:1, one launch (start us, length us, event | category | flops | bytes accessed | tf_op | source)
XLA Modules:
  0.0 391.3 jit_solution(7288154738532788065)
XLA Ops:
  5.2 68.8 %all-reduce.1 = (f32[64]{0:T(128)S(1)}, f32[]{:T(128)}) all-reduce(f32[64]{0:T(128)S(1)} %reduce_sum.67, f32[]{:T(128)} %get-tuple-element.13), channel_id=1, replica_groups=mesh['item'=128] {'item'}, use_global_device_ids=true, to_apply=%region_1.0 | all-reduce | flops 65 | bytes 520 | tf_op jit(solution)/shard_map/psum | solution.py:23
  76.3 3.5 gather_fusion.1
  83.0 5.6 %all-to-all-start = ((bf16[64,128,128]{2,0,1:T(8,128)(2,1)}), bf16[64,128,128]{2,0,1:T(8,128)(2,1)}, u32[]{:S(2)}, u32[]{:S(2)}) async-start(bf16[64,128,128]{2,0,1:T(8,128)(2,1)} %select_bitcast_fusion.1), calls=%async_computation | async-start | bytes 4194304 | tf_op jit(solution)/shard_map/all_to_all | solution.py:44
  88.6 3.2 collective-permute-start.1
  94.7 3.4 convert_reduce_fusion.1
  98.1 6.4 %convert_reduce_fusion = f32[96,128]{1,0:T(8,128)S(1)} fusion(bf16[96,4,128,128]{3,2,1,0:T(8,128)(2,1)} %param.14), kind=kLoop, calls=%fused_computation.4 | loop fusion | flops 12570624 | bytes 12632064 | tf_op jit(solution)/shard_map/reduce_sum | solution.py:62
  105.3 24.8 %collective-permute-done.1 = bf16[64,96,128]{2,0,1:T(8,128)(2,1)} collective-permute-done((bf16[64,96,128]{2,0,1:T(8,128)(2,1)}, bf16[64,96,128]{2,0,1:T(8,128)(2,1)}, u32[]{:S(2)}, u32[]{:S(2)}) %collective-permute-start.1) | collective-permute-done | bytes 1572896 | tf_op jit(solution)/shard_map/ppermute | solution.py:15
  134.5 5.9 %gather_fusion = bf16[384,64,128]{2,1,0:T(8,128)(2,1)} fusion(bf16[64,192,128]{2,0,1:T(8,128)(2,1)} %pad_maximum_fusion, s32[1024]{0:T(1024)S(1)} %pad_clamp_fusion.1), kind=kCustom, calls=%fused_computation.clone | custom fusion | bytes 12584448 | tf_op jit(solution)/shard_map/jit(_take)/gather | solution.py:39
  140.4 5.8 %convolution_bitcast_fusion.1 = f32[64,128,128]{2,0,1:T(8,128)S(1)} fusion(bf16[64,128,128]{2,0,1:T(8,128)(2,1)} %all-to-all-done, bf16[128,128,128]{2,1,0:T(8,128)(2,1)} %param.17), kind=kOutput, calls=%fused_computation.32 | convolution fusion | flops 268435456 | bytes 10485760 | tf_op jit(solution)/shard_map/cpt,put->cpu/dot_general | solution.py:45
  146.2 6.0 %fusion.10 = f32[96,64,128]{2,0,1:T(8,128)} fusion(f32[64,128,128]{2,0,1:T(8,128)S(1)} %convolution_bitcast_fusion.1, s32[128]{0:T(128)S(1)} %bitcast.82), kind=kOutput, calls=%fused_computation.16 | convolution fusion | flops 1207971840 | bytes 7340544 | tf_op jit(solution)/shard_map/cpu,pd->cdu/dot_general | solution.py:48
  152.2 10.4 %fusion.13 = f32[96,8,8,128]{3,2,1,0:T(8,128)S(1)} fusion(f32[96,64,128]{2,0,1:T(8,128)} %fusion.10, bf16[96,4,128,128]{3,2,1,0:T(8,128)(2,1)} %param.14, bf16[96,4,64,128]{3,2,1,0:T(8,128)(2,1)S(1)} %bitcast.80, pred[96,4]{1,0:T(8,128)(4,1)S(1)} %copy.22), kind=kOutput, calls=%fused_computation.25 | convolution fusion | flops 809238528 | bytes 25166208 | tf_op jit(solution)/shard_map/cdbt,dbut->cdu/dot_general | solution.py:40
  164.3 65.9 %all-reduce = (f32[64]{0:T(128)S(1)}, f32[]{:T(128)}) all-reduce(f32[64]{0:T(128)S(1)} %fusion.22, f32[]{:T(128)} %get-tuple-element.11), channel_id=1, replica_groups=mesh['item'=128] {'item'}, use_global_device_ids=true, to_apply=%region_5.8 | all-reduce | flops 65 | bytes 520 | tf_op jit(solution)/shard_map/psum | solution.py:23
  230.9 3.8 copy_bitcast_fusion
  234.6 3.5 gather_fusion.3
  238.2 3.2 select_bitcast_fusion
  241.3 5.5 %all-to-all-start.1 = ((bf16[64,128,128]{2,0,1:T(8,128)(2,1)}), bf16[64,128,128]{2,0,1:T(8,128)(2,1)}, u32[]{:S(2)}, u32[]{:S(2)}) async-start(bf16[64,128,128]{2,0,1:T(8,128)(2,1)} %select_bitcast_fusion), calls=%async_computation.1 | async-start | bytes 4194304 | tf_op jit(solution)/shard_map/all_to_all | solution.py:44
  246.9 3.2 collective-permute-start.3
  252.6 35.5 %collective-permute-done.3 = bf16[64,96,128]{2,0,1:T(8,128)(2,1)S(1)} collective-permute-done((bf16[64,96,128]{2,0,1:T(8,128)(2,1)}, bf16[64,96,128]{2,0,1:T(8,128)(2,1)S(1)}, u32[]{:S(2)}, u32[]{:S(2)}) %collective-permute-start.3) | collective-permute-done | bytes 1572896 | tf_op jit(solution)/shard_map/ppermute | solution.py:15
  290.3 5.9 %gather_fusion.2 = bf16[384,64,128]{2,1,0:T(8,128)(2,1)} fusion(bf16[64,192,128]{2,0,1:T(8,128)(2,1)} %pad_maximum_fusion.1, s32[1024]{0:T(1024)S(1)} %pad_clamp_fusion.1), kind=kCustom, calls=%fused_computation.2.clone | custom fusion | bytes 12584448 | tf_op jit(solution)/shard_map/jit(_take)/gather | solution.py:39
  296.2 5.8 %convolution_bitcast_fusion = f32[64,128,128]{2,0,1:T(8,128)S(1)} fusion(bf16[64,128,128]{2,0,1:T(8,128)(2,1)} %all-to-all-done.1, bf16[128,128,128]{2,1,0:T(8,128)(2,1)} %param.17), kind=kOutput, calls=%fused_computation.31 | convolution fusion | flops 268435456 | bytes 10485760 | tf_op jit(solution)/shard_map/cpt,put->cpu/dot_general | solution.py:45
  302.0 6.0 %fusion.8 = f32[96,64,128]{2,0,1:T(8,128)} fusion(f32[64,128,128]{2,0,1:T(8,128)S(1)} %convolution_bitcast_fusion, s32[128]{0:T(128)S(1)} %bitcast.83), kind=kOutput, calls=%fused_computation.14 | convolution fusion | flops 1207971840 | bytes 7340544 | tf_op jit(solution)/shard_map/cpu,pd->cdu/dot_general | solution.py:48
  308.0 10.4 %fusion.12 = f32[96,8,8,128]{3,2,1,0:T(8,128)S(1)} fusion(f32[96,64,128]{2,0,1:T(8,128)} %fusion.8, bf16[96,4,128,128]{3,2,1,0:T(8,128)(2,1)} %param.14, bf16[96,4,64,128]{3,2,1,0:T(8,128)(2,1)S(1)} %bitcast.79, pred[96,4]{1,0:T(8,128)(4,1)S(1)} %copy.22), kind=kOutput, calls=%fused_computation.23 | convolution fusion | flops 809238528 | bytes 25166208 | tf_op jit(solution)/shard_map/cdbt,dbut->cdu/dot_general | solution.py:40
  320.4 66.2 %psum.42 = f32[64]{0:T(128)S(1)} all-reduce(f32[64]{0:T(128)S(1)} %fusion.23), channel_id=1, replica_groups=mesh['item'=128] {'item'}, use_global_device_ids=true, to_apply=%region_11.14 | all-reduce | flops 64 | bytes 512 | tf_op jit(solution)/shard_map/psum | solution.py:23
  387.4 4.0 %add_divide_fusion = f32[64,12288]{1,0:T(8,128)} fusion(f32[64]{0:T(128)S(1)} %divide_multiply_fusion, f32[12288]{0:T(1024)S(1)} %get-tuple-element.12, f32[64,12288]{1,0:T(8,128)S(1)} %copy-done, f32[96,8,8,128]{3,2,1,0:T(8,128)} %copy-done.4), kind=kLoop, calls=%fused_computation.28 | loop fusion | flops 2359296 | bytes 9486592 | tf_op jit(solution)/shard_map/div | solution.py:19
  (51 shorter events, 28.6 us)
Async XLA Ops:
  0.0 74.6 %copy-start = (f32[64,12288]{1,0:T(8,128)S(1)}, f32[64,12288]{1,0:T(8,128)}, u32[]{:S(2)}) copy-start(f32[64,12288]{1,0:T(8,128)} %param.11) | copy-start | bytes 9437188
  83.0 11.3 %copy-start.8 = (s32[96,4]{0,1:T(4,128)S(1)}, s32[96,4]{0,1:T(4,128)}, u32[]{:S(2)}) copy-start(s32[96,4]{0,1:T(4,128)} %param.13) | copy-start | bytes 4612
  83.0 57.4 %all-to-all-start = ((bf16[64,128,128]{2,0,1:T(8,128)(2,1)}), bf16[64,128,128]{2,0,1:T(8,128)(2,1)}, u32[]{:S(2)}, u32[]{:S(2)}) async-start(bf16[64,128,128]{2,0,1:T(8,128)(2,1)} %select_bitcast_fusion.1), calls=%async_computation | async-start | bytes 4194304 | tf_op jit(solution)/shard_map/all_to_all | solution.py:44
  88.6 41.4 %collective-permute-start.1 = (bf16[64,96,128]{2,0,1:T(8,128)(2,1)}, bf16[64,96,128]{2,0,1:T(8,128)(2,1)}, u32[]{:S(2)}, u32[]{:S(2)}) collective-permute-start(bf16[64,96,128]{2,0,1:T(8,128)(2,1)} %copy_bitcast_fusion.1), channel_id=1, source_target_pairs={{1,0},{2,1},{3,2},{4,3},{5,4},{6,5},{7,6},{8,7},{9,8},{10,9},{11,1... | collective-permute-start | bytes 4718600 | tf_op jit(solution)/shard_map/ppermute | solution.py:15
  91.8 39.4 %collective-permute-start = (bf16[64,96,128]{2,0,1:T(8,128)(2,1)}, bf16[64,96,128]{2,0,1:T(8,128)(2,1)}, u32[]{:S(2)}, u32[]{:S(2)}) collective-permute-start(bf16[64,96,128]{2,0,1:T(8,128)(2,1)} %copy_bitcast_fusion.1), channel_id=1, source_target_pairs={{0,1},{1,2},{2,3},{3,4},{4,5},{5,6},{6,7},{7,8},{8,9},{9,10},{10,1... | collective-permute-start | bytes 4718600 | tf_op jit(solution)/shard_map/ppermute | solution.py:15
  98.1 6.4 %copy-start.7 = (s32[12288]{0:T(1024)S(1)}, s32[12288]{0:T(1024)}, u32[]{:S(2)}) copy-start(s32[12288]{0:T(1024)} %param.12) | copy-start | bytes 147460
  98.1 6.4 %copy-start.9 = (s32[1,128]{1,0:T(1,128)S(1)}, s32[1,128]{1,0:T(1,128)}, u32[]{:S(2)}) copy-start(s32[1,128]{1,0:T(1,128)} %param.16) | copy-start | bytes 1540
  104.4 28.0 %copy-start.5 = (bf16[64,96,128]{2,0,1:T(8,128)(2,1)S(1)}, bf16[64,96,128]{2,0,1:T(8,128)(2,1)}, u32[]{:S(2)}) copy-start(bf16[64,96,128]{2,0,1:T(8,128)(2,1)} %copy_bitcast_fusion.1) | copy-start | bytes 4718596
  146.2 6.0 %copy-start.2 = (bf16[384,64,128]{2,1,0:T(8,128)(2,1)S(1)}, bf16[384,64,128]{2,1,0:T(8,128)(2,1)}, u32[]{:S(2)}) copy-start(bf16[384,64,128]{2,1,0:T(8,128)(2,1)} %gather_fusion) | copy-start | bytes 18874372
  162.6 1.7 copy-start.3
  241.3 54.9 %all-to-all-start.1 = ((bf16[64,128,128]{2,0,1:T(8,128)(2,1)}), bf16[64,128,128]{2,0,1:T(8,128)(2,1)}, u32[]{:S(2)}, u32[]{:S(2)}) async-start(bf16[64,128,128]{2,0,1:T(8,128)(2,1)} %select_bitcast_fusion), calls=%async_computation.1 | async-start | bytes 4194304 | tf_op jit(solution)/shard_map/all_to_all | solution.py:44
  246.9 41.3 %copy-start.6 = (bf16[64,96,128]{2,0,1:T(8,128)(2,1)S(1)}, bf16[64,96,128]{2,0,1:T(8,128)(2,1)}, u32[]{:S(2)}) copy-start(bf16[64,96,128]{2,0,1:T(8,128)(2,1)} %copy_bitcast_fusion) | copy-start | bytes 4718596
  246.9 41.2 %collective-permute-start.3 = (bf16[64,96,128]{2,0,1:T(8,128)(2,1)}, bf16[64,96,128]{2,0,1:T(8,128)(2,1)S(1)}, u32[]{:S(2)}, u32[]{:S(2)}) collective-permute-start(bf16[64,96,128]{2,0,1:T(8,128)(2,1)} %copy_bitcast_fusion), channel_id=1, source_target_pairs={{1,0},{2,1},{3,2},{4,3},{5,4},{6,5},{7,6},{8,7},{9,8},{10,9},{11,1... | collective-permute-start | bytes 4718600 | tf_op jit(solution)/shard_map/ppermute | solution.py:15
  250.1 38.1 %collective-permute-start.2 = (bf16[64,96,128]{2,0,1:T(8,128)(2,1)}, bf16[64,96,128]{2,0,1:T(8,128)(2,1)S(1)}, u32[]{:S(2)}, u32[]{:S(2)}) collective-permute-start(bf16[64,96,128]{2,0,1:T(8,128)(2,1)} %copy_bitcast_fusion), channel_id=1, source_target_pairs={{0,1},{1,2},{2,3},{3,4},{4,5},{5,6},{6,7},{7,8},{8,9},{9,10},{10,1... | collective-permute-start | bytes 4718600 | tf_op jit(solution)/shard_map/ppermute | solution.py:15
  302.0 6.0 %copy-start.1 = (bf16[384,64,128]{2,1,0:T(8,128)(2,1)S(1)}, bf16[384,64,128]{2,1,0:T(8,128)(2,1)}, u32[]{:S(2)}) copy-start(bf16[384,64,128]{2,1,0:T(8,128)(2,1)} %gather_fusion.2) | copy-start | bytes 18874372
  318.4 1.7 copy-start.4
where the time goes:
time: 392 us; the launch traced here: 391 us
  blocking collectives  201 us (51%)
  waiting for transfers between devices  60.2 us (15%)
  matrix products  45.2 us (12%)
  other arithmetic  37.6 us (10%)
  local copies, waits for them, and re-layouts  24.7 us (6%)
  starting transfers between devices  22.5 us (6%)
    psum x3, blocking collectives, global_sums(): return lax.psum((parts[0], parts[1]), 'item')  201 us
    ppermute x4, waiting for transfers between devices, shifted(): return lax.ppermute(shard, axis, pairs)  60.2 us
    dot_general x2, matrix products, propagate(): jnp.einsum('cdbt,dbut->cdu', gathered, band_weights, preferred_element_ty...  20.8 us
    dot_general x2, matrix products, propagate(): jnp.einsum('cpu,pd->cdu', partial_terms, placing, precision=lax.Precision...  12 us
    gather x2, local copies, waits for them, and re-layouts, propagate(): gathered = jnp.take(window, position, axis=1)  11.8 us
    dot_general x2, matrix products, propagate(): jnp.einsum('cpt,put->cpu', incoming, remote_weights, preferred_element_ty...  11.6 us
    ppermute x4, starting transfers between devices, shifted(): return lax.ppermute(shard, axis, pairs)  11.4 us
    all_to_all x2, starting transfers between devices, propagate(): lax.all_to_all(outgoing, 'item', split_axis=1, concat_axis=1, tiled=True)  11.1 us
  transfers between devices with their start and end apart: 6, of which 2 were waited for; matrix products, arithmetic and copies ran while one was open for 7% of the time, Pallas kernels for 0%

commit v1 on v0

v1 whole, which is shorter than its diff:
```python
import functools

import jax
import jax.numpy as jnp
from jax import lax
from jax.experimental import pallas as pl
from jax.experimental.pallas import tpu as pltpu
from jax.sharding import PartitionSpec as P

PRIOR = 20.0
EXTRA = 8
F32 = jnp.float32
BF16 = jnp.bfloat16


def pieces(value, count):
    parts = []
    for _ in range(count):
        part = value.astype(BF16).astype(F32)
        parts.append(part)
        value = value - part
    return parts


def rows8(rows, base=None):
    width = 128
    index = lax.broadcasted_iota(jnp.int32, (EXTRA, width), 0)
    block = jnp.zeros((EXTRA, width), F32) if base is None else base
    for place, row in rows.items():
        block = jnp.where(index == place, row, block)
    return block


def to_row(column, shift=0):
    channels = column.shape[0]
    lane = lax.broadcasted_iota(jnp.int32, (channels, 128), 1)
    sub = lax.broadcasted_iota(jnp.int32, (channels, 128), 0)
    return jnp.sum(jnp.where(lane == sub + shift, column, 0.0), axis=0, keepdims=True)


def to_column(row, channels, shift=0):
    lane = lax.broadcasted_iota(jnp.int32, (channels, 128), 1)
    sub = lax.broadcasted_iota(jnp.int32, (channels, 128), 0)
    return jnp.sum(jnp.where(lane == sub + shift, row, 0.0), axis=1, keepdims=True)


def at_lane(scalar, place):
    lane = lax.broadcasted_iota(jnp.int32, (1, 128), 1)
    return jnp.where(lane == place, scalar, 0.0)


def pick_lane(row, place):
    lane = lax.broadcasted_iota(jnp.int32, (1, 128), 1)
    return jnp.sum(jnp.where(lane == place, row, 0.0), axis=1, keepdims=True)


def total(block):
    return jnp.sum(jnp.sum(block, axis=0, keepdims=True), axis=1, keepdims=True)


def stacked(top, bottom):
    return jnp.concatenate([top, bottom], axis=0).astype(BF16)


def product(tile, weights):
    return lax.dot_general(tile, weights, (((1,), (1,)), ((), ())), preferred_element_type=F32)


def fill_messages(send_ref, tiles_ref, out_ref, block, column_rows=None):
    count, rows, width = out_ref.shape
    top = jnp.zeros((rows - EXTRA, width), F32)
    if column_rows is None:
        shared = stacked(top, block)

    def step(q, carry):
        if column_rows is None:
            extra = shared
        else:
            high, low = pieces(column_rows[pl.ds(q, 1), :], 2)
            extra = stacked(top, rows8({6: high, 7: low}, block))
        out_ref[q] = tiles_ref[send_ref[q]] + extra
        return carry

    lax.fori_loop(0, count, step, 0, unroll=8)


def prep_kernel(send_ref, ts_ref, counts_ref, remote_ref, low_ref, high_ref, out_ref, tiles, columns, sums):
    step, steps = pl.program_id(0), pl.num_programs(0)
    channels = ts_ref.shape[0]
    here = low_ref.shape[0]
    group = remote_ref.shape[0]

    @pl.when(step == 0)
    def _():
        sums[...] = jnp.zeros_like(sums)

    for k in range(group):
        columns[pl.ds(step * group + k, 1), :] = jnp.sum(
            remote_ref[k].astype(F32), axis=0, keepdims=True
        )
    part = sums[...]
    for k in range(here):
        t = step * here + k
        block = ts_ref[:, k * 128 : (k + 1) * 128]
        count = counts_ref[pl.ds(t, 1), :].astype(F32)
        recip = 1.0 / (count + PRIOR)
        high, low = pieces(recip, 2)
        value = stacked(block * recip, rows8({0: high, 1: low, 2: jnp.ones_like(recip)}))
        tiles[t] = value

        @pl.when(step < steps // 2)
        def _():
            low_ref[k] = value

        @pl.when(step >= steps // 2)
        def _():
            high_ref[k] = value

        part = part + block
    sums[...] = part

    @pl.when(step == steps - 1)
    def _():
        row = to_row(jnp.sum(sums[...], axis=1, keepdims=True))
        row = row + at_lane(total(counts_ref[...].astype(F32)), channels)
        one, two, three = pieces(row, 3)
        fill_messages(send_ref, tiles, out_ref, rows8({3: one, 4: two, 5: three}), columns)


def column_kernel(offsets_ref, weights_ref, sums_ref):
    step = pl.program_id(0)
    here, band = weights_ref.shape[0], weights_ref.shape[1]
    reach = (sums_ref.shape[0] - pl.num_programs(0) * here) // 2

    @pl.when(step == 0)
    def _():
        sums_ref[...] = jnp.zeros_like(sums_ref)

    for k in range(here):
        t = step * here + k
        for b in range(band):
            at = t + offsets_ref[t * band + b] + reach
            row = jnp.sum(weights_ref[k, b].astype(F32), axis=0, keepdims=True)
            sums_ref[pl.ds(at, 1), :] += row


def band_kernel(with_ones, offsets_ref, below_ref, low_ref, high_ref, above_ref, weights_ref, out_ref, window):
    step = pl.program_id(0)
    here, band = weights_ref.shape[0], weights_ref.shape[1]
    reach, rows, width = below_ref.shape
    half = low_ref.shape[0]

    @pl.when(step == 0)
    def _():
        sub = lax.broadcasted_iota(jnp.int32, (rows, width), 0)
        begin = 0
        for ref in (below_ref, low_ref, high_ref, above_ref):

            def copy(k, carry, ref=ref, begin=begin):
                value = ref[k]
                if with_ones:
                    value = jnp.where(sub == rows - EXTRA + 2, 1.0, value.astype(F32)).astype(BF16)
                window[begin + k] = value
                return carry

            lax.fori_loop(0, ref.shape[0], copy, 0, unroll=4)
            begin += ref.shape[0]

    for k in range(here):
        t = step * here + k
        sources = [window[t + offsets_ref[t * band + b] + reach] for b in range(band)]
        matrices = [weights_ref[k, b] for b in range(band)]
        out_ref[k] = product(
            jnp.concatenate(sources, axis=1), jnp.concatenate(matrices, axis=1)
        )


def add_remote(landing_ref, in_ref, weights_ref, acc, seen):
    step = pl.program_id(0)
    group, rows, width = in_ref.shape

    @pl.when(step == 0)
    def _():
        acc[...] = jnp.zeros_like(acc)
        seen[...] = jnp.zeros_like(seen)

    gathered = seen[...]
    for k in range(group):
        value = in_ref[k]
        gathered = gathered + value.astype(F32)[rows - EXTRA :]
        acc[landing_ref[step * group + k]] += product(value, weights_ref[k])
    seen[...] = gathered


def copies(pairs, sems):
    return [pltpu.make_async_copy(a, b, sems.at[i]) for i, (a, b) in enumerate(pairs)]


def first_kernel(
    send_ref, landing_ref, in_ref, weights_ref, band_ref, ts_ref, counts_ref, mine_ref, from_below_ref,
    from_above_ref, low_ref, high_ref, out_ref, recip_ref, first_ref, acc, seen, band, ts, tiles, columns, sems,
):
    step, steps = pl.program_id(0), pl.num_programs(0)
    group, rows, width = in_ref.shape
    channels = rows - EXTRA
    count_tiles = counts_ref.shape[0]
    half = low_ref.shape[0]
    reach = (mine_ref.shape[0] - count_tiles) // 2

    @pl.when(step == 0)
    def _():
        for copy in copies(((band_ref, band), (ts_ref, ts)), sems):
            copy.start()
        columns[...] = mine_ref[reach : reach + count_tiles, :]
        columns[0:reach, :] += from_below_ref[...]
        columns[count_tiles - reach :, :] += from_above_ref[...]

    add_remote(landing_ref, in_ref, weights_ref, acc, seen)
    for k in range(group):
        tail = in_ref[k].astype(F32)[channels:]
        columns[pl.ds(send_ref[step * group + k], 1), :] += tail[6:7] + tail[7:8]

    @pl.when(step == steps - 1)
    def _():
        for copy in copies(((band_ref, band), (ts_ref, ts)), sems):
            copy.wait()
        known = seen[3:4, :] + seen[4:5, :] + seen[5:6, :]
        count_total = pick_lane(known, channels)
        first = PRIOR * to_column(known, channels) / count_total
        first_ref[...] = jnp.broadcast_to(known, first_ref.shape)
        zero = jnp.zeros((channels, width), F32)
        line = jnp.zeros((1, width), F32)
        carry = (zero, zero, line, line)
        for begin, ref in ((0, low_ref), (half, high_ref)):

            def finish(k, carry, begin=begin, ref=ref):
                t = begin + k
                all_totals, all_states, all_weights, all_recips = carry
                mixed = acc[t] + band[t]
                spread = mixed[channels : channels + 1] + mixed[channels + 1 : channels + 2]
                at = pl.ds(pl.multiple_of(t * width, width), width)
                totals = ts[:, at] + mixed[:channels] + first * spread
                weight = counts_ref[pl.ds(t, 1), :].astype(F32) + mixed[channels + 2 : channels + 3]
                recip = 1.0 / (weight + PRIOR)
                recip_ref[pl.ds(t, 1), :] = recip
                high, low = pieces(recip, 2)
                state = (totals * recip).astype(BF16).astype(F32)
                value = stacked(state, rows8({0: high, 1: low}))
                ref[k] = value
                tiles[t] = value
                column = columns[pl.ds(t, 1), :]
                return (
                    all_totals + totals,
                    all_states + state * column,
                    all_weights + weight,
                    all_recips + (high + low) * column,
                )

            carry = lax.fori_loop(0, half, finish, carry, unroll=4)
        all_totals, all_states, all_weights, all_recips = carry
        row = to_row(jnp.sum(all_totals, axis=1, keepdims=True))
        row = row + to_row(jnp.sum(all_states, axis=1, keepdims=True), channels)
        scalars = at_lane(total(all_weights), 0) + at_lane(total(all_recips), 1)
        one, two, three = pieces(row, 3)
        uno, due, tre = pieces(scalars, 3)
        fill_messages(
            send_ref, tiles, out_ref, rows8({2: uno, 3: one, 4: two, 5: three, 6: due, 7: tre})
        )


def last_kernel(
    landing_ref, in_ref, weights_ref, band_ref, ts_ref, recip_ref, first_ref, out_ref, acc, seen, band, ts, sems
):
    step, steps = pl.program_id(0), pl.num_programs(0)
    group, rows, width = in_ref.shape
    channels = rows - EXTRA
    count_tiles = recip_ref.shape[0]

    @pl.when(step == 0)
    def _():
        for copy in copies(((band_ref, band), (ts_ref, ts)), sems):
            copy.start()

    add_remote(landing_ref, in_ref, weights_ref, acc, seen)

    @pl.when(step == steps - 1)
    def _():
        for copy in copies(((band_ref, band), (ts_ref, ts)), sems):
            copy.wait()
        known = seen[3:4, :] + seen[4:5, :] + seen[5:6, :]
        scalars = seen[2:3, :] + seen[6:7, :] + seen[7:8, :]
        weight_total, spread_total = pick_lane(scalars, 0), pick_lane(scalars, 1)
        mean = PRIOR * to_column(known, channels) / weight_total
        mixed_total = to_column(known, channels, channels) + mean * spread_total
        last = PRIOR * (to_column(first_ref[0:1, :], channels) + mixed_total) / weight_total

        def finish(t, carry):
            mixed = acc[t] + band[t]
            spread = mixed[channels : channels + 1] + mixed[channels + 1 : channels + 2]
            at = pl.ds(pl.multiple_of(t * width, width), width)
            totals = ts[:, at] + mixed[:channels] + mean * spread
            out_ref[:, at] = (totals + last) * recip_ref[pl.ds(t, 1), :]
            return carry

        lax.fori_loop(0, count_tiles, finish, 0, unroll=4)


def params(mib):
    return pltpu.CompilerParams(vmem_limit_bytes=mib * 2**20)


def cost(flops, size):
    return pl.CostEstimate(flops=flops, bytes_accessed=size, transcendentals=0)


def whole(shape):
    zeros = (0,) * len(shape)
    return pl.BlockSpec(shape, lambda *_: zeros)


ANY = pl.BlockSpec(memory_space=pl.ANY)


def on_device(target_sums, counts, band_offsets, band_weights, send_tiles, landing_tiles, remote_weights):
    channels, columns = target_sums.shape
    count_tiles, band, width, _ = band_weights.shape
    shards = remote_weights.shape[0]
    rows = channels + EXTRA
    reach = count_tiles // 2
    half = count_tiles // 2
    counts = counts.reshape(count_tiles, width)
    send, landing, offsets = send_tiles.reshape(-1), landing_tiles.reshape(-1), band_offsets.reshape(-1)
    steps = 8
    here, group = count_tiles // steps, shards // steps
    tile_shape = jax.ShapeDtypeStruct((half, rows, width), BF16)
    message_shape = jax.ShapeDtypeStruct((shards, rows, width), BF16)
    up = [(i, i + 1) for i in range(shards - 1)]
    down = [(i + 1, i) for i in range(shards - 1)]
    sums_shape = (count_tiles + 2 * reach, width)

    low, high, outgoing = pl.pallas_call(
        prep_kernel,
        grid_spec=pltpu.PrefetchScalarGridSpec(
            num_scalar_prefetch=1,
            grid=(steps,),
            in_specs=[
                pl.BlockSpec((channels, here * width), lambda i, *_: (0, i)),
                whole((count_tiles, width)),
                pl.BlockSpec((group, width, width), lambda i, *_: (i, 0, 0)),
            ],
            out_specs=[
                pl.BlockSpec((here, rows, width), lambda i, *_: (jnp.minimum(i, steps // 2 - 1), 0, 0)),
                pl.BlockSpec((here, rows, width), lambda i, *_: (jnp.maximum(i - steps // 2, 0), 0, 0)),
                whole((shards, rows, width)),
            ],
            scratch_shapes=[
                pltpu.VMEM((count_tiles, rows, width), BF16),
                pltpu.VMEM((shards, width), F32),
                pltpu.VMEM((channels, width), F32),
            ],
        ),
        out_shape=[tile_shape, tile_shape, message_shape],
        compiler_params=params(24),
        cost_estimate=cost(10**6, 12 * 10**6),
        name="prep",
    )(send, target_sums, counts, remote_weights)

    def exchange(low, high, outgoing):
        below = lax.ppermute(high, "item", up)
        above = lax.ppermute(low, "item", down)
        incoming = lax.all_to_all(outgoing, "item", split_axis=0, concat_axis=0, tiled=True)
        return below, above, incoming

    band_steps = 12
    band_here = count_tiles // band_steps

    def band_product(with_ones, below, low, high, above):
        return pl.pallas_call(
            functools.partial(band_kernel, with_ones),
            grid_spec=pltpu.PrefetchScalarGridSpec(
                num_scalar_prefetch=1,
                grid=(band_steps,),
                in_specs=[whole((half, rows, width))] * 4
                + [pl.BlockSpec((band_here, band, width, width), lambda i, *_: (i, 0, 0, 0))],
                out_specs=pl.BlockSpec((band_here, rows, width), lambda i, *_: (i, 0, 0)),
                scratch_shapes=[pltpu.VMEM((count_tiles + 2 * reach, rows, width), BF16)],
            ),
            out_shape=jax.ShapeDtypeStruct((count_tiles, rows, width), F32),
            compiler_params=params(24),
            cost_estimate=cost(2 * 384 * 72 * 128 * 128, 20 * 10**6),
            name="band",
        )(offsets, below, low, high, above, band_weights)

    below, above, incoming = exchange(low, high, outgoing)

    column_sums = pl.pallas_call(
        column_kernel,
        grid_spec=pltpu.PrefetchScalarGridSpec(
            num_scalar_prefetch=1,
            grid=(band_steps,),
            in_specs=[pl.BlockSpec((band_here, band, width, width), lambda i, *_: (i, 0, 0, 0))],
            out_specs=whole(sums_shape),
        ),
        out_shape=jax.ShapeDtypeStruct(sums_shape, F32),
        compiler_params=params(16),
        cost_estimate=cost(10**6, 13 * 10**6),
        name="column",
    )(offsets, band_weights)
    from_below = lax.ppermute(column_sums[reach + count_tiles :], "item", up)
    from_above = lax.ppermute(column_sums[:reach], "item", down)

    mixed = band_product(True, below, low, high, above)

    remote_specs = [
        pl.BlockSpec((group, rows, width), lambda i, *_: (i, 0, 0)),
        pl.BlockSpec((group, width, width), lambda i, *_: (i, 0, 0)),
    ]
    common_scratch = [
        pltpu.VMEM((count_tiles, rows, width), F32),
        pltpu.VMEM((EXTRA, width), F32),
        pltpu.VMEM((count_tiles, rows, width), F32),
        pltpu.VMEM((channels, columns), F32),
    ]
    low, high, outgoing, recip, first = pl.pallas_call(
        first_kernel,
        grid_spec=pltpu.PrefetchScalarGridSpec(
            num_scalar_prefetch=2,
            grid=(steps,),
            in_specs=remote_specs
            + [
                ANY,
                ANY,
                whole((count_tiles, width)),
                whole(sums_shape),
                whole((reach, width)),
                whole((reach, width)),
            ],
            out_specs=[
                whole((half, rows, width)),
                whole((half, rows, width)),
                whole((shards, rows, width)),
                whole((count_tiles, width)),
                whole((8, width)),
            ],
            scratch_shapes=common_scratch
            + [
                pltpu.VMEM((count_tiles, rows, width), BF16),
                pltpu.VMEM((count_tiles, width), F32),
                pltpu.SemaphoreType.DMA((2,)),
            ],
        ),
        out_shape=[
            tile_shape,
            tile_shape,
            message_shape,
            jax.ShapeDtypeStruct((count_tiles, width), F32),
            jax.ShapeDtypeStruct((8, width), F32),
        ],
        compiler_params=params(40),
        cost_estimate=cost(2 * 128 * 72 * 128 * 128, 20 * 10**6),
        name="first",
    )(send, landing, incoming, remote_weights, mixed, target_sums, counts, column_sums, from_below, from_above)

    below, above, incoming = exchange(low, high, outgoing)
    mixed = band_product(False, below, low, high, above)
    return pl.pallas_call(
        last_kernel,
        grid_spec=pltpu.PrefetchScalarGridSpec(
            num_scalar_prefetch=1,
            grid=(steps,),
            in_specs=remote_specs + [ANY, ANY, whole((count_tiles, width)), whole((8, width))],
            out_specs=whole((channels, columns)),
            scratch_shapes=common_scratch + [pltpu.SemaphoreType.DMA((2,))],
        ),
        out_shape=jax.ShapeDtypeStruct((channels, columns), F32),
        compiler_params=params(40),
        cost_estimate=cost(2 * 128 * 72 * 128 * 128, 20 * 10**6),
        name="last",
    )(landing, incoming, remote_weights, mixed, target_sums, recip, first)


def solution(mesh):
    return jax.shard_map(
        on_device,
        mesh=mesh,
        in_specs=(
            P(None, "item"),
            P("item"),
            P("item", None),
            P("item", None, None, None),
            P("item", None),
            P("item", None),
            P("item", None, None),
        ),
        out_specs=P(None, "item"),
        check_vma=False,
    )
```

time: 392 us -> 169 us (0.43)
  blocking collectives: 201 us -> 0 us
  Pallas kernels: 0 us -> 47 us
  matrix products: 45.2 us -> 0 us
  other arithmetic: 37.6 us -> 0 us
  starting transfers between devices: 22.5 us -> 37.8 us
  waiting for transfers between devices: 60.2 us -> 50.7 us
  local copies, waits for them, and re-layouts: 24.7 us -> 30.2 us
    psum x3 -> x0, blocking collectives: 201 us -> none  [global_sums(): return lax.psum((parts[0], parts[1]), 'item')]
    pallas_call x0 -> x6, Pallas kernels: none -> 47 us  [the longest x2 16 us: band_product(): pl.pallas_call(functools.partial(band_kernel, with_ones), grid_spec=pltpu...]
    dot_general x7 -> x0, matrix products: 45.2 us -> none  [the longest x2 20.8 us: propagate(): jnp.einsum('cdbt,dbut->cdu', gathered, band_weights, preferred_element_ty...]
    unnamed x20 -> x45, local copies, waits for them, and re-layouts: 2.97 us -> 30.1 us
    gather x4 -> x0, local copies, waits for them, and re-layouts: 18.9 us -> none  [the longest x2 11.8 us: propagate(): gathered = jnp.take(window, position, axis=1)]
    reduce_sum x6 -> x0, other arithmetic: 14 us -> none  [the longest x1 6.35 us: on_device(): band_rows = jnp.sum(band_weights, axis=(1, 3), dtype=jnp.float32)]
    all_to_all x2, starting transfers between devices: 11.1 us -> 20.7 us  [exchange(): lax.all_to_all(outgoing, 'item', split_axis=0, concat_axis=0, tiled=True)]
    ppermute x4 -> x6, waiting for transfers between devices: 60.2 us -> 50.7 us  [the longest x2 47 us: exchange(): below = lax.ppermute(high, 'item', up)]
  transfers between devices with their start and end apart: 6 -> 8, of which waited for: 2 -> 4; matrix products, arithmetic and copies ran while one was open for 7% -> 0% of each run, Pallas kernels for 0% -> 11%
where the time goes in v1:
time: 169 us; the launch traced here: 166 us
  waiting for transfers between devices  50.7 us (30%)
  Pallas kernels  47 us (28%)
  starting transfers between devices  37.8 us (22%)
  local copies, waits for them, and re-layouts  30.2 us (18%)
    ppermute x2, waiting for transfers between devices, exchange(): below = lax.ppermute(high, 'item', up)  47 us
    unnamed x45, local copies, waits for them, and re-layouts  30.1 us
    all_to_all x2, starting transfers between devices, exchange(): lax.all_to_all(outgoing, 'item', split_axis=0, concat_axis=0, tiled=True)  20.7 us
    pallas_call x2, Pallas kernels, band_product(): pl.pallas_call(functools.partial(band_kernel, with_ones), grid_spec=pltpu...  16 us
    pallas_call x1, Pallas kernels, on_device(): pl.pallas_call(first_kernel, grid_spec=pltpu.PrefetchScalarGridSpec(num_s...  10.9 us
    pallas_call x1, Pallas kernels, on_device(): pl.pallas_call(last_kernel, grid_spec=pltpu.PrefetchScalarGridSpec(num_sc...  10.7 us
    ppermute x2, starting transfers between devices, exchange(): below = lax.ppermute(high, 'item', up)  7.32 us
    pallas_call x1, Pallas kernels, on_device(): pl.pallas_call(prep_kernel, grid_spec=pltpu.PrefetchScalarGridSpec(num_sc...  6.59 us
  transfers between devices with their start and end apart: 8, of which 4 were waited for; matrix products, arithmetic and copies ran while one was open for 0% of the time, Pallas kernels for 11%

profile of v1, /device:TPU:1, one launch (start us, length us, event | category | flops | bytes accessed | tf_op | source)
XLA Modules:
  0.0 165.9 jit_solution(7860174415635960473)
XLA Ops:
  0.0 2.2 %copy-done.3 = bf16[128,128,128]{2,1,0:T(8,128)(2,1)S(1)} copy-done((bf16[128,128,128]{2,1,0:T(8,128)(2,1)S(1)}, bf16[128,128,128]{2,1,0:T(8,128)(2,1)}, u32[]{:S(2)}) %copy-start.3) | copy-done | bytes 4194328
  2.2 1.9 %copy-done.5 = f32[64,12288]{1,0:T(8,128)S(1)} copy-done((f32[64,12288]{1,0:T(8,128)S(1)}, f32[64,12288]{1,0:T(8,128)}, u32[]{:S(2)}) %copy-start.5) | copy-done | bytes 3145752
  5.5 6.6 %prep.1 = (bf16[48,72,128]{2,1,0:T(8,128)(2,1)}, bf16[48,72,128]{2,1,0:T(8,128)(2,1)}, bf16[128,72,128]{2,1,0:T(8,128)(2,1)}) custom-call(s32[128]{0:T(128)S(1)} %bitcast.7, f32[64,12288]{1,0:T(8,128)S(1)} %copy-done.5, s32[96,128]{1,0:T(8,128)S(1)} %bitcast.3, bf16[128,128,128]{2,1,0:T(8,128)(2,1)S(1)} %copy-done.3), custom_call_target="tpu_custom_call" | custom-call | flops 1000000 | bytes 12000000 | tf_op jit(solution)/shard_map/prep/pallas_call | solution.py:341
  12.1 11.9 %all-to-all-start = ((bf16[128,72,128]{2,1,0:T(8,128)(2,1)}), bf16[128,72,128]{2,1,0:T(8,128)(2,1)}, u32[]{:S(2)}, u32[]{:S(2)}) async-start(bf16[128,72,128]{2,1,0:T(8,128)(2,1)} %get-tuple-element.13), calls=%async_computation | async-start | bytes 4718592 | tf_op jit(solution)/shard_map/all_to_all | solution.py:371
  24.0 3.7 %collective-permute-start = (bf16[48,72,128]{2,1,0:T(8,128)(2,1)}, bf16[48,72,128]{2,1,0:T(8,128)(2,1)}, u32[]{:S(2)}, u32[]{:S(2)}) collective-permute-start(bf16[48,72,128]{2,1,0:T(8,128)(2,1)} %get-tuple-element.14.high_ref), channel_id=1, source_target_pairs={{0,1},{1,2},{2,3},{3,4},{4,5},{5,6},{6,7},{7,8},{8,9},{9,10},{10,1... | collective-permute-start | bytes 2654216 | tf_op jit(solution)/shard_map/ppermute | solution.py:369
  27.7 1.9 %collective-permute-start.1 = (bf16[48,72,128]{2,1,0:T(8,128)(2,1)}, bf16[48,72,128]{2,1,0:T(8,128)(2,1)}, u32[]{:S(2)}, u32[]{:S(2)}) collective-permute-start(bf16[48,72,128]{2,1,0:T(8,128)(2,1)} %get-tuple-element.15.low_ref), channel_id=1, source_target_pairs={{1,0},{2,1},{3,2},{4,3},{5,4},{6,5},{7,6},{8,7},{9,8},{10,9},{11,1... | collective-permute-start | bytes 2654216 | tf_op jit(solution)/shard_map/ppermute | solution.py:370
  29.9 4.6 %copy-done = bf16[96,4,128,128]{3,2,1,0:T(8,128)(2,1)S(1)} copy-done((bf16[96,4,128,128]{3,2,1,0:T(8,128)(2,1)S(1)}, bf16[96,4,128,128]{3,2,1,0:T(8,128)(2,1)}, u32[]{:S(2)}) %copy-start) | copy-done | bytes 12582936
  34.4 2.8 %column.1.mine_ref = f32[192,128]{1,0:T(8,128)S(1)} custom-call(s32[384]{0:T(512)S(1)} %reshape.15.offsets_ref, bf16[96,4,128,128]{3,2,1,0:T(8,128)(2,1)S(1)} %copy-done), custom_call_target="tpu_custom_call" | custom-call | flops 1000000 | bytes 13000000 | tf_op jit(solution)/shard_map/column/pallas_call | solution.py:396
  37.3 2.1 %collective-permute-start.3 = (f32[48,128]{1,0:T(8,128)S(1)}, f32[48,128]{1,0:T(8,128)S(1)}, u32[]{:S(2)}, u32[]{:S(2)}) collective-permute-start(f32[48,128]{1,0:T(8,128)S(1)} %get-tuple-element.21), channel_id=1, source_target_pairs={{1,0},{2,1},{3,2},{4,3},{5,4},{6,5},{7,6},{8,7},{9,8},{10,9},{11,1... | collective-permute-start | bytes 73736 | tf_op jit(solution)/shard_map/ppermute | solution.py:410
  39.4 3.9 %collective-permute-start.2 = (f32[48,128]{1,0:T(8,128)S(1)}, f32[48,128]{1,0:T(8,128)S(1)}, u32[]{:S(2)}, u32[]{:S(2)}) collective-permute-start(f32[48,128]{1,0:T(8,128)S(1)} %get-tuple-element.22), channel_id=1, source_target_pairs={{0,1},{1,2},{2,3},{3,4},{4,5},{5,6},{6,7},{7,8},{8,9},{9,10},{10,1... | collective-permute-start | bytes 73736 | tf_op jit(solution)/shard_map/ppermute | solution.py:409
  43.3 16.7 %collective-permute-done.below_ref = bf16[48,72,128]{2,1,0:T(8,128)(2,1)} collective-permute-done((bf16[48,72,128]{2,1,0:T(8,128)(2,1)}, bf16[48,72,128]{2,1,0:T(8,128)(2,1)}, u32[]{:S(2)}, u32[]{:S(2)}) %collective-permute-start) | collective-permute-done | bytes 884768 | tf_op jit(solution)/shard_map/ppermute | solution.py:369
  60.0 1.9 %collective-permute-done.1.above_ref = bf16[48,72,128]{2,1,0:T(8,128)(2,1)} collective-permute-done((bf16[48,72,128]{2,1,0:T(8,128)(2,1)}, bf16[48,72,128]{2,1,0:T(8,128)(2,1)}, u32[]{:S(2)}, u32[]{:S(2)}) %collective-permute-start.1) | collective-permute-done | bytes 884768 | tf_op jit(solution)/shard_map/ppermute | solution.py:370
  61.8 9.3 %band.2.band_ref = f32[96,72,128]{2,1,0:T(8,128)S(1)} custom-call(s32[384]{0:T(512)S(1)} %reshape.15.offsets_ref, bf16[48,72,128]{2,1,0:T(8,128)(2,1)} %collective-permute-done.below_ref, bf16[48,72,128]{2,1,0:T(8,128)(2,1)} %get-tuple-element.15.low_ref, bf16[48,72,128]{2,1,0:T(8,128)(2,1)} %get-tuple-element.14.high_ref, ...), custom_call_target="tpu_custom_call" | custom-call | flops 905969664 | bytes 20000000 | tf_op jit(solution)/shard_map/band/pallas_call | solution.py:378
  72.9 2.0 %copy-done.10 = f32[96,72,128]{2,1,0:T(8,128)S(1)} copy-done((f32[96,72,128]{2,1,0:T(8,128)S(1)}, f32[96,72,128]{2,1,0:T(8,128)}, u32[]{:S(2)}) %copy-start.10) | copy-done | bytes 3538968
  74.9 10.9 %first.1 = (bf16[48,72,128]{2,1,0:T(8,128)(2,1)S(1)}, bf16[48,72,128]{2,1,0:T(8,128)(2,1)S(1)}, bf16[128,72,128]{2,1,0:T(8,128)(2,1)S(1)}, f32[96,128]{1,0:T(8,128)S(1)}, f32[8,128]{1,0:T(8,128)S(1)}) custom-call(s32[128]{0:T(128)S(1)} %bitcast.8, s32[128]{0:T(128)S(1)} %bitcast.5, bf16[128,72,128]{2,1,0:T(8,128)(2,1)} %all-to-all-done.in_ref, ...), custom_call_target="tpu_custom_call" | custom-call | flops 301989888 | bytes 20000000 | tf_op jit(solution)/shard_map/first/pallas_call | solution.py:424
  89.1 8.8 %all-to-all-start.1 = ((bf16[128,72,128]{2,1,0:T(8,128)(2,1)}), bf16[128,72,128]{2,1,0:T(8,128)(2,1)}, u32[]{:S(2)}, u32[]{:S(2)}) async-start(bf16[128,72,128]{2,1,0:T(8,128)(2,1)} %copy-done.11), calls=%async_computation.1 | async-start | bytes 4718592 | tf_op jit(solution)/shard_map/all_to_all | solution.py:371
  97.9 3.7 %collective-permute-start.4 = (bf16[48,72,128]{2,1,0:T(8,128)(2,1)}, bf16[48,72,128]{2,1,0:T(8,128)(2,1)S(1)}, u32[]{:S(2)}, u32[]{:S(2)}) collective-permute-start(bf16[48,72,128]{2,1,0:T(8,128)(2,1)} %copy-done.14), channel_id=1, source_target_pairs={{0,1},{1,2},{2,3},{3,4},{4,5},{5,6},{6,7},{7,8},{8,9},{9,10},{10,1... | collective-permute-start | bytes 2654216 | tf_op jit(solution)/shard_map/ppermute | solution.py:369
  101.5 1.9 %collective-permute-start.5 = (bf16[48,72,128]{2,1,0:T(8,128)(2,1)}, bf16[48,72,128]{2,1,0:T(8,128)(2,1)S(1)}, u32[]{:S(2)}, u32[]{:S(2)}) collective-permute-start(bf16[48,72,128]{2,1,0:T(8,128)(2,1)} %copy-done.12), channel_id=1, source_target_pairs={{1,0},{2,1},{3,2},{4,3},{5,4},{6,5},{7,6},{8,7},{9,8},{10,9},{11,1... | collective-permute-start | bytes 2654216 | tf_op jit(solution)/shard_map/ppermute | solution.py:370
  103.5 30.3 %collective-permute-done.4.below_ref = bf16[48,72,128]{2,1,0:T(8,128)(2,1)S(1)} collective-permute-done((bf16[48,72,128]{2,1,0:T(8,128)(2,1)}, bf16[48,72,128]{2,1,0:T(8,128)(2,1)S(1)}, u32[]{:S(2)}, u32[]{:S(2)}) %collective-permute-start.4) | collective-permute-done | bytes 884768 | tf_op jit(solution)/shard_map/ppermute | solution.py:369
  135.6 4.6 %copy-done.2 = bf16[96,4,128,128]{3,2,1,0:T(8,128)(2,1)S(1)} copy-done((bf16[96,4,128,128]{3,2,1,0:T(8,128)(2,1)S(1)}, bf16[96,4,128,128]{3,2,1,0:T(8,128)(2,1)}, u32[]{:S(2)}) %copy-start.2) | copy-done | bytes 12582936
  142.5 6.8 %band.3.band_ref = f32[96,72,128]{2,1,0:T(8,128)S(1)} custom-call(s32[384]{0:T(512)S(1)} %reshape.15.offsets_ref, bf16[48,72,128]{2,1,0:T(8,128)(2,1)S(1)} %collective-permute-done.4.below_ref, bf16[48,72,128]{2,1,0:T(8,128)(2,1)S(1)} %copy-done.13, bf16[48,72,128]{2,1,0:T(8,128)(2,1)S(1)} %copy-done.15, ...), custom_call_target="tpu_custom_call" | custom-call | flops 905969664 | bytes 20000000 | tf_op jit(solution)/shard_map/band/pallas_call | solution.py:378
  151.0 2.2 %copy-done.4 = bf16[128,128,128]{2,1,0:T(8,128)(2,1)S(1)} copy-done((bf16[128,128,128]{2,1,0:T(8,128)(2,1)S(1)}, bf16[128,128,128]{2,1,0:T(8,128)(2,1)}, u32[]{:S(2)}) %copy-start.4) | copy-done | bytes 4194328
  153.2 2.0 %copy-done.8 = f32[96,72,128]{2,1,0:T(8,128)S(1)} copy-done((f32[96,72,128]{2,1,0:T(8,128)S(1)}, f32[96,72,128]{2,1,0:T(8,128)}, u32[]{:S(2)}) %copy-start.8) | copy-done | bytes 3538968
  155.2 10.7 %last.1 = f32[64,12288]{1,0:T(8,128)} custom-call(s32[128]{0:T(128)S(1)} %bitcast.6, bf16[128,72,128]{2,1,0:T(8,128)(2,1)} %all-to-all-done.1.in_ref, bf16[128,128,128]{2,1,0:T(8,128)(2,1)S(1)} %copy-done.4, f32[96,72,128]{2,1,0:T(8,128)S(1)} %copy-done.8, f32[64,12288]{1,0:T(8,128)S(1)} %copy-done.6, f32[96,128]{1,0:T(8,128)S(1)} %get-tuple-element.19.recip_ref, ...), custom_call_target="tpu_custom_call" | custom-call | flops 301989888 | bytes 20000000 | tf_op jit(solution)/shard_map/last/pallas_call | solution.py:466
  (45 shorter events, 12.6 us)
Async XLA Ops:
  0.0 2.2 %copy-start.3 = (bf16[128,128,128]{2,1,0:T(8,128)(2,1)S(1)}, bf16[128,128,128]{2,1,0:T(8,128)(2,1)}, u32[]{:S(2)}) copy-start(bf16[128,128,128]{2,1,0:T(8,128)(2,1)} %weights_ref.9) | copy-start | bytes 12582916
  2.2 1.9 %copy-start.5 = (f32[64,12288]{1,0:T(8,128)S(1)}, f32[64,12288]{1,0:T(8,128)}, u32[]{:S(2)}) copy-start(f32[64,12288]{1,0:T(8,128)} %ts_ref.5) | copy-start | bytes 9437188
  12.1 17.5 %copy-start.21 = (s32[96,4]{0,1:T(4,128)S(1)}, s32[96,4]{0,1:T(4,128)}, u32[]{:S(2)}) copy-start(s32[96,4]{0,1:T(4,128)} %param.9) | copy-start | bytes 4612
  12.1 60.7 %all-to-all-start = ((bf16[128,72,128]{2,1,0:T(8,128)(2,1)}), bf16[128,72,128]{2,1,0:T(8,128)(2,1)}, u32[]{:S(2)}, u32[]{:S(2)}) async-start(bf16[128,72,128]{2,1,0:T(8,128)(2,1)} %get-tuple-element.13), calls=%async_computation | async-start | bytes 4718592 | tf_op jit(solution)/shard_map/all_to_all | solution.py:371
  24.0 35.9 %collective-permute-start = (bf16[48,72,128]{2,1,0:T(8,128)(2,1)}, bf16[48,72,128]{2,1,0:T(8,128)(2,1)}, u32[]{:S(2)}, u32[]{:S(2)}) collective-permute-start(bf16[48,72,128]{2,1,0:T(8,128)(2,1)} %get-tuple-element.14.high_ref), channel_id=1, source_target_pairs={{0,1},{1,2},{2,3},{3,4},{4,5},{5,6},{6,7},{7,8},{8,9},{9,10},{10,1... | collective-permute-start | bytes 2654216 | tf_op jit(solution)/shard_map/ppermute | solution.py:369
  27.7 34.1 %collective-permute-start.1 = (bf16[48,72,128]{2,1,0:T(8,128)(2,1)}, bf16[48,72,128]{2,1,0:T(8,128)(2,1)}, u32[]{:S(2)}, u32[]{:S(2)}) collective-permute-start(bf16[48,72,128]{2,1,0:T(8,128)(2,1)} %get-tuple-element.15.low_ref), channel_id=1, source_target_pairs={{1,0},{2,1},{3,2},{4,3},{5,4},{6,5},{7,6},{8,7},{9,8},{10,9},{11,1... | collective-permute-start | bytes 2654216 | tf_op jit(solution)/shard_map/ppermute | solution.py:370
  29.8 4.6 %copy-start = (bf16[96,4,128,128]{3,2,1,0:T(8,128)(2,1)S(1)}, bf16[96,4,128,128]{3,2,1,0:T(8,128)(2,1)}, u32[]{:S(2)}) copy-start(bf16[96,4,128,128]{3,2,1,0:T(8,128)(2,1)} %weights_ref.8) | copy-start | bytes 37748740
  34.4 27.4 %copy-start.1 = (bf16[96,4,128,128]{3,2,1,0:T(8,128)(2,1)S(1)}, bf16[96,4,128,128]{3,2,1,0:T(8,128)(2,1)}, u32[]{:S(2)}) copy-start(bf16[96,4,128,128]{3,2,1,0:T(8,128)(2,1)} %weights_ref.8) | copy-start | bytes 37748740
  37.3 35.6 %collective-permute-start.3 = (f32[48,128]{1,0:T(8,128)S(1)}, f32[48,128]{1,0:T(8,128)S(1)}, u32[]{:S(2)}, u32[]{:S(2)}) collective-permute-start(f32[48,128]{1,0:T(8,128)S(1)} %get-tuple-element.21), channel_id=1, source_target_pairs={{1,0},{2,1},{3,2},{4,3},{5,4},{6,5},{7,6},{8,7},{9,8},{10,9},{11,1... | collective-permute-start | bytes 73736 | tf_op jit(solution)/shard_map/ppermute | solution.py:410
  39.3 33.5 %copy-start.6 = (f32[64,12288]{1,0:T(8,128)S(1)}, f32[64,12288]{1,0:T(8,128)}, u32[]{:S(2)}) copy-start(f32[64,12288]{1,0:T(8,128)} %ts_ref.5) | copy-start | bytes 9437188
  39.3 33.5 %copy-start.17 = (s32[12288]{0:T(1024)S(1)}, s32[12288]{0:T(1024)}, u32[]{:S(2)}) copy-start(s32[12288]{0:T(1024)} %param.8) | copy-start | bytes 147460
  39.4 33.5 %copy-start.18 = (s32[1,128]{1,0:T(1,128)S(1)}, s32[1,128]{1,0:T(1,128)}, u32[]{:S(2)}) copy-start(s32[1,128]{1,0:T(1,128)} %param.12) | copy-start | bytes 1540
  39.4 33.5 %copy-start.20 = (s32[1,128]{1,0:T(1,128)S(1)}, s32[1,128]{1,0:T(1,128)}, u32[]{:S(2)}) copy-start(s32[1,128]{1,0:T(1,128)} %param.11) | copy-start | bytes 1540
  39.4 33.5 %collective-permute-start.2 = (f32[48,128]{1,0:T(8,128)S(1)}, f32[48,128]{1,0:T(8,128)S(1)}, u32[]{:S(2)}, u32[]{:S(2)}) collective-permute-start(f32[48,128]{1,0:T(8,128)S(1)} %get-tuple-element.22), channel_id=1, source_target_pairs={{0,1},{1,2},{2,3},{3,4},{4,5},{5,6},{6,7},{7,8},{8,9},{9,10},{10,1... | collective-permute-start | bytes 73736 | tf_op jit(solution)/shard_map/ppermute | solution.py:409
  71.1 1.8 %copy-start.9 = (f32[96,72,128]{2,1,0:T(8,128)}, f32[96,72,128]{2,1,0:T(8,128)S(1)}, u32[]{:S(2)}) copy-start(f32[96,72,128]{2,1,0:T(8,128)S(1)} %band.2.band_ref) | copy-start | bytes 10616836
  72.9 2.0 %copy-start.10 = (f32[96,72,128]{2,1,0:T(8,128)S(1)}, f32[96,72,128]{2,1,0:T(8,128)}, u32[]{:S(2)}) copy-start(f32[96,72,128]{2,1,0:T(8,128)} %copy-done.9) | copy-start | bytes 10616836
  85.8 1.4 copy-start.11
  89.1 62.0 %all-to-all-start.1 = ((bf16[128,72,128]{2,1,0:T(8,128)(2,1)}), bf16[128,72,128]{2,1,0:T(8,128)(2,1)}, u32[]{:S(2)}, u32[]{:S(2)}) async-start(bf16[128,72,128]{2,1,0:T(8,128)(2,1)} %copy-done.11), calls=%async_computation.1 | async-start | bytes 4718592 | tf_op jit(solution)/shard_map/all_to_all | solution.py:371
  97.9 35.9 %collective-permute-start.4 = (bf16[48,72,128]{2,1,0:T(8,128)(2,1)}, bf16[48,72,128]{2,1,0:T(8,128)(2,1)S(1)}, u32[]{:S(2)}, u32[]{:S(2)}) collective-permute-start(bf16[48,72,128]{2,1,0:T(8,128)(2,1)} %copy-done.14), channel_id=1, source_target_pairs={{0,1},{1,2},{2,3},{3,4},{4,5},{5,6},{6,7},{7,8},{8,9},{9,10},{10,1... | collective-permute-start | bytes 2654216 | tf_op jit(solution)/shard_map/ppermute | solution.py:369
  101.5 34.0 %collective-permute-start.5 = (bf16[48,72,128]{2,1,0:T(8,128)(2,1)}, bf16[48,72,128]{2,1,0:T(8,128)(2,1)S(1)}, u32[]{:S(2)}, u32[]{:S(2)}) collective-permute-start(bf16[48,72,128]{2,1,0:T(8,128)(2,1)} %copy-done.12), channel_id=1, source_target_pairs={{1,0},{2,1},{3,2},{4,3},{5,4},{6,5},{7,6},{8,7},{9,8},{10,9},{11,1... | collective-permute-start | bytes 2654216 | tf_op jit(solution)/shard_map/ppermute | solution.py:370
  135.6 4.6 %copy-start.2 = (bf16[96,4,128,128]{3,2,1,0:T(8,128)(2,1)S(1)}, bf16[96,4,128,128]{3,2,1,0:T(8,128)(2,1)}, u32[]{:S(2)}) copy-start(bf16[96,4,128,128]{3,2,1,0:T(8,128)(2,1)} %weights_ref.8) | copy-start | bytes 37748740
  149.3 1.8 %copy-start.7 = (f32[96,72,128]{2,1,0:T(8,128)}, f32[96,72,128]{2,1,0:T(8,128)S(1)}, u32[]{:S(2)}) copy-start(f32[96,72,128]{2,1,0:T(8,128)S(1)} %band.3.band_ref) | copy-start | bytes 10616836
  151.0 2.2 %copy-start.4 = (bf16[128,128,128]{2,1,0:T(8,128)(2,1)S(1)}, bf16[128,128,128]{2,1,0:T(8,128)(2,1)}, u32[]{:S(2)}) copy-start(bf16[128,128,128]{2,1,0:T(8,128)(2,1)} %weights_ref.9) | copy-start | bytes 12582916
  153.2 2.0 %copy-start.8 = (f32[96,72,128]{2,1,0:T(8,128)S(1)}, f32[96,72,128]{2,1,0:T(8,128)}, u32[]{:S(2)}) copy-start(f32[96,72,128]{2,1,0:T(8,128)} %copy-done.7) | copy-start | bytes 10616836
  (6 other events, 5.6 us)

commit v2 on v0

v2 whole, which is shorter than its diff:
```python
import functools

import jax
import jax.numpy as jnp
from jax import lax
from jax.experimental import pallas as pl
from jax.experimental.pallas import tpu as pltpu
from jax.sharding import PartitionSpec as P

PRIOR = 20.0
EXTRA = 8
F32 = jnp.float32
BF16 = jnp.bfloat16
LOADS = 8
BAND_LOADS = 12
PARTS = 4
BAND_COST = 10**11
VMEM = 60
VMEM_ROUND = 60
VMEM_BAND = 52
AHEAD = 3


def pieces(value, count):
    parts = []
    for _ in range(count):
        part = value.astype(BF16).astype(F32)
        parts.append(part)
        value = value - part
    return parts


def rows8(rows, base=None):
    width = 128
    index = lax.broadcasted_iota(jnp.int32, (EXTRA, width), 0)
    block = jnp.zeros((EXTRA, width), F32) if base is None else base
    for place, row in rows.items():
        block = jnp.where(index == place, row, block)
    return block


def to_row(column, shift=0):
    channels = column.shape[0]
    lane = lax.broadcasted_iota(jnp.int32, (channels, 128), 1)
    sub = lax.broadcasted_iota(jnp.int32, (channels, 128), 0)
    return jnp.sum(jnp.where(lane == sub + shift, column, 0.0), axis=0, keepdims=True)


def to_column(row, channels, shift=0):
    lane = lax.broadcasted_iota(jnp.int32, (channels, 128), 1)
    sub = lax.broadcasted_iota(jnp.int32, (channels, 128), 0)
    return jnp.sum(jnp.where(lane == sub + shift, row, 0.0), axis=1, keepdims=True)


def at_lane(scalar, place):
    lane = lax.broadcasted_iota(jnp.int32, (1, 128), 1)
    return jnp.where(lane == place, scalar, 0.0)


def pick_lane(row, place):
    lane = lax.broadcasted_iota(jnp.int32, (1, 128), 1)
    return jnp.sum(jnp.where(lane == place, row, 0.0), axis=1, keepdims=True)


def total(block):
    return jnp.sum(jnp.sum(block, axis=0, keepdims=True), axis=1, keepdims=True)


def stacked(top, bottom):
    return jnp.concatenate([top, bottom], axis=0).astype(BF16)


def product(tile, weights):
    return lax.dot_general(tile, weights, (((1,), (1,)), ((), ())), preferred_element_type=F32)


class Loads:
    def __init__(self, pairs, count, sems, first):
        self.parts, self.count = [], count
        for i in range(count):
            part = []
            for number, (source, target, axis) in enumerate(pairs):
                size = source.shape[axis] // count
                at = (slice(None),) * axis + (pl.ds(i * size, size),)
                sem = sems.at[first + i * len(pairs) + number]
                part.append(pltpu.make_async_copy(source.at[at], target.at[at], sem))
            self.parts.append(part)

    def start(self, i):
        if i < self.count:
            for copy in self.parts[i]:
                copy.start()

    def wait(self, i):
        for copy in self.parts[i]:
            copy.wait()


def send_messages(send_ref, tiles, messages, out_ref, sems, first_sem, block, column_rows=None):
    count, rows, width = messages.shape
    top = jnp.zeros((rows - EXTRA, width), F32)
    if column_rows is None:
        shared = stacked(top, block)
    stores = []
    part = count // PARTS
    for number in range(PARTS):

        def step(k, carry, number=number):
            q = number * part + k
            if column_rows is None:
                extra = shared
            else:
                high, low = pieces(column_rows[pl.ds(q, 1), :], 2)
                extra = stacked(top, rows8({6: high, 7: low}, block))
            messages[q] = tiles[send_ref[q]] + extra
            return carry

        lax.fori_loop(0, part, step, 0, unroll=8)
        at = pl.ds(number * part, part)
        stores.append(
            pltpu.make_async_copy(messages.at[at], out_ref.at[at], sems.at[first_sem + number])
        )
        stores[-1].start()
    return stores


def prep_kernel(
    send_ref, ts_ref, counts_ref, remote_ref, low_ref, high_ref, out_ref,
    ts, remote, tiles, messages, columns, sems, out_sems,
):
    channels, width = ts.shape[0], columns.shape[1]
    count_tiles, shards = tiles.shape[0], messages.shape[0]
    half = count_tiles // 2
    here, group = count_tiles // LOADS, shards // LOADS
    ts_loads = Loads([(ts_ref, ts, 1)], LOADS, sems, 0)
    remote_loads = Loads([(remote_ref, remote, 0)], LOADS, sems, LOADS)
    loads = [(ts_loads, i) for i in range(LOADS)] + [(remote_loads, i) for i in range(LOADS)]
    for group_loads, i in loads[: 2 * AHEAD]:
        group_loads.start(i)

    def start_next(done):
        for group_loads, i in loads[done + 2 * AHEAD : done + 2 * AHEAD + 1]:
            group_loads.start(i)

    stores = [
        pltpu.make_async_copy(tiles.at[pl.ds(0, half)], low_ref, out_sems.at[0]),
        pltpu.make_async_copy(tiles.at[pl.ds(half, half)], high_ref, out_sems.at[1]),
    ]
    part = jnp.zeros((channels, width), F32)
    for load in range(LOADS):
        ts_loads.wait(load)
        start_next(load)

        def tile(k, part, load=load):
            t = load * here + k
            block = ts[:, pl.ds(pl.multiple_of(t * width, width), width)]
            count = counts_ref[pl.ds(t, 1), :].astype(F32)
            recip = 1.0 / (count + PRIOR)
            high, low = pieces(recip, 2)
            tiles[t] = stacked(block * recip, rows8({0: high, 1: low, 2: jnp.ones_like(recip)}))
            return part + block

        part = lax.fori_loop(0, here, tile, part, unroll=4)
        if load == LOADS // 2 - 1:
            stores[0].start()
    stores[1].start()
    for load in range(LOADS):
        remote_loads.wait(load)
        start_next(LOADS + load)

        def column(k, carry, load=load):
            p = load * group + k
            columns[pl.ds(p, 1), :] = jnp.sum(remote[p].astype(F32), axis=0, keepdims=True)
            return carry

        lax.fori_loop(0, group, column, 0, unroll=4)
    row = to_row(jnp.sum(part, axis=1, keepdims=True))
    row = row + at_lane(total(counts_ref[...].astype(F32)), channels)
    one, two, three = pieces(row, 3)
    block = rows8({3: one, 4: two, 5: three})
    stores += send_messages(send_ref, tiles, messages, out_ref, out_sems, 2, block, columns)
    for store in stores:
        store.wait()


def band_kernel(
    with_ones, offsets_ref, ts_ref, counts_ref, below_ref, low_ref, high_ref, above_ref, weights_ref, out_ref, *rest
):
    if with_ones:
        sums_ref, ts, weights, window, result, sems, out_sems = rest
    else:
        ts, weights, window, result, sems, out_sems = rest
    count_tiles, band = weights.shape[:2]
    reach, rows, width = below_ref.shape
    channels = rows - EXTRA
    here = count_tiles // BAND_LOADS
    parts = []
    for i, ref in enumerate((below_ref, low_ref, high_ref, above_ref)):
        parts.append(pltpu.make_async_copy(ref, window.at[pl.ds(i * reach, reach)], sems.at[2 * BAND_LOADS + i]))
        parts[-1].start()
    loads = Loads([(weights_ref, weights, 0), (ts_ref, ts, 1)], BAND_LOADS, sems, 0)
    for load in range(AHEAD):
        loads.start(load)
    if with_ones:
        sums_ref[...] = jnp.zeros_like(sums_ref)
    for copy in parts:
        copy.wait()
    if with_ones:
        sub = lax.broadcasted_iota(jnp.int32, (rows, width), 0)
        for begin in (0, reach + count_tiles):

            def fix(k, carry, begin=begin):
                value = window[begin + k].astype(F32)
                window[begin + k] = jnp.where(sub == channels + 2, 1.0, value).astype(BF16)
                return carry

            lax.fori_loop(0, reach, fix, 0, unroll=4)
    stores = Loads([(result, out_ref, 0)], BAND_LOADS, out_sems, 0)
    for load in range(BAND_LOADS):
        loads.start(load + AHEAD)
        loads.wait(load)

        def tile(k, carry, load=load):
            t = load * here + k
            places = [t + offsets_ref[t * band + b] + reach for b in range(band)]
            matrices = [weights[t, b] for b in range(band)]
            sources = jnp.concatenate([window[place] for place in places], axis=1)
            mixed = product(sources, jnp.concatenate(matrices, axis=1))
            known = [ts[:, pl.ds(pl.multiple_of(t * width, width), width)]]
            known.append(rows8({2: counts_ref[pl.ds(t, 1), :].astype(F32)}))
            result[t] = mixed + jnp.concatenate(known, axis=0)
            if with_ones:
                for place, matrix in zip(places, matrices):
                    sums_ref[pl.ds(place, 1), :] += jnp.sum(matrix.astype(F32), axis=0, keepdims=True)
            return carry

        lax.fori_loop(0, here, tile, 0, unroll=4)
        stores.start(load)
    for load in range(BAND_LOADS):
        stores.wait(load)


def add_remote(landing_ref, in_ref, weights_ref, band_ref, incoming, weights, band, acc, sems, each=None):
    shards, rows, width = incoming.shape
    group = shards // LOADS
    loads = Loads([(in_ref, incoming, 0), (weights_ref, weights, 0)], LOADS, sems, 0)
    band_loads = Loads([(band_ref, band, 0)], PARTS, sems, 2 * LOADS)
    for load in range(AHEAD):
        loads.start(load)

    def clear(t, carry):
        acc[t] = jnp.zeros((rows, width), F32)
        return carry

    lax.fori_loop(0, acc.shape[0], clear, 0, unroll=8)
    seen = jnp.zeros((EXTRA, width), F32)
    for load in range(LOADS):
        loads.start(load + AHEAD)
        if load + AHEAD >= LOADS:
            band_loads.start(load + AHEAD - LOADS)
        loads.wait(load)

        def tile(k, seen, load=load):
            p = load * group + k
            value = incoming[p]
            tail = value.astype(F32)[rows - EXTRA :]
            acc[landing_ref[p]] += product(value, weights[p])
            if each is not None:
                each(p, tail)
            return seen + tail

        seen = lax.fori_loop(0, group, tile, seen, unroll=16)
    for part in range(AHEAD, PARTS):
        band_loads.start(part)
    return seen, band_loads


def first_kernel(
    send_ref, landing_ref, in_ref, weights_ref, band_ref, columns_ref,
    low_ref, high_ref, out_ref, recip_ref, first_ref,
    incoming, weights, band, acc, tiles, messages, columns, recips, firsts, sems, out_sems,
):
    shards, rows, width = incoming.shape
    channels = rows - EXTRA
    count_tiles = acc.shape[0]
    half = count_tiles // 2
    column_load = pltpu.make_async_copy(columns_ref, columns, out_sems.at[0])
    column_load.start()
    column_load.wait()

    def each(p, tail):
        columns[pl.ds(send_ref[p], 1), :] += tail[6:7] + tail[7:8]

    seen, band_loads = add_remote(
        landing_ref, in_ref, weights_ref, band_ref, incoming, weights, band, acc, sems, each
    )
    known = seen[3:4, :] + seen[4:5, :] + seen[5:6, :]
    count_total = pick_lane(known, channels)
    first = jnp.broadcast_to(PRIOR * to_column(known, channels) / count_total, (channels, width))
    firsts[...] = jnp.broadcast_to(known, firsts.shape)
    zero = jnp.zeros((channels, width), F32)
    line = jnp.zeros((1, width), F32)
    carry = (zero, zero, line, line)
    stores = []
    part = count_tiles // PARTS
    for number in range(PARTS):
        band_loads.wait(number)

        def finish(k, carry, number=number):
            t = number * part + k
            all_totals, all_states, all_weights, all_recips = carry
            mixed = acc[t] + band[t]
            spread = mixed[channels : channels + 1] + mixed[channels + 1 : channels + 2]
            totals = mixed[:channels] + first * spread
            weight = mixed[channels + 2 : channels + 3]
            recip = 1.0 / (weight + PRIOR)
            recips[pl.ds(t, 1), :] = recip
            high, low = pieces(recip, 2)
            state = (totals * recip).astype(BF16).astype(F32)
            tiles[t] = stacked(state, rows8({0: high, 1: low}))
            column = columns[pl.ds(t, 1), :]
            return (
                all_totals + totals,
                all_states + state * column,
                all_weights + weight,
                all_recips + (high + low) * column,
            )

        carry = lax.fori_loop(0, part, finish, carry, unroll=4)
        ref = low_ref if number < PARTS // 2 else high_ref
        at = pl.ds(number * part % half, part)
        stores.append(
            pltpu.make_async_copy(tiles.at[pl.ds(number * part, part)], ref.at[at], out_sems.at[number])
        )
        stores[-1].start()
    for source, ref in ((recips, recip_ref), (firsts, first_ref)):
        stores.append(pltpu.make_async_copy(source, ref, out_sems.at[len(stores)]))
        stores[-1].start()
    all_totals, all_states, all_weights, all_recips = carry
    row = to_row(jnp.sum(all_totals, axis=1, keepdims=True))
    row = row + to_row(jnp.sum(all_states, axis=1, keepdims=True), channels)
    scalars = at_lane(total(all_weights), 0) + at_lane(total(all_recips), 1)
    one, two, three = pieces(row, 3)
    uno, due, tre = pieces(scalars, 3)
    block = rows8({2: uno, 3: one, 4: two, 5: three, 6: due, 7: tre})
    stores += send_messages(send_ref, tiles, messages, out_ref, out_sems, len(stores), block)
    for store in stores:
        store.wait()


def last_kernel(
    landing_ref, in_ref, weights_ref, band_ref, recip_ref, first_ref, out_ref,
    incoming, weights, band, acc, result, recips, firsts, sems, out_sems,
):
    shards, rows, width = incoming.shape
    channels = rows - EXTRA
    count_tiles = acc.shape[0]
    small = [
        pltpu.make_async_copy(recip_ref, recips, out_sems.at[0]),
        pltpu.make_async_copy(first_ref, firsts, out_sems.at[1]),
    ]
    for load in small:
        load.start()
    seen, band_loads = add_remote(
        landing_ref, in_ref, weights_ref, band_ref, incoming, weights, band, acc, sems
    )
    for load in small:
        load.wait()
    known = seen[3:4, :] + seen[4:5, :] + seen[5:6, :]
    scalars = seen[2:3, :] + seen[6:7, :] + seen[7:8, :]
    weight_total, spread_total = pick_lane(scalars, 0), pick_lane(scalars, 1)
    mean = PRIOR * to_column(known, channels) / weight_total
    mixed_total = to_column(known, channels, channels) + mean * spread_total
    last = PRIOR * (to_column(firsts[0:1, :], channels) + mixed_total) / weight_total
    mean, last = jnp.broadcast_to(mean, (channels, width)), jnp.broadcast_to(last, (channels, width))
    stores = []
    part = count_tiles // PARTS
    for number in range(PARTS):
        band_loads.wait(number)

        def finish(k, carry, number=number):
            t = number * part + k
            mixed = acc[t] + band[t]
            spread = mixed[channels : channels + 1] + mixed[channels + 1 : channels + 2]
            at = pl.ds(pl.multiple_of(t * width, width), width)
            result[:, at] = (mixed[:channels] + mean * spread + last) * recips[pl.ds(t, 1), :]
            return carry

        lax.fori_loop(0, part, finish, 0, unroll=4)
        at = pl.ds(number * part * width, part * width)
        stores.append(pltpu.make_async_copy(result.at[:, at], out_ref.at[:, at], out_sems.at[number]))
        stores[-1].start()
    for store in stores:
        store.wait()


def params(mib):
    return pltpu.CompilerParams(vmem_limit_bytes=mib * 2**20)


def cost(flops, size):
    return pl.CostEstimate(flops=flops, bytes_accessed=size, transcendentals=0)


def whole(shape):
    zeros = (0,) * len(shape)
    return pl.BlockSpec(shape, lambda *_: zeros)


ANY = pl.BlockSpec(memory_space=pl.ANY)


def shapes(count_tiles, rows, shards, width=128):
    tile = jax.ShapeDtypeStruct((count_tiles // 2, rows, width), BF16)
    message = jax.ShapeDtypeStruct((shards, rows, width), BF16)
    return tile, message


def call(kernel, prefetch, in_specs, out_specs, out_shape, scratch, name, estimate, limit=VMEM):
    return pl.pallas_call(
        kernel,
        grid_spec=pltpu.PrefetchScalarGridSpec(
            num_scalar_prefetch=prefetch,
            grid=(1,),
            in_specs=in_specs,
            out_specs=out_specs,
            scratch_shapes=scratch,
        ),
        out_shape=out_shape,
        compiler_params=params(limit),
        cost_estimate=estimate,
        name=name,
    )


def sems(count):
    return pltpu.SemaphoreType.DMA((count,))


def prep(send, ts, counts, remote_weights):
    channels, columns = ts.shape
    count_tiles, width = counts.shape
    shards = remote_weights.shape[0]
    rows = channels + EXTRA
    tile, message = shapes(count_tiles, rows, shards)
    scratch = [
        pltpu.VMEM(ts.shape, F32),
        pltpu.VMEM(remote_weights.shape, BF16),
        pltpu.VMEM((count_tiles, rows, width), BF16),
        pltpu.VMEM(message.shape, BF16),
        pltpu.VMEM((shards, width), F32),
        sems(2 * LOADS),
        sems(2 + PARTS),
    ]
    return call(
        prep_kernel, 1, [ANY, whole(counts.shape), ANY], [ANY] * 3, [tile, tile, message], scratch, "prep",
        cost(10**6, 12 * 10**6),
    )(send, ts, counts, remote_weights)


def band_product(with_ones, offsets, ts, counts, below, low, high, above, band_weights):
    count_tiles, _, width, _ = band_weights.shape
    rows = low.shape[1]
    shape = (count_tiles, rows, width)
    scratch = [
        pltpu.VMEM(ts.shape, F32),
        pltpu.VMEM(band_weights.shape, BF16),
        pltpu.VMEM((2 * count_tiles, rows, width), BF16),
        pltpu.VMEM(shape, F32),
        sems(2 * BAND_LOADS + 4),
        sems(BAND_LOADS),
    ]
    out_shape, out_specs = [jax.ShapeDtypeStruct(shape, F32)], [ANY]
    if with_ones:
        out_shape.append(jax.ShapeDtypeStruct((2 * count_tiles, width), F32))
        out_specs.append(whole(out_shape[1].shape))
    return call(
        functools.partial(band_kernel, with_ones), 1, [ANY, whole(counts.shape)] + [ANY] * 5, out_specs,
        out_shape, scratch, "band", cost(BAND_COST, 20 * 10**6), VMEM_BAND,
    )(offsets, ts, counts, below, low, high, above, band_weights)


def round_scratch(incoming, remote_weights, mixed):
    return [
        pltpu.VMEM(incoming.shape, BF16),
        pltpu.VMEM(remote_weights.shape, BF16),
        pltpu.VMEM(mixed.shape, F32),
        pltpu.VMEM(mixed.shape, F32),
    ]


def first_round(send, landing, incoming, remote_weights, mixed, columns):
    shards, rows, width = incoming.shape
    count_tiles = mixed.shape[0]
    tile, message = shapes(count_tiles, rows, shards)
    recip = jax.ShapeDtypeStruct((count_tiles, width), F32)
    first = jax.ShapeDtypeStruct((8, width), F32)
    scratch = round_scratch(incoming, remote_weights, mixed) + [
        pltpu.VMEM(mixed.shape, BF16),
        pltpu.VMEM(incoming.shape, BF16),
        pltpu.VMEM(columns.shape, F32),
        pltpu.VMEM(recip.shape, F32),
        pltpu.VMEM(first.shape, F32),
        sems(PARTS + 2 * LOADS),
        sems(2 + 2 * PARTS),
    ]
    return call(
        first_kernel, 2, [ANY] * 4, [ANY] * 5, [tile, tile, message, recip, first], scratch, "first",
        cost(2 * 128 * 72 * 128 * 128, 20 * 10**6), VMEM_ROUND,
    )(send, landing, incoming, remote_weights, mixed, columns)


def last_round(landing, incoming, remote_weights, mixed, recip, first):
    rows, width = incoming.shape[1:]
    shape = (rows - EXTRA, mixed.shape[0] * width)
    scratch = round_scratch(incoming, remote_weights, mixed) + [
        pltpu.VMEM(shape, F32),
        pltpu.VMEM(recip.shape, F32),
        pltpu.VMEM(first.shape, F32),
        sems(PARTS + 2 * LOADS),
        sems(PARTS),
    ]
    return call(
        last_kernel, 1, [ANY] * 5, ANY, jax.ShapeDtypeStruct(shape, F32), scratch, "last",
        cost(2 * 128 * 72 * 128 * 128, 20 * 10**6), VMEM_ROUND,
    )(landing, incoming, remote_weights, mixed, recip, first)


def on_device(target_sums, counts, band_offsets, band_weights, send_tiles, landing_tiles, remote_weights):
    count_tiles, _, width, _ = band_weights.shape
    shards = remote_weights.shape[0]
    reach = count_tiles // 2
    counts = counts.reshape(count_tiles, width)
    send, landing, offsets = send_tiles.reshape(-1), landing_tiles.reshape(-1), band_offsets.reshape(-1)
    up = [(i, i + 1) for i in range(shards - 1)]
    down = [(i + 1, i) for i in range(shards - 1)]

    def exchange(low, high, outgoing):
        below = lax.ppermute(high, "item", up)
        above = lax.ppermute(low, "item", down)
        incoming = lax.all_to_all(outgoing, "item", split_axis=0, concat_axis=0, tiled=True)
        return below, above, incoming

    low, high, outgoing = prep(send, target_sums, counts, remote_weights)
    below, above, incoming = exchange(low, high, outgoing)
    mixed, sums = band_product(True, offsets, target_sums, counts, below, low, high, above, band_weights)
    from_below = lax.ppermute(sums[reach + count_tiles :], "item", up)
    from_above = lax.ppermute(sums[:reach], "item", down)
    columns = sums[reach : reach + count_tiles] + jnp.concatenate([from_below, from_above], axis=0)
    low, high, outgoing, recip, first = first_round(send, landing, incoming, remote_weights, mixed, columns)
    below, above, incoming = exchange(low, high, outgoing)
    (mixed,) = band_product(False, offsets, target_sums, counts, below, low, high, above, band_weights)
    return last_round(landing, incoming, remote_weights, mixed, recip, first)


def solution(mesh):
    return jax.shard_map(
        on_device,
        mesh=mesh,
        in_specs=(
            P(None, "item"),
            P("item"),
            P("item", None),
            P("item", None, None, None),
            P("item", None),
            P("item", None),
            P("item", None, None),
        ),
        out_specs=P(None, "item"),
        check_vma=False,
    )
```

time: 392 us -> 150 us (0.38)
  the two profiles are of different devices: /device:TPU:1 before, /device:TPU:27 now
where the time goes in v2:
time: 150 us; the launch traced here: 149 us
  waiting for transfers between devices  63.8 us (43%)
  Pallas kernels  48.2 us (32%)
  starting transfers between devices  34.1 us (23%)
  local copies, waits for them, and re-layouts  2.17 us (1%)
    ppermute x2, waiting for transfers between devices, exchange(): above = lax.ppermute(low, 'item', down)  61 us
    pallas_call x2, Pallas kernels, band_product(): call(functools.partial(band_kernel, with_ones), 1, [ANY, whole(counts.sha...  22.7 us
    all_to_all x2, starting transfers between devices, exchange(): lax.all_to_all(outgoing, 'item', split_axis=0, concat_axis=0, tiled=True)  19.1 us
    pallas_call x1, Pallas kernels, first_round(): call(first_kernel, 2, [ANY] * 4, [ANY] * 5, [tile, tile, message, recip,...  9.87 us
    pallas_call x1, Pallas kernels, last_round(): call(last_kernel, 1, [ANY] * 5, ANY, jax.ShapeDtypeStruct(shape, F32), sc...  8.14 us
    pallas_call x1, Pallas kernels, prep(): call(prep_kernel, 1, [ANY, whole(counts.shape), ANY], [ANY] * 3, [tile, t...  7.51 us
    ppermute x2, starting transfers between devices, exchange(): below = lax.ppermute(high, 'item', up)  6.29 us
    ppermute x2, starting transfers between devices, exchange(): above = lax.ppermute(low, 'item', down)  4.33 us
  transfers between devices with their start and end apart: 8, of which 3 were waited for; matrix products, arithmetic and copies ran while one was open for 1% of the time, Pallas kernels for 15%

profile of v2, /device:TPU:27, one launch (start us, length us, event | category | flops | bytes accessed | tf_op | source)
XLA Modules:
  0.0 149.2 jit_solution(12156415276287854635)
XLA Ops:
  0.0 7.5 %prep.1 = (bf16[48,72,128]{2,1,0:T(8,128)(2,1)}, bf16[48,72,128]{2,1,0:T(8,128)(2,1)}, bf16[128,72,128]{2,1,0:T(8,128)(2,1)}) custom-call(s32[128]{0:T(128)} %bitcast.8, f32[64,12288]{1,0:T(8,128)} %ts_ref.5, s32[96,128]{1,0:T(8,128)} %bitcast.3, bf16[128,128,128]{2,1,0:T(8,128)(2,1)} %weights_ref.7), custom_call_target="tpu_custom_call" | custom-call | flops 1000000 | bytes 12000000 | tf_op jit(solution)/shard_map/prep/pallas_call | solution.py:455
  7.5 0.0 copy-start.3
  7.5 0.0 copy-start
  7.6 4.2 %collective-permute-start = (bf16[48,72,128]{2,1,0:T(8,128)(2,1)}, bf16[48,72,128]{2,1,0:T(8,128)(2,1)S(1)}, u32[]{:S(2)}, u32[]{:S(2)}) collective-permute-start(bf16[48,72,128]{2,1,0:T(8,128)(2,1)} %get-tuple-element.16.high_ref), channel_id=1, source_target_pairs={{0,1},{1,2},{2,3},{3,4},{4,5},{5,6},{6,7},{7,8},{8,9},{9,10},{10,1... | collective-permute-start | bytes 2654216 | tf_op jit(solution)/shard_map/ppermute | solution.py:539
  11.8 1.9 %collective-permute-start.1 = (bf16[48,72,128]{2,1,0:T(8,128)(2,1)}, bf16[48,72,128]{2,1,0:T(8,128)(2,1)S(1)}, u32[]{:S(2)}, u32[]{:S(2)}) collective-permute-start(bf16[48,72,128]{2,1,0:T(8,128)(2,1)} %get-tuple-element.17.low_ref), channel_id=1, source_target_pairs={{1,0},{2,1},{3,2},{4,3},{5,4},{6,5},{7,6},{8,7},{9,8},{10,9},{11,1... | collective-permute-start | bytes 2654216 | tf_op jit(solution)/shard_map/ppermute | solution.py:540
  13.7 10.5 %all-to-all-start = ((bf16[128,72,128]{2,1,0:T(8,128)(2,1)}), bf16[128,72,128]{2,1,0:T(8,128)(2,1)}, u32[]{:S(2)}, u32[]{:S(2)}) async-start(bf16[128,72,128]{2,1,0:T(8,128)(2,1)} %get-tuple-element.15), calls=%async_computation | async-start | bytes 4718592 | tf_op jit(solution)/shard_map/all_to_all | solution.py:541
  24.3 0.1 copy.8
  24.4 0.1 reshape.15.offsets_ref
  24.5 0.0 collective-permute-done.below_ref
  24.5 29.3 %collective-permute-done.1.above_ref = bf16[48,72,128]{2,1,0:T(8,128)(2,1)S(1)} collective-permute-done((bf16[48,72,128]{2,1,0:T(8,128)(2,1)}, bf16[48,72,128]{2,1,0:T(8,128)(2,1)S(1)}, u32[]{:S(2)}, u32[]{:S(2)}) %collective-permute-start.1) | collective-permute-done | bytes 884768 | tf_op jit(solution)/shard_map/ppermute | solution.py:540
  53.8 0.9 copy-done.4
  54.7 11.4 %band.2 = (f32[96,72,128]{2,1,0:T(8,128)}, f32[192,128]{1,0:T(8,128)S(1)}) custom-call(s32[384]{0:T(512)S(1)} %reshape.15.offsets_ref, f32[64,12288]{1,0:T(8,128)} %ts_ref.5, s32[96,128]{1,0:T(8,128)S(1)} %bitcast.4, bf16[48,72,128]{2,1,0:T(8,128)(2,1)S(1)} %collective-permute-done.below_ref, bf16[48,72,128]{2,1,0:T(8,128)(2,1)S(1)} %copy-done.2, ...), custom_call_target="tpu_custom_call" | custom-call | flops 99999997952 | bytes 20000000 | tf_op jit(solution)/shard_map/band/pallas_call | solution.py:477
  66.2 1.9 %collective-permute-start.2 = (f32[48,128]{1,0:T(8,128)S(1)}, f32[48,128]{1,0:T(8,128)S(1)}, u32[]{:S(2)}, u32[]{:S(2)}) collective-permute-start(f32[48,128]{1,0:T(8,128)S(1)} %get-tuple-element.25), channel_id=1, source_target_pairs={{0,1},{1,2},{2,3},{3,4},{4,5},{5,6},{6,7},{7,8},{8,9},{9,10},{10,1... | collective-permute-start | bytes 73736 | tf_op jit(solution)/shard_map/ppermute | solution.py:547
  68.1 2.4 %collective-permute-start.3 = (f32[48,128]{1,0:T(8,128)S(1)}, f32[48,128]{1,0:T(8,128)S(1)}, u32[]{:S(2)}, u32[]{:S(2)}) collective-permute-start(f32[48,128]{1,0:T(8,128)S(1)} %get-tuple-element.26), channel_id=1, source_target_pairs={{1,0},{2,1},{3,2},{4,3},{5,4},{6,5},{7,6},{8,7},{9,8},{10,9},{11,1... | collective-permute-start | bytes 73736 | tf_op jit(solution)/shard_map/ppermute | solution.py:548
  70.5 2.7 %collective-permute-done.3 = f32[48,128]{1,0:T(8,128)S(1)} collective-permute-done((f32[48,128]{1,0:T(8,128)S(1)}, f32[48,128]{1,0:T(8,128)S(1)}, u32[]{:S(2)}, u32[]{:S(2)}) %collective-permute-start.3) | collective-permute-done | bytes 24608 | tf_op jit(solution)/shard_map/ppermute | solution.py:548
  73.2 0.6 maximum_add_fusion.columns_ref
  73.9 9.9 %first.1 = (bf16[48,72,128]{2,1,0:T(8,128)(2,1)}, bf16[48,72,128]{2,1,0:T(8,128)(2,1)}, bf16[128,72,128]{2,1,0:T(8,128)(2,1)}, f32[96,128]{1,0:T(8,128)}, f32[8,128]{1,0:T(8,128)}) custom-call(s32[128]{0:T(128)} %bitcast.9, s32[128]{0:T(128)} %bitcast.6, bf16[128,72,128]{2,1,0:T(8,128)(2,1)} %all-to-all-done.in_ref, bf16[128,128,128]{2,1,0:T(8,128)(2,1)} %weights_ref.7, ...), custom_call_target="tpu_custom_call" | custom-call | flops 301989888 | bytes 20000000 | tf_op jit(solution)/shard_map/first/pallas_call | solution.py:507
  83.8 2.1 %collective-permute-start.4 = (bf16[48,72,128]{2,1,0:T(8,128)(2,1)}, bf16[48,72,128]{2,1,0:T(8,128)(2,1)S(1)}, u32[]{:S(2)}, u32[]{:S(2)}) collective-permute-start(bf16[48,72,128]{2,1,0:T(8,128)(2,1)} %get-tuple-element.21.high_ref), channel_id=1, source_target_pairs={{0,1},{1,2},{2,3},{3,4},{4,5},{5,6},{6,7},{7,8},{8,9},{9,10},{10,1... | collective-permute-start | bytes 2654216 | tf_op jit(solution)/shard_map/ppermute | solution.py:539
  85.8 2.4 %collective-permute-start.5 = (bf16[48,72,128]{2,1,0:T(8,128)(2,1)}, bf16[48,72,128]{2,1,0:T(8,128)(2,1)S(1)}, u32[]{:S(2)}, u32[]{:S(2)}) collective-permute-start(bf16[48,72,128]{2,1,0:T(8,128)(2,1)} %get-tuple-element.22.low_ref), channel_id=1, source_target_pairs={{1,0},{2,1},{3,2},{4,3},{5,4},{6,5},{7,6},{8,7},{9,8},{10,9},{11,1... | collective-permute-start | bytes 2654216 | tf_op jit(solution)/shard_map/ppermute | solution.py:540
  88.2 8.6 %all-to-all-start.1 = ((bf16[128,72,128]{2,1,0:T(8,128)(2,1)}), bf16[128,72,128]{2,1,0:T(8,128)(2,1)}, u32[]{:S(2)}, u32[]{:S(2)}) async-start(bf16[128,72,128]{2,1,0:T(8,128)(2,1)} %get-tuple-element.20), calls=%async_computation.1 | async-start | bytes 4718592 | tf_op jit(solution)/shard_map/all_to_all | solution.py:541
  96.9 31.8 %collective-permute-done.5.above_ref = bf16[48,72,128]{2,1,0:T(8,128)(2,1)S(1)} collective-permute-done((bf16[48,72,128]{2,1,0:T(8,128)(2,1)}, bf16[48,72,128]{2,1,0:T(8,128)(2,1)S(1)}, u32[]{:S(2)}, u32[]{:S(2)}) %collective-permute-start.5) | collective-permute-done | bytes 884768 | tf_op jit(solution)/shard_map/ppermute | solution.py:540
  128.6 1.0 copy-done.5
  129.6 11.2 %band.3.band_ref = f32[96,72,128]{2,1,0:T(8,128)} custom-call(s32[384]{0:T(512)S(1)} %reshape.15.offsets_ref, f32[64,12288]{1,0:T(8,128)} %ts_ref.5, s32[96,128]{1,0:T(8,128)S(1)} %bitcast.5, bf16[48,72,128]{2,1,0:T(8,128)(2,1)S(1)} %collective-permute-done.4.below_ref, bf16[48,72,128]{2,1,0:T(8,128)(2,1)S(1)} %copy-done.1, ...), custom_call_target="tpu_custom_call" | custom-call | flops 99999997952 | bytes 20000000 | tf_op jit(solution)/shard_map/band/pallas_call | solution.py:477
  140.9 8.1 %last.1 = f32[64,12288]{1,0:T(8,128)} custom-call(s32[128]{0:T(128)} %bitcast.7, bf16[128,72,128]{2,1,0:T(8,128)(2,1)} %all-to-all-done.1.in_ref, bf16[128,128,128]{2,1,0:T(8,128)(2,1)} %weights_ref.7, f32[96,72,128]{2,1,0:T(8,128)} %band.3.band_ref, f32[96,128]{1,0:T(8,128)} %get-tuple-element.23.recip_ref, f32[8,128]{1,0:T(8,128)} %get-tuple-element.24.first_ref), custom_call_target="tpu_custom_call" | custom-call | flops 301989888 | bytes 20000000 | tf_op jit(solution)/shard_map/last/pallas_call | solution.py:523
  (13 shorter events, 0.0 us)
Async XLA Ops:
  7.5 16.7 %copy-start.3 = (s32[96,4]{0,1:T(4,128)S(1)}, s32[96,4]{0,1:T(4,128)}, u32[]{:S(2)}) copy-start(s32[96,4]{0,1:T(4,128)} %param.9) | copy-start | bytes 4612
  7.5 47.2 %copy-start = (s32[12288]{0:T(1024)S(1)}, s32[12288]{0:T(1024)}, u32[]{:S(2)}) copy-start(s32[12288]{0:T(1024)} %param.8) | copy-start | bytes 147460
  7.5 47.1 %copy-start.2 = (bf16[48,72,128]{2,1,0:T(8,128)(2,1)S(1)}, bf16[48,72,128]{2,1,0:T(8,128)(2,1)}, u32[]{:S(2)}) copy-start(bf16[48,72,128]{2,1,0:T(8,128)(2,1)} %get-tuple-element.17.low_ref) | copy-start | bytes 2654212
  7.6 16.9 %collective-permute-start = (bf16[48,72,128]{2,1,0:T(8,128)(2,1)}, bf16[48,72,128]{2,1,0:T(8,128)(2,1)S(1)}, u32[]{:S(2)}, u32[]{:S(2)}) collective-permute-start(bf16[48,72,128]{2,1,0:T(8,128)(2,1)} %get-tuple-element.16.high_ref), channel_id=1, source_target_pairs={{0,1},{1,2},{2,3},{3,4},{4,5},{5,6},{6,7},{7,8},{8,9},{9,10},{10,1... | collective-permute-start | bytes 2654216 | tf_op jit(solution)/shard_map/ppermute | solution.py:539
  11.8 42.0 %collective-permute-start.1 = (bf16[48,72,128]{2,1,0:T(8,128)(2,1)}, bf16[48,72,128]{2,1,0:T(8,128)(2,1)S(1)}, u32[]{:S(2)}, u32[]{:S(2)}) collective-permute-start(bf16[48,72,128]{2,1,0:T(8,128)(2,1)} %get-tuple-element.17.low_ref), channel_id=1, source_target_pairs={{1,0},{2,1},{3,2},{4,3},{5,4},{6,5},{7,6},{8,7},{9,8},{10,9},{11,1... | collective-permute-start | bytes 2654216 | tf_op jit(solution)/shard_map/ppermute | solution.py:540
  13.7 60.1 %all-to-all-start = ((bf16[128,72,128]{2,1,0:T(8,128)(2,1)}), bf16[128,72,128]{2,1,0:T(8,128)(2,1)}, u32[]{:S(2)}, u32[]{:S(2)}) async-start(bf16[128,72,128]{2,1,0:T(8,128)(2,1)} %get-tuple-element.15), calls=%async_computation | async-start | bytes 4718592 | tf_op jit(solution)/shard_map/all_to_all | solution.py:541
  53.8 0.9 copy-start.4
  66.2 4.3 %collective-permute-start.2 = (f32[48,128]{1,0:T(8,128)S(1)}, f32[48,128]{1,0:T(8,128)S(1)}, u32[]{:S(2)}, u32[]{:S(2)}) collective-permute-start(f32[48,128]{1,0:T(8,128)S(1)} %get-tuple-element.25), channel_id=1, source_target_pairs={{0,1},{1,2},{2,3},{3,4},{4,5},{5,6},{6,7},{7,8},{8,9},{9,10},{10,1... | collective-permute-start | bytes 73736 | tf_op jit(solution)/shard_map/ppermute | solution.py:547
  68.1 5.1 %collective-permute-start.3 = (f32[48,128]{1,0:T(8,128)S(1)}, f32[48,128]{1,0:T(8,128)S(1)}, u32[]{:S(2)}, u32[]{:S(2)}) collective-permute-start(f32[48,128]{1,0:T(8,128)S(1)} %get-tuple-element.26), channel_id=1, source_target_pairs={{1,0},{2,1},{3,2},{4,3},{5,4},{6,5},{7,6},{8,7},{9,8},{10,9},{11,1... | collective-permute-start | bytes 73736 | tf_op jit(solution)/shard_map/ppermute | solution.py:548
  83.7 45.9 %copy-start.1 = (bf16[48,72,128]{2,1,0:T(8,128)(2,1)S(1)}, bf16[48,72,128]{2,1,0:T(8,128)(2,1)}, u32[]{:S(2)}) copy-start(bf16[48,72,128]{2,1,0:T(8,128)(2,1)} %get-tuple-element.22.low_ref) | copy-start | bytes 2654212
  83.8 13.1 %collective-permute-start.4 = (bf16[48,72,128]{2,1,0:T(8,128)(2,1)}, bf16[48,72,128]{2,1,0:T(8,128)(2,1)S(1)}, u32[]{:S(2)}, u32[]{:S(2)}) collective-permute-start(bf16[48,72,128]{2,1,0:T(8,128)(2,1)} %get-tuple-element.21.high_ref), channel_id=1, source_target_pairs={{0,1},{1,2},{2,3},{3,4},{4,5},{5,6},{6,7},{7,8},{8,9},{9,10},{10,1... | collective-permute-start | bytes 2654216 | tf_op jit(solution)/shard_map/ppermute | solution.py:539
  85.8 42.8 %collective-permute-start.5 = (bf16[48,72,128]{2,1,0:T(8,128)(2,1)}, bf16[48,72,128]{2,1,0:T(8,128)(2,1)S(1)}, u32[]{:S(2)}, u32[]{:S(2)}) collective-permute-start(bf16[48,72,128]{2,1,0:T(8,128)(2,1)} %get-tuple-element.22.low_ref), channel_id=1, source_target_pairs={{1,0},{2,1},{3,2},{4,3},{5,4},{6,5},{7,6},{8,7},{9,8},{10,9},{11,1... | collective-permute-start | bytes 2654216 | tf_op jit(solution)/shard_map/ppermute | solution.py:540
  88.2 52.7 %all-to-all-start.1 = ((bf16[128,72,128]{2,1,0:T(8,128)(2,1)}), bf16[128,72,128]{2,1,0:T(8,128)(2,1)}, u32[]{:S(2)}, u32[]{:S(2)}) async-start(bf16[128,72,128]{2,1,0:T(8,128)(2,1)} %get-tuple-element.20), calls=%async_computation.1 | async-start | bytes 4718592 | tf_op jit(solution)/shard_map/all_to_all | solution.py:541
  128.6 1.0 copy-start.5

commit v3 on v2

--- a/solution.py
+++ b/solution.py
@@ -19,6 +19,8 @@
 VMEM_ROUND = 60
 VMEM_BAND = 52
 AHEAD = 3
+GROUP = 16
+SLOTS = 3
 
 
 def pieces(value, count):
@@ -94,6 +96,12 @@
     def wait(self, i):
         for copy in self.parts[i]:
             copy.wait()
+
+
+def two_products(tiles, weights):
+    rows, width = tiles[0].shape
+    both = product(jnp.concatenate(tiles, axis=0), jnp.concatenate(weights, axis=0))
+    return both[:rows, :width], both[rows:, width:]
 
 
 def send_messages(send_ref, tiles, messages, out_ref, sems, first_sem, block, column_rows=None):
@@ -183,38 +191,51 @@
         store.wait()
 
 
-def band_kernel(
-    with_ones, offsets_ref, ts_ref, counts_ref, below_ref, low_ref, high_ref, above_ref, weights_ref, out_ref, *rest
-):
+def list_far_pairs(offsets_ref, far_ref, count_tiles, band, reach):
+    room = far_ref.shape[0] // 4
+
+    def pair(i, found):
+        destination = i // band
+        source = destination + offsets_ref[i]
+        below = source < 0
+        far = jnp.logical_or(below, source >= count_tiles)
+        far_ref[found] = source + jnp.where(below, reach, reach - count_tiles)
+        far_ref[room + found] = i
+        far_ref[2 * room + found] = destination
+        return found + far.astype(jnp.int32)
+
+    found = lax.fori_loop(0, count_tiles * band, pair, 0, unroll=8)
+    for i in range(GROUP):
+        far_ref[found + i] = 2 * reach
+        far_ref[room + found + i] = 0
+        far_ref[2 * room + found + i] = 0
+    far_ref[3 * room] = found
+
+
+def band_kernel(with_ones, offsets_ref, ts_ref, counts_ref, low_ref, high_ref, weights_ref, out_ref, *rest):
     if with_ones:
-        sums_ref, ts, weights, window, result, sems, out_sems = rest
+        sums_ref, far_ref, ts, weights, window, result, sems, out_sems = rest
     else:
         ts, weights, window, result, sems, out_sems = rest
     count_tiles, band = weights.shape[:2]
-    reach, rows, width = below_ref.shape
+    half, rows, width = low_ref.shape
     channels = rows - EXTRA
     here = count_tiles // BAND_LOADS
     parts = []
-    for i, ref in enumerate((below_ref, low_ref, high_ref, above_ref)):
-        parts.append(pltpu.make_async_copy(ref, window.at[pl.ds(i * reach, reach)], sems.at[2 * BAND_LOADS + i]))
+    for i, ref in enumerate((low_ref, high_ref)):
+        parts.append(pltpu.make_async_copy(ref, window.at[pl.ds(i * half, half)], sems.at[2 * BAND_LOADS + i]))
         parts[-1].start()
     loads = Loads([(weights_ref, weights, 0), (ts_ref, ts, 1)], BAND_LOADS, sems, 0)
     for load in range(AHEAD):
         loads.start(load)
+    sub = lax.broadcasted_iota(jnp.int32, (rows, width), 0)
+    window[count_tiles] = jnp.where(sub == channels + 2, 1.0, 0.0).astype(BF16)
     if with_ones:
         sums_ref[...] = jnp.zeros_like(sums_ref)
+        reach = (sums_ref.shape[0] - count_tiles) // 2
+        list_far_pairs(offsets_ref, far_ref, count_tiles, band, reach)
     for copy in parts:
         copy.wait()
-    if with_ones:
-        sub = lax.broadcasted_iota(jnp.int32, (rows, width), 0)
-        for begin in (0, reach + count_tiles):
-
-            def fix(k, carry, begin=begin):
-                value = window[begin + k].astype(F32)
-                window[begin + k] = jnp.where(sub == channels + 2, 1.0, value).astype(BF16)
-                return carry
-
-            lax.fori_loop(0, reach, fix, 0, unroll=4)
     stores = Loads([(result, out_ref, 0)], BAND_LOADS, out_sems, 0)
     for load in range(BAND_LOADS):
         loads.start(load + AHEAD)
@@ -222,16 +243,17 @@
 
         def tile(k, carry, load=load):
             t = load * here + k
-            places = [t + offsets_ref[t * band + b] + reach for b in range(band)]
+            places = [t + offsets_ref[t * band + b] for b in range(band)]
+            near = [jnp.logical_and(place >= 0, place < count_tiles) for place in places]
+            sources = [window[jnp.where(n, place, count_tiles)] for n, place in zip(near, places)]
             matrices = [weights[t, b] for b in range(band)]
-            sources = jnp.concatenate([window[place] for place in places], axis=1)
-            mixed = product(sources, jnp.concatenate(matrices, axis=1))
+            mixed = product(jnp.concatenate(sources, axis=1), jnp.concatenate(matrices, axis=1))
             known = [ts[:, pl.ds(pl.multiple_of(t * width, width), width)]]
             known.append(rows8({2: counts_ref[pl.ds(t, 1), :].astype(F32)}))
             result[t] = mixed + jnp.concatenate(known, axis=0)
             if with_ones:
                 for place, matrix in zip(places, matrices):
-                    sums_ref[pl.ds(place, 1), :] += jnp.sum(matrix.astype(F32), axis=0, keepdims=True)
+                    sums_ref[pl.ds(place + reach, 1), :] += jnp.sum(matrix.astype(F32), axis=0, keepdims=True)
             return carry
 
         lax.fori_loop(0, here, tile, 0, unroll=4)
@@ -240,47 +262,101 @@
         stores.wait(load)
 
 
-def add_remote(landing_ref, in_ref, weights_ref, band_ref, incoming, weights, band, acc, sems, each=None):
+def add_far(landing_ref, far_ref, ins, scratch, each=None):
+    in_ref, weights_ref, band_ref, below_ref, above_ref, band_weights_ref = ins
+    incoming, weights, band, acc, halo, far_weights, sems, far_sems = scratch
     shards, rows, width = incoming.shape
     group = shards // LOADS
+    reach = below_ref.shape[0]
+    room = far_ref.shape[0] // 4
     loads = Loads([(in_ref, incoming, 0), (weights_ref, weights, 0)], LOADS, sems, 0)
     band_loads = Loads([(band_ref, band, 0)], PARTS, sems, 2 * LOADS)
+    halo_loads = [
+        pltpu.make_async_copy(below_ref, halo.at[pl.ds(0, reach)], sems.at[2 * LOADS + PARTS]),
+        pltpu.make_async_copy(above_ref, halo.at[pl.ds(reach, reach)], sems.at[2 * LOADS + PARTS + 1]),
+    ]
     for load in range(AHEAD):
         loads.start(load)
+    groups = (far_ref[3 * room] + GROUP - 1) // GROUP
+
+    def far_copies(g):
+        slot = lax.rem(g, SLOTS)
+        result = []
+        for k in range(GROUP):
+            pair = far_ref[room + g * GROUP + k]
+            source = band_weights_ref.at[pair]
+            result.append(
+                pltpu.make_async_copy(source, far_weights.at[slot * GROUP + k], far_sems.at[slot * GROUP + k])
+            )
+        return result
+
+    def start_group(g):
+        @pl.when(g < groups)
+        def _():
+            for copy in far_copies(g):
+                copy.start()
 
     def clear(t, carry):
         acc[t] = jnp.zeros((rows, width), F32)
         return carry
 
     lax.fori_loop(0, acc.shape[0], clear, 0, unroll=8)
+    halo[2 * reach] = jnp.zeros((rows, width), BF16)
     seen = jnp.zeros((EXTRA, width), F32)
     for load in range(LOADS):
         loads.start(load + AHEAD)
-        if load + AHEAD >= LOADS:
-            band_loads.start(load + AHEAD - LOADS)
+        if load + AHEAD == LOADS:
+            for copy in halo_loads:
+                copy.start()
+        if load + AHEAD > LOADS:
+            start_group(load + AHEAD - LOADS - 1)
         loads.wait(load)
 
-        def tile(k, seen, load=load):
-            p = load * group + k
-            value = incoming[p]
-            tail = value.astype(F32)[rows - EXTRA :]
-            acc[landing_ref[p]] += product(value, weights[p])
-            if each is not None:
-                each(p, tail)
-            return seen + tail
-
-        seen = lax.fori_loop(0, group, tile, seen, unroll=16)
-    for part in range(AHEAD, PARTS):
+        def pair(k, seen, load=load):
+            p = load * group + 2 * k
+            values = [incoming[p], incoming[p + 1]]
+            tails = [value.astype(F32)[rows - EXTRA :] for value in values]
+            mixed = two_products(values, [weights[p], weights[p + 1]])
+            for i in range(2):
+                acc[landing_ref[p + i]] += mixed[i]
+                if each is not None:
+                    each(p + i, tails[i])
+            return seen + (tails[0] + tails[1])
+
+        seen = lax.fori_loop(0, group // 2, pair, seen, unroll=8)
+    for copy in halo_loads:
+        copy.wait()
+    for part in range(PARTS):
         band_loads.start(part)
+    for g in range(AHEAD - 1, SLOTS):
+        start_group(g)
+    sub = lax.broadcasted_iota(jnp.int32, (EXTRA, width), 0)
+
+    def far_group(g, carry):
+        for copy in far_copies(g):
+            copy.wait()
+        slot = lax.rem(g, SLOTS)
+        for k in range(0, GROUP, 2):
+            at = [g * GROUP + k + i for i in range(2)]
+            mixed = two_products(
+                [halo[far_ref[i]] for i in at], [far_weights[slot * GROUP + k + i] for i in range(2)]
+            )
+            for i in range(2):
+                tail = jnp.where(sub == 2, 0.0, mixed[i][rows - EXTRA :])
+                full = jnp.concatenate([mixed[i][: rows - EXTRA], tail], axis=0)
+                acc[far_ref[2 * room + at[i]]] += full
+        start_group(g + SLOTS)
+        return carry
+
+    lax.fori_loop(0, groups, far_group, 0)
     return seen, band_loads
 
 
-def first_kernel(
-    send_ref, landing_ref, in_ref, weights_ref, band_ref, columns_ref,
-    low_ref, high_ref, out_ref, recip_ref, first_ref,
-    incoming, weights, band, acc, tiles, messages, columns, recips, firsts, sems, out_sems,
-):
-    shards, rows, width = incoming.shape
+def first_kernel(send_ref, landing_ref, far_ref, *refs):
+    ins, columns_ref, (low_ref, high_ref, out_ref, recip_ref, first_ref) = refs[:6], refs[6], refs[7:12]
+    scratch, (tiles, messages, columns, recips, firsts, out_sems) = refs[12:20], refs[20:]
+    band, acc = scratch[2:4]
+    _, rows, width = scratch[0].shape
     channels = rows - EXTRA
     count_tiles = acc.shape[0]
     half = count_tiles // 2
@@ -291,9 +367,7 @@
     def each(p, tail):
         columns[pl.ds(send_ref[p], 1), :] += tail[6:7] + tail[7:8]
 
-    seen, band_loads = add_remote(
-        landing_ref, in_ref, weights_ref, band_ref, incoming, weights, band, acc, sems, each
-    )
+    seen, band_loads = add_far(landing_ref, far_ref, ins, scratch, each)
     known = seen[3:4, :] + seen[4:5, :] + seen[5:6, :]
     count_total = pick_lane(known, channels)
     first = jnp.broadcast_to(PRIOR * to_column(known, channels) / count_total, (channels, width))
@@ -348,11 +422,11 @@
         store.wait()
 
 
-def last_kernel(
-    landing_ref, in_ref, weights_ref, band_ref, recip_ref, first_ref, out_ref,
-    incoming, weights, band, acc, result, recips, firsts, sems, out_sems,
-):
-    shards, rows, width = incoming.shape
+def last_kernel(landing_ref, far_ref, *refs):
+    ins, (recip_ref, first_ref, out_ref) = refs[:6], refs[6:9]
+    scratch, (result, recips, firsts, out_sems) = refs[9:17], refs[17:]
+    band, acc = scratch[2:4]
+    _, rows, width = scratch[0].shape
     channels = rows - EXTRA
     count_tiles = acc.shape[0]
     small = [
@@ -361,9 +435,7 @@
     ]
     for load in small:
         load.start()
-    seen, band_loads = add_remote(
-        landing_ref, in_ref, weights_ref, band_ref, incoming, weights, band, acc, sems
-    )
+    seen, band_loads = add_far(landing_ref, far_ref, ins, scratch)
     for load in small:
         load.wait()
     known = seen[3:4, :] + seen[4:5, :] + seen[5:6, :]
@@ -458,72 +530,77 @@
     )(send, ts, counts, remote_weights)
 
 
-def band_product(with_ones, offsets, ts, counts, below, low, high, above, band_weights):
-    count_tiles, _, width, _ = band_weights.shape
+def band_product(with_ones, offsets, ts, counts, low, high, band_weights):
+    count_tiles, band, width, _ = band_weights.shape
     rows = low.shape[1]
     shape = (count_tiles, rows, width)
     scratch = [
         pltpu.VMEM(ts.shape, F32),
         pltpu.VMEM(band_weights.shape, BF16),
-        pltpu.VMEM((2 * count_tiles, rows, width), BF16),
+        pltpu.VMEM((count_tiles + 1, rows, width), BF16),
         pltpu.VMEM(shape, F32),
-        sems(2 * BAND_LOADS + 4),
+        sems(2 * BAND_LOADS + 2),
         sems(BAND_LOADS),
     ]
     out_shape, out_specs = [jax.ShapeDtypeStruct(shape, F32)], [ANY]
     if with_ones:
+        room = -(-(count_tiles * band + GROUP + 1) // 512) * 512
         out_shape.append(jax.ShapeDtypeStruct((2 * count_tiles, width), F32))
-        out_specs.append(whole(out_shape[1].shape))
+        out_shape.append(jax.ShapeDtypeStruct((4 * room,), jnp.int32))
+        out_specs += [whole(out_shape[1].shape), pl.BlockSpec(memory_space=pltpu.SMEM)]
     return call(
-        functools.partial(band_kernel, with_ones), 1, [ANY, whole(counts.shape)] + [ANY] * 5, out_specs,
+        functools.partial(band_kernel, with_ones), 1, [ANY, whole(counts.shape)] + [ANY] * 3, out_specs,
         out_shape, scratch, "band", cost(BAND_COST, 20 * 10**6), VMEM_BAND,
-    )(offsets, ts, counts, below, low, high, above, band_weights)
-
-
-def round_scratch(incoming, remote_weights, mixed):
+    )(offsets, ts, counts, low, high, band_weights)
+
+
+def round_scratch(incoming, remote_weights, mixed, below):
+    rows, width = below.shape[1:]
     return [
         pltpu.VMEM(incoming.shape, BF16),
         pltpu.VMEM(remote_weights.shape, BF16),
         pltpu.VMEM(mixed.shape, F32),
         pltpu.VMEM(mixed.shape, F32),
-    ]
-
-
-def first_round(send, landing, incoming, remote_weights, mixed, columns):
+        pltpu.VMEM((2 * below.shape[0] + 1, rows, width), BF16),
+        pltpu.VMEM((SLOTS * GROUP, width, width), BF16),
+        sems(PARTS + 2 * LOADS + 2),
+        sems(SLOTS * GROUP),
+    ]
+
+
+def first_round(send, landing, far, incoming, remote_weights, mixed, below, above, band_weights, columns):
     shards, rows, width = incoming.shape
     count_tiles = mixed.shape[0]
     tile, message = shapes(count_tiles, rows, shards)
     recip = jax.ShapeDtypeStruct((count_tiles, width), F32)
     first = jax.ShapeDtypeStruct((8, width), F32)
-    scratch = round_scratch(incoming, remote_weights, mixed) + [
+    scratch = round_scratch(incoming, remote_weights, mixed, below) + [
         pltpu.VMEM(mixed.shape, BF16),
         pltpu.VMEM(incoming.shape, BF16),
         pltpu.VMEM(columns.shape, F32),
         pltpu.VMEM(recip.shape, F32),
         pltpu.VMEM(first.shape, F32),
-        sems(PARTS + 2 * LOADS),
         sems(2 + 2 * PARTS),
     ]
     return call(
-        first_kernel, 2, [ANY] * 4, [ANY] * 5, [tile, tile, message, recip, first], scratch, "first",
+        first_kernel, 3, [ANY] * 7, [ANY] * 5, [tile, tile, message, recip, first], scratch, "first",
         cost(2 * 128 * 72 * 128 * 128, 20 * 10**6), VMEM_ROUND,
-    )(send, landing, incoming, remote_weights, mixed, columns)
-
-
-def last_round(landing, incoming, remote_weights, mixed, recip, first):
+    )(send, landing, far, incoming, remote_weights, mixed, below, above, band_weights, columns)
+
+
+def last_round(landing, far, incoming, remote_weights, mixed, below, above, band_weights, recip, first):
     rows, width = incoming.shape[1:]
     shape = (rows - EXTRA, mixed.shape[0] * width)
-    scratch = round_scratch(incoming, remote_weights, mixed) + [
+    scratch = round_scratch(incoming, remote_weights, mixed, below) + [
         pltpu.VMEM(shape, F32),
         pltpu.VMEM(recip.shape, F32),
         pltpu.VMEM(first.shape, F32),
-        sems(PARTS + 2 * LOADS),
         sems(PARTS),
     ]
     return call(
-        last_kernel, 1, [ANY] * 5, ANY, jax.ShapeDtypeStruct(shape, F32), scratch, "last",
+        last_kernel, 2, [ANY] * 8, ANY, jax.ShapeDtypeStruct(shape, F32), scratch, "last",
         cost(2 * 128 * 72 * 128 * 128, 20 * 10**6), VMEM_ROUND,
-    )(landing, incoming, remote_weights, mixed, recip, first)
+    )(landing, far, incoming, remote_weights, mixed, below, above, band_weights, recip, first)
 
 
 def on_device(target_sums, counts, band_offsets, band_weights, send_tiles, landing_tiles, remote_weights):
@@ -532,6 +609,7 @@
     reach = count_tiles // 2
     counts = counts.reshape(count_tiles, width)
     send, landing, offsets = send_tiles.reshape(-1), landing_tiles.reshape(-1), band_offsets.reshape(-1)
+    flat_weights = band_weights.reshape(-1, width, width)
     up = [(i, i + 1) for i in range(shards - 1)]
     down = [(i + 1, i) for i in range(shards - 1)]
 
@@ -543,14 +621,18 @@
 
     low, high, outgoing = prep(send, target_sums, counts, remote_weights)
     below, above, incoming = exchange(low, high, outgoing)
-    mixed, sums = band_product(True, offsets, target_sums, counts, below, low, high, above, band_weights)
+    mixed, sums, far = band_product(True, offsets, target_sums, counts, low, high, band_weights)
     from_below = lax.ppermute(sums[reach + count_tiles :], "item", up)
     from_above = lax.ppermute(sums[:reach], "item", down)
     columns = sums[reach : reach + count_tiles] + jnp.concatenate([from_below, from_above], axis=0)
-    low, high, outgoing, recip, first = first_round(send, landing, incoming, remote_weights, mixed, columns)
+    low, high, outgoing, recip, first = first_round(
+        send, landing, far, incoming, remote_weights, mixed, below, above, flat_weights, columns
+    )
     below, above, incoming = exchange(low, high, outgoing)
-    (mixed,) = band_product(False, offsets, target_sums, counts, below, low, high, above, band_weights)
-    return last_round(landing, incoming, remote_weights, mixed, recip, first)
+    (mixed,) = band_product(False, offsets, target_sums, counts, low, high, band_weights)
+    return last_round(
+        landing, far, incoming, remote_weights, mixed, below, above, flat_weights, recip, first
+    )
 
 
 def solution(mesh):

time: 150 us -> 135 us (0.900)
  the two profiles are of different devices: /device:TPU:27 before, /device:TPU:24 now
where the time goes in v3:
time: 135 us; the launch traced here: 134 us
  Pallas kernels  59.2 us (44%)
  starting transfers between devices  44.2 us (33%)
  waiting for transfers between devices  28.2 us (21%)
    pallas_call x2, Pallas kernels, band_product(): call(functools.partial(band_kernel, with_ones), 1, [ANY, whole(counts.sha...  24.5 us
    all_to_all x2, starting transfers between devices, exchange(): lax.all_to_all(outgoing, 'item', split_axis=0, concat_axis=0, tiled=True)  15.5 us
    ppermute x2, starting transfers between devices, exchange(): above = lax.ppermute(low, 'item', down)  14.9 us
    pallas_call x1, Pallas kernels, first_round(): call(first_kernel, 3, [ANY] * 7, [ANY] * 5, [tile, tile, message, recip,...  14.6 us
    ppermute x2, waiting for transfers between devices, exchange(): above = lax.ppermute(low, 'item', down)  14.4 us
    pallas_call x1, Pallas kernels, last_round(): call(last_kernel, 2, [ANY] * 8, ANY, jax.ShapeDtypeStruct(shape, F32), sc...  12.6 us
    ppermute x1, starting transfers between devices, on_device(): from_above = lax.ppermute(sums[:reach], 'item', down)  7.88 us
    ppermute x1, waiting for transfers between devices, on_device(): from_below = lax.ppermute(sums[reach + count_tiles:], 'item', up)  7.6 us
  transfers between devices with their start and end apart: 8, of which 3 were waited for; matrix products, arithmetic and copies ran while one was open for 1% of the time, Pallas kernels for 18%

profile of v3, /device:TPU:24, one launch (start us, length us, event | category | flops | bytes accessed | tf_op | source)
XLA Modules:
  0.0 133.9 jit_solution(7998149852632482984)
XLA Ops:
  0.0 7.5 %prep.1 = (bf16[48,72,128]{2,1,0:T(8,128)(2,1)}, bf16[48,72,128]{2,1,0:T(8,128)(2,1)}, bf16[128,72,128]{2,1,0:T(8,128)(2,1)}) custom-call(s32[128]{0:T(128)} %bitcast.11, f32[64,12288]{1,0:T(8,128)} %ts_ref.5, s32[96,128]{1,0:T(8,128)} %bitcast.4, bf16[128,128,128]{2,1,0:T(8,128)(2,1)} %refs_1_.3), custom_call_target="tpu_custom_call" | custom-call | flops 1000000 | bytes 12000000 | tf_op jit(solution)/shard_map/prep/pallas_call | solution.py:527
  7.5 0.0 copy-start.8
  7.6 0.0 copy-start
  7.6 10.7 %all-to-all-start = ((bf16[128,72,128]{2,1,0:T(8,128)(2,1)}), bf16[128,72,128]{2,1,0:T(8,128)(2,1)}, u32[]{:S(2)}, u32[]{:S(2)}) async-start(bf16[128,72,128]{2,1,0:T(8,128)(2,1)} %get-tuple-element.19), calls=%async_computation | async-start | bytes 4718592 | tf_op jit(solution)/shard_map/all_to_all | solution.py:619
  18.3 7.5 %collective-permute-start.1 = (bf16[48,72,128]{2,1,0:T(8,128)(2,1)S(1)}, bf16[48,72,128]{2,1,0:T(8,128)(2,1)S(1)}, u32[]{:S(2)}, u32[]{:S(2)}) collective-permute-start(bf16[48,72,128]{2,1,0:T(8,128)(2,1)S(1)} %copy-done.3), channel_id=1, source_target_pairs={{1,0},{2,1},{3,2},{4,3},{5,4},{6,5},{7,6},{8,7},{9,8},{10,9},{11,1... | collective-permute-start | bytes 2654216 | tf_op jit(solution)/shard_map/ppermute | solution.py:618
  25.8 1.9 %collective-permute-start = (bf16[48,72,128]{2,1,0:T(8,128)(2,1)S(1)}, bf16[48,72,128]{2,1,0:T(8,128)(2,1)}, u32[]{:S(2)}, u32[]{:S(2)}) collective-permute-start(bf16[48,72,128]{2,1,0:T(8,128)(2,1)S(1)} %copy-done.2), channel_id=1, source_target_pairs={{0,1},{1,2},{2,3},{3,4},{4,5},{5,6},{6,7},{7,8},{8,9},{9,10},{10,1... | collective-permute-start | bytes 2654216 | tf_op jit(solution)/shard_map/ppermute | solution.py:617
  27.7 0.1 copy.8
  27.9 0.1 reshape.16.offsets_ref
  28.0 13.9 %band.2 = (f32[96,72,128]{2,1,0:T(8,128)}, f32[192,128]{1,0:T(8,128)S(1)}, s32[2048]{0:T(1024)S(1)}) custom-call(s32[384]{0:T(512)S(1)} %reshape.16.offsets_ref, f32[64,12288]{1,0:T(8,128)} %ts_ref.5, s32[96,128]{1,0:T(8,128)S(1)} %bitcast.5, bf16[48,72,128]{2,1,0:T(8,128)(2,1)S(1)} %copy-done.3, bf16[48,72,128]{2,1,0:T(8,128)(2,1)S(1)} %copy-done.2, ...), custom_call_target="tpu_custom_call" | custom-call | flops 99999997952 | bytes 20000000 | tf_op jit(solution)/shard_map/band/pallas_call | solution.py:551
  41.9 1.9 %collective-permute-start.2 = (f32[48,128]{1,0:T(8,128)S(1)}, f32[48,128]{1,0:T(8,128)S(1)}, u32[]{:S(2)}, u32[]{:S(2)}) collective-permute-start(f32[48,128]{1,0:T(8,128)S(1)} %get-tuple-element.27), channel_id=1, source_target_pairs={{0,1},{1,2},{2,3},{3,4},{4,5},{5,6},{6,7},{7,8},{8,9},{9,10},{10,1... | collective-permute-start | bytes 73736 | tf_op jit(solution)/shard_map/ppermute | solution.py:625
  43.8 7.9 %collective-permute-start.3 = (f32[48,128]{1,0:T(8,128)S(1)}, f32[48,128]{1,0:T(8,128)S(1)}, u32[]{:S(2)}, u32[]{:S(2)}) collective-permute-start(f32[48,128]{1,0:T(8,128)S(1)} %get-tuple-element.28), channel_id=1, source_target_pairs={{1,0},{2,1},{3,2},{4,3},{5,4},{6,5},{7,6},{8,7},{9,8},{10,9},{11,1... | collective-permute-start | bytes 73736 | tf_op jit(solution)/shard_map/ppermute | solution.py:626
  51.7 7.6 %collective-permute-done.2 = f32[48,128]{1,0:T(8,128)S(1)} collective-permute-done((f32[48,128]{1,0:T(8,128)S(1)}, f32[48,128]{1,0:T(8,128)S(1)}, u32[]{:S(2)}, u32[]{:S(2)}) %collective-permute-start.2) | collective-permute-done | bytes 24608 | tf_op jit(solution)/shard_map/ppermute | solution.py:625
  59.3 0.0 collective-permute-done.3
  59.3 0.6 maximum_add_fusion.refs_6_
  59.9 0.0 collective-permute-done.1.refs_4_
  59.9 1.0 copy-done.6
  60.9 14.6 %first.1 = (bf16[48,72,128]{2,1,0:T(8,128)(2,1)}, bf16[48,72,128]{2,1,0:T(8,128)(2,1)}, bf16[128,72,128]{2,1,0:T(8,128)(2,1)}, f32[96,128]{1,0:T(8,128)}, f32[8,128]{1,0:T(8,128)}) custom-call(s32[128]{0:T(128)} %bitcast.12, s32[128]{0:T(128)} %bitcast.9, s32[2048]{0:T(1024)} %copy-done.1, bf16[128,72,128]{2,1,0:T(8,128)(2,1)} %all-to-all-done.refs_0_, ...), custom_call_target="tpu_custom_call" | custom-call | flops 301989888 | bytes 20000000 | tf_op jit(solution)/shard_map/first/pallas_call | solution.py:585
  75.5 4.8 %all-to-all-start.1 = ((bf16[128,72,128]{2,1,0:T(8,128)(2,1)}), bf16[128,72,128]{2,1,0:T(8,128)(2,1)}, u32[]{:S(2)}, u32[]{:S(2)}) async-start(bf16[128,72,128]{2,1,0:T(8,128)(2,1)} %get-tuple-element.22), calls=%async_computation.1 | async-start | bytes 4718592 | tf_op jit(solution)/shard_map/all_to_all | solution.py:619
  80.4 7.4 %collective-permute-start.5 = (bf16[48,72,128]{2,1,0:T(8,128)(2,1)S(1)}, bf16[48,72,128]{2,1,0:T(8,128)(2,1)S(1)}, u32[]{:S(2)}, u32[]{:S(2)}) collective-permute-start(bf16[48,72,128]{2,1,0:T(8,128)(2,1)S(1)} %copy-done.5), channel_id=1, source_target_pairs={{1,0},{2,1},{3,2},{4,3},{5,4},{6,5},{7,6},{8,7},{9,8},{10,9},{11,1... | collective-permute-start | bytes 2654216 | tf_op jit(solution)/shard_map/ppermute | solution.py:618
  87.8 2.1 %collective-permute-start.4 = (bf16[48,72,128]{2,1,0:T(8,128)(2,1)S(1)}, bf16[48,72,128]{2,1,0:T(8,128)(2,1)}, u32[]{:S(2)}, u32[]{:S(2)}) collective-permute-start(bf16[48,72,128]{2,1,0:T(8,128)(2,1)S(1)} %copy-done.4), channel_id=1, source_target_pairs={{0,1},{1,2},{2,3},{3,4},{4,5},{5,6},{6,7},{7,8},{8,9},{9,10},{10,1... | collective-permute-start | bytes 2654216 | tf_op jit(solution)/shard_map/ppermute | solution.py:617
  89.9 10.6 %band.3.refs_2_ = f32[96,72,128]{2,1,0:T(8,128)} custom-call(s32[384]{0:T(512)S(1)} %reshape.16.offsets_ref, f32[64,12288]{1,0:T(8,128)} %ts_ref.5, s32[96,128]{1,0:T(8,128)S(1)} %bitcast.6, bf16[48,72,128]{2,1,0:T(8,128)(2,1)S(1)} %copy-done.5, bf16[48,72,128]{2,1,0:T(8,128)(2,1)S(1)} %copy-done.4, bf16[96,4,128,128]{3,2,1,0:T(8,128)(2,1)} %weights_ref.3), custom_call_target="tpu_custom_call" | custom-call | flops 99999997952 | bytes 20000000 | tf_op jit(solution)/shard_map/band/pallas_call | solution.py:551
  100.5 14.4 %collective-permute-done.5.refs_4_ = bf16[48,72,128]{2,1,0:T(8,128)(2,1)S(1)} collective-permute-done((bf16[48,72,128]{2,1,0:T(8,128)(2,1)S(1)}, bf16[48,72,128]{2,1,0:T(8,128)(2,1)S(1)}, u32[]{:S(2)}, u32[]{:S(2)}) %collective-permute-start.5) | collective-permute-done | bytes 884768 | tf_op jit(solution)/shard_map/ppermute | solution.py:618
  114.9 6.1 %collective-permute-done.4.refs_3_ = bf16[48,72,128]{2,1,0:T(8,128)(2,1)} collective-permute-done((bf16[48,72,128]{2,1,0:T(8,128)(2,1)S(1)}, bf16[48,72,128]{2,1,0:T(8,128)(2,1)}, u32[]{:S(2)}, u32[]{:S(2)}) %collective-permute-start.4) | collective-permute-done | bytes 884768 | tf_op jit(solution)/shard_map/ppermute | solution.py:617
  121.1 12.6 %last.1 = f32[64,12288]{1,0:T(8,128)} custom-call(s32[128]{0:T(128)} %bitcast.10, s32[2048]{0:T(1024)} %copy-done.1, bf16[128,72,128]{2,1,0:T(8,128)(2,1)} %all-to-all-done.1.refs_0_, bf16[128,128,128]{2,1,0:T(8,128)(2,1)} %refs_1_.3, f32[96,72,128]{2,1,0:T(8,128)} %band.3.refs_2_, bf16[48,72,128]{2,1,0:T(8,128)(2,1)} %collective-permute-done.4.refs_3_, ...), custom_call_target="tpu_custom_call" | custom-call | flops 301989888 | bytes 20000000 | tf_op jit(solution)/shard_map/last/pallas_call | solution.py:600
  (19 shorter events, 0.0 us)
Async XLA Ops:
  7.5 10.7 %copy-start.3 = (bf16[48,72,128]{2,1,0:T(8,128)(2,1)S(1)}, bf16[48,72,128]{2,1,0:T(8,128)(2,1)}, u32[]{:S(2)}) copy-start(bf16[48,72,128]{2,1,0:T(8,128)(2,1)} %get-tuple-element.16.low_ref) | copy-start | bytes 2654212
  7.5 18.3 %copy-start.2 = (bf16[48,72,128]{2,1,0:T(8,128)(2,1)S(1)}, bf16[48,72,128]{2,1,0:T(8,128)(2,1)}, u32[]{:S(2)}) copy-start(bf16[48,72,128]{2,1,0:T(8,128)(2,1)} %get-tuple-element.17.high_ref) | copy-start | bytes 2654212
  7.5 20.2 %copy-start.8 = (s32[96,4]{0,1:T(4,128)S(1)}, s32[96,4]{0,1:T(4,128)}, u32[]{:S(2)}) copy-start(s32[96,4]{0,1:T(4,128)} %param.9) | copy-start | bytes 4612
  7.6 20.4 %copy-start = (s32[12288]{0:T(1024)S(1)}, s32[12288]{0:T(1024)}, u32[]{:S(2)}) copy-start(s32[12288]{0:T(1024)} %param.8) | copy-start | bytes 147460
  7.6 52.4 %all-to-all-start = ((bf16[128,72,128]{2,1,0:T(8,128)(2,1)}), bf16[128,72,128]{2,1,0:T(8,128)(2,1)}, u32[]{:S(2)}, u32[]{:S(2)}) async-start(bf16[128,72,128]{2,1,0:T(8,128)(2,1)} %get-tuple-element.19), calls=%async_computation | async-start | bytes 4718592 | tf_op jit(solution)/shard_map/all_to_all | solution.py:619
  18.3 41.6 %collective-permute-start.1 = (bf16[48,72,128]{2,1,0:T(8,128)(2,1)S(1)}, bf16[48,72,128]{2,1,0:T(8,128)(2,1)S(1)}, u32[]{:S(2)}, u32[]{:S(2)}) collective-permute-start(bf16[48,72,128]{2,1,0:T(8,128)(2,1)S(1)} %copy-done.3), channel_id=1, source_target_pairs={{1,0},{2,1},{3,2},{4,3},{5,4},{6,5},{7,6},{8,7},{9,8},{10,9},{11,1... | collective-permute-start | bytes 2654216 | tf_op jit(solution)/shard_map/ppermute | solution.py:618
  25.8 34.1 %collective-permute-start = (bf16[48,72,128]{2,1,0:T(8,128)(2,1)S(1)}, bf16[48,72,128]{2,1,0:T(8,128)(2,1)}, u32[]{:S(2)}, u32[]{:S(2)}) collective-permute-start(bf16[48,72,128]{2,1,0:T(8,128)(2,1)S(1)} %copy-done.2), channel_id=1, source_target_pairs={{0,1},{1,2},{2,3},{3,4},{4,5},{5,6},{6,7},{7,8},{8,9},{9,10},{10,1... | collective-permute-start | bytes 2654216 | tf_op jit(solution)/shard_map/ppermute | solution.py:617
  41.8 18.1 %copy-start.1 = (s32[2048]{0:T(1024)}, s32[2048]{0:T(1024)S(1)}, u32[]{:S(2)}) copy-start(s32[2048]{0:T(1024)S(1)} %get-tuple-element.18.far_ref) | copy-start | bytes 24580
  41.9 17.4 %collective-permute-start.2 = (f32[48,128]{1,0:T(8,128)S(1)}, f32[48,128]{1,0:T(8,128)S(1)}, u32[]{:S(2)}, u32[]{:S(2)}) collective-permute-start(f32[48,128]{1,0:T(8,128)S(1)} %get-tuple-element.27), channel_id=1, source_target_pairs={{0,1},{1,2},{2,3},{3,4},{4,5},{5,6},{6,7},{7,8},{8,9},{9,10},{10,1... | collective-permute-start | bytes 73736 | tf_op jit(solution)/shard_map/ppermute | solution.py:625
  43.8 15.5 %collective-permute-start.3 = (f32[48,128]{1,0:T(8,128)S(1)}, f32[48,128]{1,0:T(8,128)S(1)}, u32[]{:S(2)}, u32[]{:S(2)}) collective-permute-start(f32[48,128]{1,0:T(8,128)S(1)} %get-tuple-element.28), channel_id=1, source_target_pairs={{1,0},{2,1},{3,2},{4,3},{5,4},{6,5},{7,6},{8,7},{9,8},{10,9},{11,1... | collective-permute-start | bytes 73736 | tf_op jit(solution)/shard_map/ppermute | solution.py:626
  59.9 1.0 copy-start.6
  75.5 4.8 %copy-start.5 = (bf16[48,72,128]{2,1,0:T(8,128)(2,1)S(1)}, bf16[48,72,128]{2,1,0:T(8,128)(2,1)}, u32[]{:S(2)}) copy-start(bf16[48,72,128]{2,1,0:T(8,128)(2,1)} %get-tuple-element.23.low_ref) | copy-start | bytes 2654212
  75.5 12.2 %copy-start.4 = (bf16[48,72,128]{2,1,0:T(8,128)(2,1)S(1)}, bf16[48,72,128]{2,1,0:T(8,128)(2,1)}, u32[]{:S(2)}) copy-start(bf16[48,72,128]{2,1,0:T(8,128)(2,1)} %get-tuple-element.24.high_ref) | copy-start | bytes 2654212
  75.5 45.5 %all-to-all-start.1 = ((bf16[128,72,128]{2,1,0:T(8,128)(2,1)}), bf16[128,72,128]{2,1,0:T(8,128)(2,1)}, u32[]{:S(2)}, u32[]{:S(2)}) async-start(bf16[128,72,128]{2,1,0:T(8,128)(2,1)} %get-tuple-element.22), calls=%async_computation.1 | async-start | bytes 4718592 | tf_op jit(solution)/shard_map/all_to_all | solution.py:619
  80.4 34.6 %collective-permute-start.5 = (bf16[48,72,128]{2,1,0:T(8,128)(2,1)S(1)}, bf16[48,72,128]{2,1,0:T(8,128)(2,1)S(1)}, u32[]{:S(2)}, u32[]{:S(2)}) collective-permute-start(bf16[48,72,128]{2,1,0:T(8,128)(2,1)S(1)} %copy-done.5), channel_id=1, source_target_pairs={{1,0},{2,1},{3,2},{4,3},{5,4},{6,5},{7,6},{8,7},{9,8},{10,9},{11,1... | collective-permute-start | bytes 2654216 | tf_op jit(solution)/shard_map/ppermute | solution.py:618
  87.8 33.3 %collective-permute-start.4 = (bf16[48,72,128]{2,1,0:T(8,128)(2,1)S(1)}, bf16[48,72,128]{2,1,0:T(8,128)(2,1)}, u32[]{:S(2)}, u32[]{:S(2)}) collective-permute-start(bf16[48,72,128]{2,1,0:T(8,128)(2,1)S(1)} %copy-done.4), channel_id=1, source_target_pairs={{0,1},{1,2},{2,3},{3,4},{4,5},{5,6},{6,7},{7,8},{8,9},{9,10},{10,1... | collective-permute-start | bytes 2654216 | tf_op jit(solution)/shard_map/ppermute | solution.py:617
  114.9 6.1 %copy-start.7 = (bf16[48,72,128]{2,1,0:T(8,128)(2,1)}, bf16[48,72,128]{2,1,0:T(8,128)(2,1)S(1)}, u32[]{:S(2)}) copy-start(bf16[48,72,128]{2,1,0:T(8,128)(2,1)S(1)} %collective-permute-done.5.refs_4_) | copy-start | bytes 2654212

commit v4 on v2

--- a/solution.py
+++ b/solution.py
@@ -15,6 +15,7 @@
 BAND_LOADS = 12
 PARTS = 4
 BAND_COST = 10**11
+MESSAGE_COST = 10**6
 VMEM = 60
 VMEM_ROUND = 60
 VMEM_BAND = 52
@@ -96,60 +97,78 @@
             copy.wait()
 
 
-def send_messages(send_ref, tiles, messages, out_ref, sems, first_sem, block, column_rows=None):
+def two_products(tiles, weights):
+    rows, width = tiles[0].shape
+    both = product(jnp.concatenate(tiles, axis=0), jnp.concatenate(weights, axis=0))
+    return both[:rows, :width], both[rows:, width:]
+
+
+def message_kernel(with_columns, send_ref, low_ref, high_ref, block_ref, *rest):
+    if with_columns:
+        remote_ref, out_ref, tiles, messages, block, sems, out_sems, remote, columns = rest
+    else:
+        out_ref, tiles, messages, block, sems, out_sems = rest
     count, rows, width = messages.shape
+    half = low_ref.shape[0]
+    loads = [
+        pltpu.make_async_copy(low_ref, tiles.at[pl.ds(0, half)], sems.at[0]),
+        pltpu.make_async_copy(high_ref, tiles.at[pl.ds(half, half)], sems.at[1]),
+        pltpu.make_async_copy(block_ref, block, sems.at[2]),
+    ]
+    for load in loads:
+        load.start()
     top = jnp.zeros((rows - EXTRA, width), F32)
-    if column_rows is None:
-        shared = stacked(top, block)
-    stores = []
     part = count // PARTS
+    if with_columns:
+        remote_loads = Loads([(remote_ref, remote, 0)], PARTS, sems, 3)
+        for i in range(PARTS):
+            remote_loads.start(i)
+    for load in loads:
+        load.wait()
+    shared = block[...]
+    stores = Loads([(messages, out_ref, 0)], PARTS, out_sems, 0)
     for number in range(PARTS):
+        if with_columns:
+            remote_loads.wait(number)
+
+            def column(k, carry, number=number):
+                q = number * part + k
+                columns[pl.ds(q, 1), :] = jnp.sum(remote[q].astype(F32), axis=0, keepdims=True)
+                return carry
+
+            lax.fori_loop(0, part, column, 0, unroll=8)
 
         def step(k, carry, number=number):
             q = number * part + k
-            if column_rows is None:
-                extra = shared
-            else:
-                high, low = pieces(column_rows[pl.ds(q, 1), :], 2)
-                extra = stacked(top, rows8({6: high, 7: low}, block))
-            messages[q] = tiles[send_ref[q]] + extra
+            extra = shared
+            if with_columns:
+                high, low = pieces(columns[pl.ds(q, 1), :], 2)
+                extra = rows8({6: high, 7: low}, shared)
+            messages[q] = tiles[send_ref[q]] + stacked(top, extra)
             return carry
 
         lax.fori_loop(0, part, step, 0, unroll=8)
-        at = pl.ds(number * part, part)
-        stores.append(
-            pltpu.make_async_copy(messages.at[at], out_ref.at[at], sems.at[first_sem + number])
-        )
-        stores[-1].start()
-    return stores
-
-
-def prep_kernel(
-    send_ref, ts_ref, counts_ref, remote_ref, low_ref, high_ref, out_ref,
-    ts, remote, tiles, messages, columns, sems, out_sems,
-):
-    channels, width = ts.shape[0], columns.shape[1]
-    count_tiles, shards = tiles.shape[0], messages.shape[0]
+        stores.start(number)
+    for number in range(PARTS):
+        stores.wait(number)
+
+
+def prep_kernel(ts_ref, counts_ref, low_ref, high_ref, block_ref, ts, tiles, sems, out_sems):
+    channels, width = ts.shape[0], counts_ref.shape[1]
+    count_tiles = tiles.shape[0]
     half = count_tiles // 2
-    here, group = count_tiles // LOADS, shards // LOADS
-    ts_loads = Loads([(ts_ref, ts, 1)], LOADS, sems, 0)
-    remote_loads = Loads([(remote_ref, remote, 0)], LOADS, sems, LOADS)
-    loads = [(ts_loads, i) for i in range(LOADS)] + [(remote_loads, i) for i in range(LOADS)]
-    for group_loads, i in loads[: 2 * AHEAD]:
-        group_loads.start(i)
-
-    def start_next(done):
-        for group_loads, i in loads[done + 2 * AHEAD : done + 2 * AHEAD + 1]:
-            group_loads.start(i)
-
+    here = count_tiles // LOADS
+    loads = Loads([(ts_ref, ts, 1)], LOADS, sems, 0)
+    for load in range(2 * AHEAD):
+        loads.start(load)
     stores = [
         pltpu.make_async_copy(tiles.at[pl.ds(0, half)], low_ref, out_sems.at[0]),
         pltpu.make_async_copy(tiles.at[pl.ds(half, half)], high_ref, out_sems.at[1]),
     ]
     part = jnp.zeros((channels, width), F32)
     for load in range(LOADS):
-        ts_loads.wait(load)
-        start_next(load)
+        loads.wait(load)
+        loads.start(load + 2 * AHEAD)
 
         def tile(k, part, load=load):
             t = load * here + k
@@ -164,21 +183,10 @@
         if load == LOADS // 2 - 1:
             stores[0].start()
     stores[1].start()
-    for load in range(LOADS):
-        remote_loads.wait(load)
-        start_next(LOADS + load)
-
-        def column(k, carry, load=load):
-            p = load * group + k
-            columns[pl.ds(p, 1), :] = jnp.sum(remote[p].astype(F32), axis=0, keepdims=True)
-            return carry
-
-        lax.fori_loop(0, group, column, 0, unroll=4)
     row = to_row(jnp.sum(part, axis=1, keepdims=True))
     row = row + at_lane(total(counts_ref[...].astype(F32)), channels)
     one, two, three = pieces(row, 3)
-    block = rows8({3: one, 4: two, 5: three})
-    stores += send_messages(send_ref, tiles, messages, out_ref, out_sems, 2, block, columns)
+    block_ref[...] = rows8({3: one, 4: two, 5: three})
     for store in stores:
         store.wait()
 
@@ -260,16 +268,18 @@
             band_loads.start(load + AHEAD - LOADS)
         loads.wait(load)
 
-        def tile(k, seen, load=load):
-            p = load * group + k
-            value = incoming[p]
-            tail = value.astype(F32)[rows - EXTRA :]
-            acc[landing_ref[p]] += product(value, weights[p])
-            if each is not None:
-                each(p, tail)
-            return seen + tail
-
-        seen = lax.fori_loop(0, group, tile, seen, unroll=16)
+        def pair(k, seen, load=load):
+            p = load * group + 2 * k
+            values = [incoming[p], incoming[p + 1]]
+            tails = [value.astype(F32)[rows - EXTRA :] for value in values]
+            mixed = two_products(values, [weights[p], weights[p + 1]])
+            for i in range(2):
+                acc[landing_ref[p + i]] += mixed[i]
+                if each is not None:
+                    each(p + i, tails[i])
+            return seen + (tails[0] + tails[1])
+
+        seen = lax.fori_loop(0, group // 2, pair, seen, unroll=8)
     for part in range(AHEAD, PARTS):
         band_loads.start(part)
     return seen, band_loads
@@ -277,8 +287,8 @@
 
 def first_kernel(
     send_ref, landing_ref, in_ref, weights_ref, band_ref, columns_ref,
-    low_ref, high_ref, out_ref, recip_ref, first_ref,
-    incoming, weights, band, acc, tiles, messages, columns, recips, firsts, sems, out_sems,
+    low_ref, high_ref, block_ref, recip_ref, first_ref,
+    incoming, weights, band, acc, tiles, columns, recips, firsts, block, sems, out_sems,
 ):
     shards, rows, width = incoming.shape
     channels = rows - EXTRA
@@ -333,17 +343,16 @@
             pltpu.make_async_copy(tiles.at[pl.ds(number * part, part)], ref.at[at], out_sems.at[number])
         )
         stores[-1].start()
-    for source, ref in ((recips, recip_ref), (firsts, first_ref)):
-        stores.append(pltpu.make_async_copy(source, ref, out_sems.at[len(stores)]))
-        stores[-1].start()
     all_totals, all_states, all_weights, all_recips = carry
     row = to_row(jnp.sum(all_totals, axis=1, keepdims=True))
     row = row + to_row(jnp.sum(all_states, axis=1, keepdims=True), channels)
     scalars = at_lane(total(all_weights), 0) + at_lane(total(all_recips), 1)
     one, two, three = pieces(row, 3)
     uno, due, tre = pieces(scalars, 3)
-    block = rows8({2: uno, 3: one, 4: two, 5: three, 6: due, 7: tre})
-    stores += send_messages(send_ref, tiles, messages, out_ref, out_sems, len(stores), block)
+    block[...] = rows8({2: uno, 3: one, 4: two, 5: three, 6: due, 7: tre})
+    for source, ref in ((recips, recip_ref), (firsts, first_ref), (block, block_ref)):
+        stores.append(pltpu.make_async_copy(source, ref, out_sems.at[len(stores)]))
+        stores[-1].start()
     for store in stores:
         store.wait()
 
@@ -437,25 +446,38 @@
     return pltpu.SemaphoreType.DMA((count,))
 
 
-def prep(send, ts, counts, remote_weights):
+def prep(ts, counts, shards):
     channels, columns = ts.shape
     count_tiles, width = counts.shape
-    shards = remote_weights.shape[0]
     rows = channels + EXTRA
-    tile, message = shapes(count_tiles, rows, shards)
+    tile, _ = shapes(count_tiles, rows, shards)
+    scratch = [pltpu.VMEM(ts.shape, F32), pltpu.VMEM((count_tiles, rows, width), BF16), sems(LOADS), sems(2)]
+    block = jax.ShapeDtypeStruct((EXTRA, width), F32)
+    return call(
+        prep_kernel, 0, [ANY, whole(counts.shape)], [ANY, ANY, whole(block.shape)], [tile, tile, block], scratch,
+        "prep", cost(10**6, 5 * 10**6),
+    )(ts, counts)
+
+
+def fill_messages(send, low, high, block, remote_weights=None):
+    half, rows, width = low.shape
+    shards = send.shape[0]
+    _, message = shapes(2 * half, rows, shards)
     scratch = [
-        pltpu.VMEM(ts.shape, F32),
-        pltpu.VMEM(remote_weights.shape, BF16),
-        pltpu.VMEM((count_tiles, rows, width), BF16),
+        pltpu.VMEM((2 * half, rows, width), BF16),
         pltpu.VMEM(message.shape, BF16),
-        pltpu.VMEM((shards, width), F32),
-        sems(2 * LOADS),
-        sems(2 + PARTS),
-    ]
+        pltpu.VMEM(block.shape, F32),
+        sems(3 + PARTS),
+        sems(PARTS),
+    ]
+    operands = [send, low, high, block]
+    if remote_weights is not None:
+        operands.append(remote_weights)
+        scratch += [pltpu.VMEM(remote_weights.shape, BF16), pltpu.VMEM((shards, width), F32)]
     return call(
-        prep_kernel, 1, [ANY, whole(counts.shape), ANY], [ANY] * 3, [tile, tile, message], scratch, "prep",
-        cost(10**6, 12 * 10**6),
-    )(send, ts, counts, remote_weights)
+        functools.partial(message_kernel, remote_weights is not None), 1, [ANY] * (len(operands) - 1), ANY,
+        message, scratch, "messages", cost(MESSAGE_COST, 5 * 10**6),
+    )(*operands)
 
 
 def band_product(with_ones, offsets, ts, counts, below, low, high, above, band_weights):
@@ -492,20 +514,20 @@
 def first_round(send, landing, incoming, remote_weights, mixed, columns):
     shards, rows, width = incoming.shape
     count_tiles = mixed.shape[0]
-    tile, message = shapes(count_tiles, rows, shards)
+    tile, _ = shapes(count_tiles, rows, shards)
     recip = jax.ShapeDtypeStruct((count_tiles, width), F32)
     first = jax.ShapeDtypeStruct((8, width), F32)
     scratch = round_scratch(incoming, remote_weights, mixed) + [
         pltpu.VMEM(mixed.shape, BF16),
-        pltpu.VMEM(incoming.shape, BF16),
         pltpu.VMEM(columns.shape, F32),
         pltpu.VMEM(recip.shape, F32),
         pltpu.VMEM(first.shape, F32),
+        pltpu.VMEM((EXTRA, width), F32),
         sems(PARTS + 2 * LOADS),
-        sems(2 + 2 * PARTS),
+        sems(3 + PARTS),
     ]
     return call(
-        first_kernel, 2, [ANY] * 4, [ANY] * 5, [tile, tile, message, recip, first], scratch, "first",
+        first_kernel, 2, [ANY] * 4, [ANY] * 5, [tile, tile, first, recip, first], scratch, "first",
         cost(2 * 128 * 72 * 128 * 128, 20 * 10**6), VMEM_ROUND,
     )(send, landing, incoming, remote_weights, mixed, columns)
 
@@ -535,20 +557,21 @@
     up = [(i, i + 1) for i in range(shards - 1)]
     down = [(i + 1, i) for i in range(shards - 1)]
 
-    def exchange(low, high, outgoing):
+    def exchange(low, high, block, *weights):
         below = lax.ppermute(high, "item", up)
         above = lax.ppermute(low, "item", down)
+        outgoing = fill_messages(send, low, high, block, *weights)
         incoming = lax.all_to_all(outgoing, "item", split_axis=0, concat_axis=0, tiled=True)
         return below, above, incoming
 
-    low, high, outgoing = prep(send, target_sums, counts, remote_weights)
-    below, above, incoming = exchange(low, high, outgoing)
+    low, high, block = prep(target_sums, counts, shards)
+    below, above, incoming = exchange(low, high, block, remote_weights)
     mixed, sums = band_product(True, offsets, target_sums, counts, below, low, high, above, band_weights)
     from_below = lax.ppermute(sums[reach + count_tiles :], "item", up)
     from_above = lax.ppermute(sums[:reach], "item", down)
     columns = sums[reach : reach + count_tiles] + jnp.concatenate([from_below, from_above], axis=0)
-    low, high, outgoing, recip, first = first_round(send, landing, incoming, remote_weights, mixed, columns)
-    below, above, incoming = exchange(low, high, outgoing)
+    low, high, block, recip, first = first_round(send, landing, incoming, remote_weights, mixed, columns)
+    below, above, incoming = exchange(low, high, block)
     (mixed,) = band_product(False, offsets, target_sums, counts, below, low, high, above, band_weights)
     return last_round(landing, incoming, remote_weights, mixed, recip, first)
 

time: 150 us -> 129 us (0.86)
  the two profiles are of different devices: /device:TPU:27 before, /device:TPU:1 now
where the time goes in v4:
time: 129 us
  Pallas kernels  51 us (40%)
  starting transfers between devices  40.2 us (31%)
  waiting for transfers between devices  34.3 us (27%)
  local copies, waits for them, and re-layouts  2.14 us (2%)
    all_to_all x2, waiting for transfers between devices, exchange(): lax.all_to_all(outgoing, 'item', split_axis=0, concat_axis=0, tiled=True)  29.9 us
    pallas_call x2, Pallas kernels, band_product(): call(functools.partial(band_kernel, with_ones), 1, [ANY, whole(counts.sha...  22.7 us
    all_to_all x2, starting transfers between devices, exchange(): lax.all_to_all(outgoing, 'item', split_axis=0, concat_axis=0, tiled=True)  22.2 us
    pallas_call x2, Pallas kernels, fill_messages(): call(functools.partial(message_kernel, remote_weights is not None), 1, [A...  8.41 us
    pallas_call x1, Pallas kernels, first_round(): call(first_kernel, 2, [ANY] * 4, [ANY] * 5, [tile, tile, first, recip, fi...  8.04 us
    pallas_call x1, Pallas kernels, last_round(): call(last_kernel, 1, [ANY] * 5, ANY, jax.ShapeDtypeStruct(shape, F32), sc...  7.08 us
    ppermute x2, starting transfers between devices, exchange(): above = lax.ppermute(low, 'item', down)  6.78 us
    ppermute x2, starting transfers between devices, exchange(): below = lax.ppermute(high, 'item', up)  5.64 us
  transfers between devices with their start and end apart: 8, of which 3 were waited for; matrix products, arithmetic and copies ran while one was open for 1% of the time, Pallas kernels for 24%

profile of v4, /device:TPU:1, one launch (start us, length us, event | category | flops | bytes accessed | tf_op | source)
XLA Modules:
  0.0 128.6 jit_solution(13351328680986426166)
XLA Ops:
  0.0 4.7 %prep.1 = (bf16[48,72,128]{2,1,0:T(8,128)(2,1)}, bf16[48,72,128]{2,1,0:T(8,128)(2,1)}, f32[8,128]{1,0:T(8,128)}) custom-call(f32[64,12288]{1,0:T(8,128)} %ts_ref.5, s32[96,128]{1,0:T(8,128)} %bitcast.3), custom_call_target="tpu_custom_call" | custom-call | flops 1000000 | bytes 5000000 | tf_op jit(solution)/shard_map/prep/pallas_call | solution.py:456
  4.7 3.3 %collective-permute-start.1 = (bf16[48,72,128]{2,1,0:T(8,128)(2,1)}, bf16[48,72,128]{2,1,0:T(8,128)(2,1)S(1)}, u32[]{:S(2)}, u32[]{:S(2)}) collective-permute-start(bf16[48,72,128]{2,1,0:T(8,128)(2,1)} %get-tuple-element.15.low_ref), channel_id=1, source_target_pairs={{1,0},{2,1},{3,2},{4,3},{5,4},{6,5},{7,6},{8,7},{9,8},{10,9},{11,1... | collective-permute-start | bytes 2654216 | tf_op jit(solution)/shard_map/ppermute | solution.py:562
  8.1 3.5 %collective-permute-start = (bf16[48,72,128]{2,1,0:T(8,128)(2,1)}, bf16[48,72,128]{2,1,0:T(8,128)(2,1)S(1)}, u32[]{:S(2)}, u32[]{:S(2)}) collective-permute-start(bf16[48,72,128]{2,1,0:T(8,128)(2,1)} %get-tuple-element.16.high_ref), channel_id=1, source_target_pairs={{0,1},{1,2},{2,3},{3,4},{4,5},{5,6},{6,7},{7,8},{8,9},{9,10},{10,1... | collective-permute-start | bytes 2654216 | tf_op jit(solution)/shard_map/ppermute | solution.py:561
  11.6 4.7 %messages.2 = bf16[128,72,128]{2,1,0:T(8,128)(2,1)} custom-call(s32[128]{0:T(128)} %bitcast.6, bf16[48,72,128]{2,1,0:T(8,128)(2,1)} %get-tuple-element.15.low_ref, bf16[48,72,128]{2,1,0:T(8,128)(2,1)} %get-tuple-element.16.high_ref, f32[8,128]{1,0:T(8,128)} %get-tuple-element.17.block_ref, bf16[128,128,128]{2,1,0:T(8,128)(2,1)} %weights_ref.7), custom_call_target="tpu_custom_call" | custom-call | flops 1000000 | bytes 5000000 | tf_op jit(solution)/shard_map/messages/pallas_call | solution.py:477
  16.3 0.0 copy-start.3
  16.4 14.0 %all-to-all-start = ((bf16[128,72,128]{2,1,0:T(8,128)(2,1)}), bf16[128,72,128]{2,1,0:T(8,128)(2,1)}, u32[]{:S(2)}, u32[]{:S(2)}) async-start(bf16[128,72,128]{2,1,0:T(8,128)(2,1)} %messages.2), calls=%async_computation | async-start | bytes 4718592 | tf_op jit(solution)/shard_map/all_to_all | solution.py:564
  30.4 0.1 copy.8
  30.5 0.1 reshape.15.offsets_ref
  30.6 0.9 copy-done.4
  31.5 11.5 %band.2 = (f32[96,72,128]{2,1,0:T(8,128)}, f32[192,128]{1,0:T(8,128)S(1)}) custom-call(s32[384]{0:T(512)S(1)} %reshape.15.offsets_ref, f32[64,12288]{1,0:T(8,128)} %ts_ref.5, s32[96,128]{1,0:T(8,128)S(1)} %bitcast.4, bf16[48,72,128]{2,1,0:T(8,128)(2,1)S(1)} %collective-permute-done.below_ref, bf16[48,72,128]{2,1,0:T(8,128)(2,1)S(1)} %copy-done.1, ...), custom_call_target="tpu_custom_call" | custom-call | flops 99999997952 | bytes 20000000 | tf_op jit(solution)/shard_map/band/pallas_call | solution.py:499
  43.0 3.6 %collective-permute-start.2 = (f32[48,128]{1,0:T(8,128)S(1)}, f32[48,128]{1,0:T(8,128)S(1)}, u32[]{:S(2)}, u32[]{:S(2)}) collective-permute-start(f32[48,128]{1,0:T(8,128)S(1)} %get-tuple-element.25), channel_id=1, source_target_pairs={{0,1},{1,2},{2,3},{3,4},{4,5},{5,6},{6,7},{7,8},{8,9},{9,10},{10,1... | collective-permute-start | bytes 73736 | tf_op jit(solution)/shard_map/ppermute | solution.py:570
  46.7 1.9 %collective-permute-start.3 = (f32[48,128]{1,0:T(8,128)S(1)}, f32[48,128]{1,0:T(8,128)S(1)}, u32[]{:S(2)}, u32[]{:S(2)}) collective-permute-start(f32[48,128]{1,0:T(8,128)S(1)} %get-tuple-element.26), channel_id=1, source_target_pairs={{1,0},{2,1},{3,2},{4,3},{5,4},{6,5},{7,6},{8,7},{9,8},{10,9},{11,1... | collective-permute-start | bytes 73736 | tf_op jit(solution)/shard_map/ppermute | solution.py:571
  48.6 4.4 %collective-permute-done.3 = f32[48,128]{1,0:T(8,128)S(1)} collective-permute-done((f32[48,128]{1,0:T(8,128)S(1)}, f32[48,128]{1,0:T(8,128)S(1)}, u32[]{:S(2)}, u32[]{:S(2)}) %collective-permute-start.3) | collective-permute-done | bytes 24608 | tf_op jit(solution)/shard_map/ppermute | solution.py:571
  53.0 0.6 maximum_add_fusion.columns_ref
  53.6 9.5 %all-to-all-done.in_ref = bf16[128,72,128]{2,1,0:T(8,128)(2,1)} async-done(((bf16[128,72,128]{2,1,0:T(8,128)(2,1)}), bf16[128,72,128]{2,1,0:T(8,128)(2,1)}, u32[]{:S(2)}, u32[]{:S(2)}) %all-to-all-start) | async-done | bytes 2359328 | tf_op jit(solution)/shard_map/all_to_all | solution.py:564
  63.1 8.0 %first.1 = (bf16[48,72,128]{2,1,0:T(8,128)(2,1)}, bf16[48,72,128]{2,1,0:T(8,128)(2,1)}, f32[8,128]{1,0:T(8,128)}, f32[96,128]{1,0:T(8,128)}, f32[8,128]{1,0:T(8,128)}) custom-call(s32[128]{0:T(128)} %bitcast.7, s32[128]{0:T(128)} %bitcast.9, bf16[128,72,128]{2,1,0:T(8,128)(2,1)} %all-to-all-done.in_ref, bf16[128,128,128]{2,1,0:T(8,128)(2,1)} %weights_ref.7, ...), custom_call_target="tpu_custom_call" | custom-call | flops 301989888 | bytes 20000000 | tf_op jit(solution)/shard_map/first/pallas_call | solution.py:529
  71.2 3.5 %collective-permute-start.5 = (bf16[48,72,128]{2,1,0:T(8,128)(2,1)}, bf16[48,72,128]{2,1,0:T(8,128)(2,1)S(1)}, u32[]{:S(2)}, u32[]{:S(2)}) collective-permute-start(bf16[48,72,128]{2,1,0:T(8,128)(2,1)} %get-tuple-element.20.low_ref), channel_id=1, source_target_pairs={{1,0},{2,1},{3,2},{4,3},{5,4},{6,5},{7,6},{8,7},{9,8},{10,9},{11,1... | collective-permute-start | bytes 2654216 | tf_op jit(solution)/shard_map/ppermute | solution.py:562
  74.6 2.1 %collective-permute-start.4 = (bf16[48,72,128]{2,1,0:T(8,128)(2,1)}, bf16[48,72,128]{2,1,0:T(8,128)(2,1)S(1)}, u32[]{:S(2)}, u32[]{:S(2)}) collective-permute-start(bf16[48,72,128]{2,1,0:T(8,128)(2,1)} %get-tuple-element.21.high_ref), channel_id=1, source_target_pairs={{0,1},{1,2},{2,3},{3,4},{4,5},{5,6},{6,7},{7,8},{8,9},{9,10},{10,1... | collective-permute-start | bytes 2654216 | tf_op jit(solution)/shard_map/ppermute | solution.py:561
  76.7 3.7 %messages.3 = bf16[128,72,128]{2,1,0:T(8,128)(2,1)} custom-call(s32[128]{0:T(128)} %bitcast.8, bf16[48,72,128]{2,1,0:T(8,128)(2,1)} %get-tuple-element.20.low_ref, bf16[48,72,128]{2,1,0:T(8,128)(2,1)} %get-tuple-element.21.high_ref, f32[8,128]{1,0:T(8,128)} %get-tuple-element.22.block_ref), custom_call_target="tpu_custom_call" | custom-call | flops 1000000 | bytes 5000000 | tf_op jit(solution)/shard_map/messages/pallas_call | solution.py:477
  80.4 8.2 %all-to-all-start.1 = ((bf16[128,72,128]{2,1,0:T(8,128)(2,1)}), bf16[128,72,128]{2,1,0:T(8,128)(2,1)}, u32[]{:S(2)}, u32[]{:S(2)}) async-start(bf16[128,72,128]{2,1,0:T(8,128)(2,1)} %messages.3), calls=%async_computation.1 | async-start | bytes 4718592 | tf_op jit(solution)/shard_map/all_to_all | solution.py:564
  88.7 1.0 copy-done.5
  89.7 11.2 %band.3.band_ref = f32[96,72,128]{2,1,0:T(8,128)} custom-call(s32[384]{0:T(512)S(1)} %reshape.15.offsets_ref, f32[64,12288]{1,0:T(8,128)} %ts_ref.5, s32[96,128]{1,0:T(8,128)S(1)} %bitcast.5, bf16[48,72,128]{2,1,0:T(8,128)(2,1)S(1)} %collective-permute-done.4.below_ref, bf16[48,72,128]{2,1,0:T(8,128)(2,1)S(1)} %copy-done, ...), custom_call_target="tpu_custom_call" | custom-call | flops 99999997952 | bytes 20000000 | tf_op jit(solution)/shard_map/band/pallas_call | solution.py:499
  101.0 20.4 %all-to-all-done.1.in_ref = bf16[128,72,128]{2,1,0:T(8,128)(2,1)} async-done(((bf16[128,72,128]{2,1,0:T(8,128)(2,1)}), bf16[128,72,128]{2,1,0:T(8,128)(2,1)}, u32[]{:S(2)}, u32[]{:S(2)}) %all-to-all-start.1) | async-done | bytes 2359328 | tf_op jit(solution)/shard_map/all_to_all | solution.py:564
  121.4 7.1 %last.1 = f32[64,12288]{1,0:T(8,128)} custom-call(s32[128]{0:T(128)} %bitcast.10, bf16[128,72,128]{2,1,0:T(8,128)(2,1)} %all-to-all-done.1.in_ref, bf16[128,128,128]{2,1,0:T(8,128)(2,1)} %weights_ref.7, f32[96,72,128]{2,1,0:T(8,128)} %band.3.band_ref, f32[96,128]{1,0:T(8,128)} %get-tuple-element.23.recip_ref, f32[8,128]{1,0:T(8,128)} %get-tuple-element.24.first_ref), custom_call_target="tpu_custom_call" | custom-call | flops 301989888 | bytes 20000000 | tf_op jit(solution)/shard_map/last/pallas_call | solution.py:545
  (15 shorter events, 0.0 us)
Async XLA Ops:
  4.7 25.9 %collective-permute-start.1 = (bf16[48,72,128]{2,1,0:T(8,128)(2,1)}, bf16[48,72,128]{2,1,0:T(8,128)(2,1)S(1)}, u32[]{:S(2)}, u32[]{:S(2)}) collective-permute-start(bf16[48,72,128]{2,1,0:T(8,128)(2,1)} %get-tuple-element.15.low_ref), channel_id=1, source_target_pairs={{1,0},{2,1},{3,2},{4,3},{5,4},{6,5},{7,6},{8,7},{9,8},{10,9},{11,1... | collective-permute-start | bytes 2654216 | tf_op jit(solution)/shard_map/ppermute | solution.py:562
  8.1 22.6 %collective-permute-start = (bf16[48,72,128]{2,1,0:T(8,128)(2,1)}, bf16[48,72,128]{2,1,0:T(8,128)(2,1)S(1)}, u32[]{:S(2)}, u32[]{:S(2)}) collective-permute-start(bf16[48,72,128]{2,1,0:T(8,128)(2,1)} %get-tuple-element.16.high_ref), channel_id=1, source_target_pairs={{0,1},{1,2},{2,3},{3,4},{4,5},{5,6},{6,7},{7,8},{8,9},{9,10},{10,1... | collective-permute-start | bytes 2654216 | tf_op jit(solution)/shard_map/ppermute | solution.py:561
  16.3 14.0 %copy-start.3 = (s32[96,4]{0,1:T(4,128)S(1)}, s32[96,4]{0,1:T(4,128)}, u32[]{:S(2)}) copy-start(s32[96,4]{0,1:T(4,128)} %param.9) | copy-start | bytes 4612
  16.4 15.2 %copy-start.1 = (bf16[48,72,128]{2,1,0:T(8,128)(2,1)S(1)}, bf16[48,72,128]{2,1,0:T(8,128)(2,1)}, u32[]{:S(2)}) copy-start(bf16[48,72,128]{2,1,0:T(8,128)(2,1)} %get-tuple-element.15.low_ref) | copy-start | bytes 2654212
  16.4 15.2 %copy-start.2 = (s32[12288]{0:T(1024)S(1)}, s32[12288]{0:T(1024)}, u32[]{:S(2)}) copy-start(s32[12288]{0:T(1024)} %param.8) | copy-start | bytes 147460
  16.4 46.7 %all-to-all-start = ((bf16[128,72,128]{2,1,0:T(8,128)(2,1)}), bf16[128,72,128]{2,1,0:T(8,128)(2,1)}, u32[]{:S(2)}, u32[]{:S(2)}) async-start(bf16[128,72,128]{2,1,0:T(8,128)(2,1)} %messages.2), calls=%async_computation | async-start | bytes 4718592 | tf_op jit(solution)/shard_map/all_to_all | solution.py:564
  30.6 0.9 copy-start.4
  43.0 5.6 %collective-permute-start.2 = (f32[48,128]{1,0:T(8,128)S(1)}, f32[48,128]{1,0:T(8,128)S(1)}, u32[]{:S(2)}, u32[]{:S(2)}) collective-permute-start(f32[48,128]{1,0:T(8,128)S(1)} %get-tuple-element.25), channel_id=1, source_target_pairs={{0,1},{1,2},{2,3},{3,4},{4,5},{5,6},{6,7},{7,8},{8,9},{9,10},{10,1... | collective-permute-start | bytes 73736 | tf_op jit(solution)/shard_map/ppermute | solution.py:570
  46.7 6.3 %collective-permute-start.3 = (f32[48,128]{1,0:T(8,128)S(1)}, f32[48,128]{1,0:T(8,128)S(1)}, u32[]{:S(2)}, u32[]{:S(2)}) collective-permute-start(f32[48,128]{1,0:T(8,128)S(1)} %get-tuple-element.26), channel_id=1, source_target_pairs={{1,0},{2,1},{3,2},{4,3},{5,4},{6,5},{7,6},{8,7},{9,8},{10,9},{11,1... | collective-permute-start | bytes 73736 | tf_op jit(solution)/shard_map/ppermute | solution.py:571
  71.2 17.5 %collective-permute-start.5 = (bf16[48,72,128]{2,1,0:T(8,128)(2,1)}, bf16[48,72,128]{2,1,0:T(8,128)(2,1)S(1)}, u32[]{:S(2)}, u32[]{:S(2)}) collective-permute-start(bf16[48,72,128]{2,1,0:T(8,128)(2,1)} %get-tuple-element.20.low_ref), channel_id=1, source_target_pairs={{1,0},{2,1},{3,2},{4,3},{5,4},{6,5},{7,6},{8,7},{9,8},{10,9},{11,1... | collective-permute-start | bytes 2654216 | tf_op jit(solution)/shard_map/ppermute | solution.py:562
  74.6 14.1 %collective-permute-start.4 = (bf16[48,72,128]{2,1,0:T(8,128)(2,1)}, bf16[48,72,128]{2,1,0:T(8,128)(2,1)S(1)}, u32[]{:S(2)}, u32[]{:S(2)}) collective-permute-start(bf16[48,72,128]{2,1,0:T(8,128)(2,1)} %get-tuple-element.21.high_ref), channel_id=1, source_target_pairs={{0,1},{1,2},{2,3},{3,4},{4,5},{5,6},{6,7},{7,8},{8,9},{9,10},{10,1... | collective-permute-start | bytes 2654216 | tf_op jit(solution)/shard_map/ppermute | solution.py:561
  80.4 9.3 %copy-start = (bf16[48,72,128]{2,1,0:T(8,128)(2,1)S(1)}, bf16[48,72,128]{2,1,0:T(8,128)(2,1)}, u32[]{:S(2)}) copy-start(bf16[48,72,128]{2,1,0:T(8,128)(2,1)} %get-tuple-element.20.low_ref) | copy-start | bytes 2654212
  80.4 40.9 %all-to-all-start.1 = ((bf16[128,72,128]{2,1,0:T(8,128)(2,1)}), bf16[128,72,128]{2,1,0:T(8,128)(2,1)}, u32[]{:S(2)}, u32[]{:S(2)}) async-start(bf16[128,72,128]{2,1,0:T(8,128)(2,1)} %messages.3), calls=%async_computation.1 | async-start | bytes 4718592 | tf_op jit(solution)/shard_map/all_to_all | solution.py:564
  88.7 1.0 copy-start.5

commit v5 on v4

--- a/solution.py
+++ b/solution.py
@@ -103,16 +103,36 @@
     return both[:rows, :width], both[rows:, width:]
 
 
-def message_kernel(with_columns, send_ref, low_ref, high_ref, block_ref, *rest):
+class Halves:
+    def __init__(self, odd, tiles, half, inner_ref, outer_ref, sems, first, parts):
+        self.odd, self.copies, size = odd, [], half // (parts // 2)
+        for i in range(parts):
+            source, at = tiles.at[pl.ds(i * size, size)], pl.ds(i * size % half, size)
+            inner = pltpu.make_async_copy(source, inner_ref.at[at], sems.at[first + i])
+            outer = pltpu.make_async_copy(source, outer_ref.at[at], sems.at[first + i])
+            upper = i >= parts // 2
+            self.copies.append((outer, inner) if upper else (inner, outer))
+
+    def start(self, i):
+        pl.when(self.odd == 1)(self.copies[i][0].start)
+        pl.when(self.odd == 0)(self.copies[i][1].start)
+
+    def wait(self, i):
+        pl.when(self.odd == 1)(self.copies[i][0].wait)
+        pl.when(self.odd == 0)(self.copies[i][1].wait)
+
+
+def message_kernel(with_columns, odd_ref, send_ref, inner_ref, outer_ref, block_ref, *rest):
     if with_columns:
         remote_ref, out_ref, tiles, messages, block, sems, out_sems, remote, columns = rest
     else:
         out_ref, tiles, messages, block, sems, out_sems = rest
     count, rows, width = messages.shape
-    half = low_ref.shape[0]
+    half = inner_ref.shape[0]
+    odd = odd_ref[0]
     loads = [
-        pltpu.make_async_copy(low_ref, tiles.at[pl.ds(0, half)], sems.at[0]),
-        pltpu.make_async_copy(high_ref, tiles.at[pl.ds(half, half)], sems.at[1]),
+        pltpu.make_async_copy(inner_ref, tiles.at[pl.ds((1 - odd) * half, half)], sems.at[0]),
+        pltpu.make_async_copy(outer_ref, tiles.at[pl.ds(odd * half, half)], sems.at[1]),
         pltpu.make_async_copy(block_ref, block, sems.at[2]),
     ]
     for load in loads:
@@ -153,7 +173,7 @@
         stores.wait(number)
 
 
-def prep_kernel(ts_ref, counts_ref, low_ref, high_ref, block_ref, ts, tiles, sems, out_sems):
+def prep_kernel(odd_ref, ts_ref, counts_ref, inner_ref, outer_ref, block_ref, ts, tiles, sems, out_sems):
     channels, width = ts.shape[0], counts_ref.shape[1]
     count_tiles = tiles.shape[0]
     half = count_tiles // 2
@@ -161,10 +181,7 @@
     loads = Loads([(ts_ref, ts, 1)], LOADS, sems, 0)
     for load in range(2 * AHEAD):
         loads.start(load)
-    stores = [
-        pltpu.make_async_copy(tiles.at[pl.ds(0, half)], low_ref, out_sems.at[0]),
-        pltpu.make_async_copy(tiles.at[pl.ds(half, half)], high_ref, out_sems.at[1]),
-    ]
+    stores = Halves(odd_ref[0], tiles, half, inner_ref, outer_ref, out_sems, 0, PARTS)
     part = jnp.zeros((channels, width), F32)
     for load in range(LOADS):
         loads.wait(load)
@@ -180,32 +197,36 @@
             return part + block
 
         part = lax.fori_loop(0, here, tile, part, unroll=4)
-        if load == LOADS // 2 - 1:
-            stores[0].start()
-    stores[1].start()
+        if (load + 1) % (LOADS // PARTS) == 0:
+            stores.start(load // (LOADS // PARTS))
     row = to_row(jnp.sum(part, axis=1, keepdims=True))
     row = row + at_lane(total(counts_ref[...].astype(F32)), channels)
     one, two, three = pieces(row, 3)
     block_ref[...] = rows8({3: one, 4: two, 5: three})
-    for store in stores:
-        store.wait()
+    for i in range(PARTS):
+        stores.wait(i)
 
 
 def band_kernel(
-    with_ones, offsets_ref, ts_ref, counts_ref, below_ref, low_ref, high_ref, above_ref, weights_ref, out_ref, *rest
+    with_ones, odd_ref, offsets_ref, ts_ref, counts_ref, inner_ref, outer_ref, from_inner_ref, from_outer_ref,
+    weights_ref, out_ref, *rest
 ):
     if with_ones:
         sums_ref, ts, weights, window, result, sems, out_sems = rest
     else:
         ts, weights, window, result, sems, out_sems = rest
     count_tiles, band = weights.shape[:2]
-    reach, rows, width = below_ref.shape
+    reach, rows, width = inner_ref.shape
     channels = rows - EXTRA
     here = count_tiles // BAND_LOADS
+    odd = odd_ref[0]
     parts = []
-    for i, ref in enumerate((below_ref, low_ref, high_ref, above_ref)):
-        parts.append(pltpu.make_async_copy(ref, window.at[pl.ds(i * reach, reach)], sems.at[2 * BAND_LOADS + i]))
-        parts[-1].start()
+    for i, (ref, at) in enumerate(
+        ((inner_ref, 2 - odd), (outer_ref, 1 + odd), (from_inner_ref, 3 - 3 * odd), (from_outer_ref, 3 * odd))
+    ):
+        copy = pltpu.make_async_copy(ref, window.at[pl.ds(at * reach, reach)], sems.at[2 * BAND_LOADS + i])
+        copy.start()
+        parts.append(copy)
     loads = Loads([(weights_ref, weights, 0), (ts_ref, ts, 1)], BAND_LOADS, sems, 0)
     for load in range(AHEAD):
         loads.start(load)
@@ -286,8 +307,8 @@
 
 
 def first_kernel(
-    send_ref, landing_ref, in_ref, weights_ref, band_ref, columns_ref,
-    low_ref, high_ref, block_ref, recip_ref, first_ref,
+    odd_ref, send_ref, landing_ref, in_ref, weights_ref, band_ref, columns_ref,
+    inner_ref, outer_ref, block_ref, recip_ref, first_ref,
     incoming, weights, band, acc, tiles, columns, recips, firsts, block, sems, out_sems,
 ):
     shards, rows, width = incoming.shape
@@ -312,6 +333,7 @@
     line = jnp.zeros((1, width), F32)
     carry = (zero, zero, line, line)
     stores = []
+    halves = Halves(odd_ref[0], tiles, half, inner_ref, outer_ref, out_sems, 3, PARTS)
     part = count_tiles // PARTS
     for number in range(PARTS):
         band_loads.wait(number)
@@ -337,12 +359,7 @@
             )
 
         carry = lax.fori_loop(0, part, finish, carry, unroll=4)
-        ref = low_ref if number < PARTS // 2 else high_ref
-        at = pl.ds(number * part % half, part)
-        stores.append(
-            pltpu.make_async_copy(tiles.at[pl.ds(number * part, part)], ref.at[at], out_sems.at[number])
-        )
-        stores[-1].start()
+        halves.start(number)
     all_totals, all_states, all_weights, all_recips = carry
     row = to_row(jnp.sum(all_totals, axis=1, keepdims=True))
     row = row + to_row(jnp.sum(all_states, axis=1, keepdims=True), channels)
@@ -355,6 +372,8 @@
         stores[-1].start()
     for store in stores:
         store.wait()
+    for number in range(PARTS):
+        halves.wait(number)
 
 
 def last_kernel(
@@ -446,21 +465,21 @@
     return pltpu.SemaphoreType.DMA((count,))
 
 
-def prep(ts, counts, shards):
+def prep(odd, ts, counts, shards):
     channels, columns = ts.shape
     count_tiles, width = counts.shape
     rows = channels + EXTRA
     tile, _ = shapes(count_tiles, rows, shards)
-    scratch = [pltpu.VMEM(ts.shape, F32), pltpu.VMEM((count_tiles, rows, width), BF16), sems(LOADS), sems(2)]
+    scratch = [pltpu.VMEM(ts.shape, F32), pltpu.VMEM((count_tiles, rows, width), BF16), sems(LOADS), sems(PARTS)]
     block = jax.ShapeDtypeStruct((EXTRA, width), F32)
     return call(
-        prep_kernel, 0, [ANY, whole(counts.shape)], [ANY, ANY, whole(block.shape)], [tile, tile, block], scratch,
+        prep_kernel, 1, [ANY, whole(counts.shape)], [ANY, ANY, whole(block.shape)], [tile, tile, block], scratch,
         "prep", cost(10**6, 5 * 10**6),
-    )(ts, counts)
-
-
-def fill_messages(send, low, high, block, remote_weights=None):
-    half, rows, width = low.shape
+    )(odd, ts, counts)
+
+
+def fill_messages(odd, send, inner, outer, block, remote_weights=None):
+    half, rows, width = inner.shape
     shards = send.shape[0]
     _, message = shapes(2 * half, rows, shards)
     scratch = [
@@ -470,19 +489,19 @@
         sems(3 + PARTS),
         sems(PARTS),
     ]
-    operands = [send, low, high, block]
+    operands = [odd, send, inner, outer, block]
     if remote_weights is not None:
         operands.append(remote_weights)
         scratch += [pltpu.VMEM(remote_weights.shape, BF16), pltpu.VMEM((shards, width), F32)]
     return call(
-        functools.partial(message_kernel, remote_weights is not None), 1, [ANY] * (len(operands) - 1), ANY,
+        functools.partial(message_kernel, remote_weights is not None), 2, [ANY] * (len(operands) - 2), ANY,
         message, scratch, "messages", cost(MESSAGE_COST, 5 * 10**6),
     )(*operands)
 
 
-def band_product(with_ones, offsets, ts, counts, below, low, high, above, band_weights):
+def band_product(with_ones, odd, offsets, ts, counts, inner, outer, from_inner, from_outer, band_weights):
     count_tiles, _, width, _ = band_weights.shape
-    rows = low.shape[1]
+    rows = inner.shape[1]
     shape = (count_tiles, rows, width)
     scratch = [
         pltpu.VMEM(ts.shape, F32),
@@ -497,9 +516,9 @@
         out_shape.append(jax.ShapeDtypeStruct((2 * count_tiles, width), F32))
         out_specs.append(whole(out_shape[1].shape))
     return call(
-        functools.partial(band_kernel, with_ones), 1, [ANY, whole(counts.shape)] + [ANY] * 5, out_specs,
+        functools.partial(band_kernel, with_ones), 2, [ANY, whole(counts.shape)] + [ANY] * 5, out_specs,
         out_shape, scratch, "band", cost(BAND_COST, 20 * 10**6), VMEM_BAND,
-    )(offsets, ts, counts, below, low, high, above, band_weights)
+    )(odd, offsets, ts, counts, inner, outer, from_inner, from_outer, band_weights)
 
 
 def round_scratch(incoming, remote_weights, mixed):
@@ -511,7 +530,7 @@
     ]
 
 
-def first_round(send, landing, incoming, remote_weights, mixed, columns):
+def first_round(odd, send, landing, incoming, remote_weights, mixed, columns):
     shards, rows, width = incoming.shape
     count_tiles = mixed.shape[0]
     tile, _ = shapes(count_tiles, rows, shards)
@@ -527,9 +546,9 @@
         sems(3 + PARTS),
     ]
     return call(
-        first_kernel, 2, [ANY] * 4, [ANY] * 5, [tile, tile, first, recip, first], scratch, "first",
+        first_kernel, 3, [ANY] * 4, [ANY] * 5, [tile, tile, first, recip, first], scratch, "first",
         cost(2 * 128 * 72 * 128 * 128, 20 * 10**6), VMEM_ROUND,
-    )(send, landing, incoming, remote_weights, mixed, columns)
+    )(odd, send, landing, incoming, remote_weights, mixed, columns)
 
 
 def last_round(landing, incoming, remote_weights, mixed, recip, first):
@@ -554,25 +573,36 @@
     reach = count_tiles // 2
     counts = counts.reshape(count_tiles, width)
     send, landing, offsets = send_tiles.reshape(-1), landing_tiles.reshape(-1), band_offsets.reshape(-1)
-    up = [(i, i + 1) for i in range(shards - 1)]
-    down = [(i + 1, i) for i in range(shards - 1)]
-
-    def exchange(low, high, block, *weights):
-        below = lax.ppermute(high, "item", up)
-        above = lax.ppermute(low, "item", down)
-        outgoing = fill_messages(send, low, high, block, *weights)
+    parity = lax.axis_index("item") % 2
+    odd = parity.reshape(1)
+    inner_pairs = [(i, i ^ 1) for i in range(shards)]
+    outer_pairs = [(i, i + 1 if i % 2 else i - 1) for i in range(1, shards - 1)]
+
+    def swap(inner, outer):
+        return lax.ppermute(inner, "item", inner_pairs), lax.ppermute(outer, "item", outer_pairs)
+
+    def exchange(inner, outer, block, *weights):
+        halo = swap(inner, outer)
+        outgoing = fill_messages(odd, send, inner, outer, block, *weights)
         incoming = lax.all_to_all(outgoing, "item", split_axis=0, concat_axis=0, tiled=True)
-        return below, above, incoming
-
-    low, high, block = prep(target_sums, counts, shards)
-    below, above, incoming = exchange(low, high, block, remote_weights)
-    mixed, sums = band_product(True, offsets, target_sums, counts, below, low, high, above, band_weights)
-    from_below = lax.ppermute(sums[reach + count_tiles :], "item", up)
-    from_above = lax.ppermute(sums[:reach], "item", down)
-    columns = sums[reach : reach + count_tiles] + jnp.concatenate([from_below, from_above], axis=0)
-    low, high, block, recip, first = first_round(send, landing, incoming, remote_weights, mixed, columns)
-    below, above, incoming = exchange(low, high, block)
-    (mixed,) = band_product(False, offsets, target_sums, counts, below, low, high, above, band_weights)
+        return halo, incoming
+
+    inner, outer, block = prep(odd, target_sums, counts, shards)
+    halo, incoming = exchange(inner, outer, block, remote_weights)
+    mixed, sums = band_product(True, odd, offsets, target_sums, counts, inner, outer, *halo, band_weights)
+    below, above = sums[:reach], sums[reach + count_tiles :]
+    from_inner, from_outer = swap(
+        jnp.where(parity == 1, below, above), jnp.where(parity == 1, above, below)
+    )
+    lower, upper = (
+        jnp.where(parity == 1, from_inner, from_outer), jnp.where(parity == 1, from_outer, from_inner)
+    )
+    columns = sums[reach : reach + count_tiles] + jnp.concatenate([lower, upper], axis=0)
+    inner, outer, block, recip, first = first_round(
+        odd, send, landing, incoming, remote_weights, mixed, columns
+    )
+    halo, incoming = exchange(inner, outer, block)
+    (mixed,) = band_product(False, odd, offsets, target_sums, counts, inner, outer, *halo, band_weights)
     return last_round(landing, incoming, remote_weights, mixed, recip, first)
 
 

time: 129 us -> 121 us (0.938)
  starting transfers between devices: 40.2 us -> 30.3 us
  waiting for transfers between devices: 34.3 us -> 37 us
    ppermute x6, starting transfers between devices: 18 us -> 12.4 us  [the longest x3 8.08 us: swap(): lax.ppermute(outer, 'item', outer_pairs)]
    all_to_all x2, starting transfers between devices: 22.2 us -> 17.9 us  [exchange(): lax.all_to_all(outgoing, 'item', split_axis=0, concat_axis=0, tiled=True)]
    all_to_all x2, waiting for transfers between devices: 29.9 us -> 31.8 us  [exchange(): lax.all_to_all(outgoing, 'item', split_axis=0, concat_axis=0, tiled=True)]
  transfers between devices with their start and end apart: 8 -> 8, of which waited for: 3 -> 4; matrix products, arithmetic and copies ran while one was open for 1% -> 1% of each run, Pallas kernels for 24% -> 26%
where the time goes in v5:
time: 121 us; the launch traced here: 120 us
  Pallas kernels  50.8 us (42%)
  waiting for transfers between devices  37 us (31%)
  starting transfers between devices  30.3 us (25%)
    all_to_all x2, waiting for transfers between devices, exchange(): lax.all_to_all(outgoing, 'item', split_axis=0, concat_axis=0, tiled=True)  31.8 us
    pallas_call x2, Pallas kernels, band_product(): call(functools.partial(band_kernel, with_ones), 2, [ANY, whole(counts.sha...  22.7 us
    all_to_all x2, starting transfers between devices, exchange(): lax.all_to_all(outgoing, 'item', split_axis=0, concat_axis=0, tiled=True)  17.9 us
    pallas_call x2, Pallas kernels, fill_messages(): call(functools.partial(message_kernel, remote_weights is not None), 2, [A...  8.42 us
    ppermute x3, starting transfers between devices, swap(): lax.ppermute(outer, 'item', outer_pairs)  8.08 us
    pallas_call x1, Pallas kernels, first_round(): call(first_kernel, 3, [ANY] * 4, [ANY] * 5, [tile, tile, first, recip, fi...  8.06 us
    pallas_call x1, Pallas kernels, last_round(): call(last_kernel, 1, [ANY] * 5, ANY, jax.ShapeDtypeStruct(shape, F32), sc...  7.07 us
    ppermute x3, waiting for transfers between devices, swap(): lax.ppermute(outer, 'item', outer_pairs)  5.2 us
  transfers between devices with their start and end apart: 8, of which 4 were waited for; matrix products, arithmetic and copies ran while one was open for 1% of the time, Pallas kernels for 26%

profile of v5, /device:TPU:1, one launch (start us, length us, event | category | flops | bytes accessed | tf_op | source)
XLA Modules:
  0.0 120.3 jit_solution(10770041116591375638)
XLA Ops:
  0.0 4.6 %prep.1 = (bf16[48,72,128]{2,1,0:T(8,128)(2,1)}, bf16[48,72,128]{2,1,0:T(8,128)(2,1)}, f32[8,128]{1,0:T(8,128)}) custom-call(s32[1]{0:T(128)} %bitcast.1.odd_ref, f32[64,12288]{1,0:T(8,128)} %ts_ref.5, s32[96,128]{1,0:T(8,128)} %bitcast.4), custom_call_target="tpu_custom_call" | custom-call | flops 1000000 | bytes 5000000 | tf_op jit(solution)/shard_map/prep/pallas_call | solution.py:475
  4.6 1.5 %collective-permute-start = (bf16[48,72,128]{2,1,0:T(8,128)(2,1)}, bf16[48,72,128]{2,1,0:T(8,128)(2,1)S(1)}, u32[]{:S(2)}, u32[]{:S(2)}) collective-permute-start(bf16[48,72,128]{2,1,0:T(8,128)(2,1)} %get-tuple-element.15.inner_ref), channel_id=1, source_target_pairs={{0,1},{1,0},{2,3},{3,2},{4,5},{5,4},{6,7},{7,6},{8,9},{9,8},{10,11... | collective-permute-start | bytes 2654216 | tf_op jit(solution)/shard_map/ppermute | solution.py:582
  6.1 3.5 %collective-permute-start.1 = (bf16[48,72,128]{2,1,0:T(8,128)(2,1)}, bf16[48,72,128]{2,1,0:T(8,128)(2,1)}, u32[]{:S(2)}, u32[]{:S(2)}) collective-permute-start(bf16[48,72,128]{2,1,0:T(8,128)(2,1)} %get-tuple-element.16.outer_ref), channel_id=1, source_target_pairs={{1,2},{2,1},{3,4},{4,3},{5,6},{6,5},{7,8},{8,7},{9,10},{10,9},{11,... | collective-permute-start | bytes 2654216 | tf_op jit(solution)/shard_map/ppermute | solution.py:582
  9.7 4.7 %messages.2 = bf16[128,72,128]{2,1,0:T(8,128)(2,1)} custom-call(s32[1]{0:T(128)} %bitcast.1.odd_ref, s32[128]{0:T(128)} %bitcast.7, bf16[48,72,128]{2,1,0:T(8,128)(2,1)} %get-tuple-element.15.inner_ref, bf16[48,72,128]{2,1,0:T(8,128)(2,1)} %get-tuple-element.16.outer_ref, f32[8,128]{1,0:T(8,128)} %get-tuple-element.17.block_ref, ...), custom_call_target="tpu_custom_call" | custom-call | flops 1000000 | bytes 5000000 | tf_op jit(solution)/shard_map/messages/pallas_call | solution.py:496
  14.4 0.0 copy-start.5
  14.4 10.1 %all-to-all-start = ((bf16[128,72,128]{2,1,0:T(8,128)(2,1)}), bf16[128,72,128]{2,1,0:T(8,128)(2,1)}, u32[]{:S(2)}, u32[]{:S(2)}) async-start(bf16[128,72,128]{2,1,0:T(8,128)(2,1)} %messages.2), calls=%async_computation | async-start | bytes 4718592 | tf_op jit(solution)/shard_map/all_to_all | solution.py:587
  24.5 0.1 copy.8
  24.6 0.1 reshape.19.offsets_ref
  24.8 0.9 copy-done.6
  25.7 11.4 %band.2 = (f32[96,72,128]{2,1,0:T(8,128)}, f32[192,128]{1,0:T(8,128)S(1)}) custom-call(s32[1]{0:T(128)} %bitcast.1.odd_ref, s32[384]{0:T(512)S(1)} %reshape.19.offsets_ref, f32[64,12288]{1,0:T(8,128)} %ts_ref.5, s32[96,128]{1,0:T(8,128)S(1)} %bitcast.5, bf16[48,72,128]{2,1,0:T(8,128)(2,1)S(1)} %copy-done, bf16[48,72,128]{2,1,0:T(8,128)(2,1)S(1)} %copy-done.1, ...), custom_call_target="tpu_custom_call" | custom-call | flops 99999997952 | bytes 20000000 | tf_op jit(solution)/shard_map/band/pallas_call | solution.py:518
  37.1 1.2 %collective-permute-start.2 = (f32[48,128]{1,0:T(8,128)S(1)}, f32[48,128]{1,0:T(8,128)S(1)}, u32[]{:S(2)}, u32[]{:S(2)}) collective-permute-start(f32[48,128]{1,0:T(8,128)S(1)} %get-tuple-element.25), channel_id=1, source_target_pairs={{0,1},{1,0},{2,3},{3,2},{4,5},{5,4},{6,7},{7,6},{8,9},{9,8},{10,11... | collective-permute-start | bytes 73736 | tf_op jit(solution)/shard_map/ppermute | solution.py:582
  38.4 2.6 %collective-permute-start.3 = (f32[48,128]{1,0:T(8,128)S(1)}, f32[48,128]{1,0:T(8,128)S(1)}, u32[]{:S(2)}, u32[]{:S(2)}) collective-permute-start(f32[48,128]{1,0:T(8,128)S(1)} %get-tuple-element.26), channel_id=1, source_target_pairs={{1,2},{2,1},{3,4},{4,3},{5,6},{6,5},{7,8},{8,7},{9,10},{10,9},{11,... | collective-permute-start | bytes 73736 | tf_op jit(solution)/shard_map/ppermute | solution.py:582
  41.0 4.0 %collective-permute-done.3 = f32[48,128]{1,0:T(8,128)S(1)} collective-permute-done((f32[48,128]{1,0:T(8,128)S(1)}, f32[48,128]{1,0:T(8,128)S(1)}, u32[]{:S(2)}, u32[]{:S(2)}) %collective-permute-start.3) | collective-permute-done | bytes 24608 | tf_op jit(solution)/shard_map/ppermute | solution.py:582
  45.0 0.6 maximum_add_fusion.columns_ref
  45.6 11.6 %all-to-all-done.in_ref = bf16[128,72,128]{2,1,0:T(8,128)(2,1)} async-done(((bf16[128,72,128]{2,1,0:T(8,128)(2,1)}), bf16[128,72,128]{2,1,0:T(8,128)(2,1)}, u32[]{:S(2)}, u32[]{:S(2)}) %all-to-all-start) | async-done | bytes 2359328 | tf_op jit(solution)/shard_map/all_to_all | solution.py:587
  57.2 8.1 %first.1 = (bf16[48,72,128]{2,1,0:T(8,128)(2,1)}, bf16[48,72,128]{2,1,0:T(8,128)(2,1)}, f32[8,128]{1,0:T(8,128)}, f32[96,128]{1,0:T(8,128)}, f32[8,128]{1,0:T(8,128)}) custom-call(s32[1]{0:T(128)} %bitcast.1.odd_ref, s32[128]{0:T(128)} %bitcast.8, s32[128]{0:T(128)} %bitcast.10, bf16[128,72,128]{2,1,0:T(8,128)(2,1)} %all-to-all-done.in_ref, ...), custom_call_target="tpu_custom_call" | custom-call | flops 301989888 | bytes 20000000 | tf_op jit(solution)/shard_map/first/pallas_call | solution.py:548
  65.3 1.6 %collective-permute-start.4 = (bf16[48,72,128]{2,1,0:T(8,128)(2,1)}, bf16[48,72,128]{2,1,0:T(8,128)(2,1)S(1)}, u32[]{:S(2)}, u32[]{:S(2)}) collective-permute-start(bf16[48,72,128]{2,1,0:T(8,128)(2,1)} %get-tuple-element.20.inner_ref), channel_id=1, source_target_pairs={{0,1},{1,0},{2,3},{3,2},{4,5},{5,4},{6,7},{7,6},{8,9},{9,8},{10,11... | collective-permute-start | bytes 2654216 | tf_op jit(solution)/shard_map/ppermute | solution.py:582
  66.9 1.9 %collective-permute-start.5 = (bf16[48,72,128]{2,1,0:T(8,128)(2,1)}, bf16[48,72,128]{2,1,0:T(8,128)(2,1)}, u32[]{:S(2)}, u32[]{:S(2)}) collective-permute-start(bf16[48,72,128]{2,1,0:T(8,128)(2,1)} %get-tuple-element.21.outer_ref), channel_id=1, source_target_pairs={{1,2},{2,1},{3,4},{4,3},{5,6},{6,5},{7,8},{8,7},{9,10},{10,9},{11,... | collective-permute-start | bytes 2654216 | tf_op jit(solution)/shard_map/ppermute | solution.py:582
  68.9 3.7 %messages.3 = bf16[128,72,128]{2,1,0:T(8,128)(2,1)} custom-call(s32[1]{0:T(128)} %bitcast.1.odd_ref, s32[128]{0:T(128)} %bitcast.9, bf16[48,72,128]{2,1,0:T(8,128)(2,1)} %get-tuple-element.20.inner_ref, bf16[48,72,128]{2,1,0:T(8,128)(2,1)} %get-tuple-element.21.outer_ref, f32[8,128]{1,0:T(8,128)} %get-tuple-element.22.block_ref), custom_call_target="tpu_custom_call" | custom-call | flops 1000000 | bytes 5000000 | tf_op jit(solution)/shard_map/messages/pallas_call | solution.py:496
  72.6 7.8 %all-to-all-start.1 = ((bf16[128,72,128]{2,1,0:T(8,128)(2,1)}), bf16[128,72,128]{2,1,0:T(8,128)(2,1)}, u32[]{:S(2)}, u32[]{:S(2)}) async-start(bf16[128,72,128]{2,1,0:T(8,128)(2,1)} %messages.3), calls=%async_computation.1 | async-start | bytes 4718592 | tf_op jit(solution)/shard_map/all_to_all | solution.py:587
  80.4 1.2 collective-permute-done.5.from_outer_ref
  81.6 11.2 %band.3.band_ref = f32[96,72,128]{2,1,0:T(8,128)} custom-call(s32[1]{0:T(128)} %bitcast.1.odd_ref, s32[384]{0:T(512)S(1)} %reshape.19.offsets_ref, f32[64,12288]{1,0:T(8,128)} %ts_ref.5, s32[96,128]{1,0:T(8,128)S(1)} %bitcast.6, bf16[48,72,128]{2,1,0:T(8,128)(2,1)S(1)} %copy-done.2, bf16[48,72,128]{2,1,0:T(8,128)(2,1)S(1)} %copy-done.3, ...), custom_call_target="tpu_custom_call" | custom-call | flops 99999997952 | bytes 20000000 | tf_op jit(solution)/shard_map/band/pallas_call | solution.py:518
  92.8 20.2 %all-to-all-done.1.in_ref = bf16[128,72,128]{2,1,0:T(8,128)(2,1)} async-done(((bf16[128,72,128]{2,1,0:T(8,128)(2,1)}), bf16[128,72,128]{2,1,0:T(8,128)(2,1)}, u32[]{:S(2)}, u32[]{:S(2)}) %all-to-all-start.1) | async-done | bytes 2359328 | tf_op jit(solution)/shard_map/all_to_all | solution.py:587
  113.1 7.1 %last.1 = f32[64,12288]{1,0:T(8,128)} custom-call(s32[128]{0:T(128)} %bitcast.11, bf16[128,72,128]{2,1,0:T(8,128)(2,1)} %all-to-all-done.1.in_ref, bf16[128,128,128]{2,1,0:T(8,128)(2,1)} %weights_ref.7, f32[96,72,128]{2,1,0:T(8,128)} %band.3.band_ref, f32[96,128]{1,0:T(8,128)} %get-tuple-element.23.recip_ref, f32[8,128]{1,0:T(8,128)} %get-tuple-element.24.first_ref), custom_call_target="tpu_custom_call" | custom-call | flops 301989888 | bytes 20000000 | tf_op jit(solution)/shard_map/last/pallas_call | solution.py:564
  (20 shorter events, 0.1 us)
Async XLA Ops:
  4.6 20.1 %collective-permute-start = (bf16[48,72,128]{2,1,0:T(8,128)(2,1)}, bf16[48,72,128]{2,1,0:T(8,128)(2,1)S(1)}, u32[]{:S(2)}, u32[]{:S(2)}) collective-permute-start(bf16[48,72,128]{2,1,0:T(8,128)(2,1)} %get-tuple-element.15.inner_ref), channel_id=1, source_target_pairs={{0,1},{1,0},{2,3},{3,2},{4,5},{5,4},{6,7},{7,6},{8,9},{9,8},{10,11... | collective-permute-start | bytes 2654216 | tf_op jit(solution)/shard_map/ppermute | solution.py:582
  6.1 18.6 %collective-permute-start.1 = (bf16[48,72,128]{2,1,0:T(8,128)(2,1)}, bf16[48,72,128]{2,1,0:T(8,128)(2,1)}, u32[]{:S(2)}, u32[]{:S(2)}) collective-permute-start(bf16[48,72,128]{2,1,0:T(8,128)(2,1)} %get-tuple-element.16.outer_ref), channel_id=1, source_target_pairs={{1,2},{2,1},{3,4},{4,3},{5,6},{6,5},{7,8},{8,7},{9,10},{10,9},{11,... | collective-permute-start | bytes 2654216 | tf_op jit(solution)/shard_map/ppermute | solution.py:582
  14.4 10.1 %copy-start.5 = (s32[96,4]{0,1:T(4,128)S(1)}, s32[96,4]{0,1:T(4,128)}, u32[]{:S(2)}) copy-start(s32[96,4]{0,1:T(4,128)} %param.9) | copy-start | bytes 4612
  14.4 11.3 %copy-start = (bf16[48,72,128]{2,1,0:T(8,128)(2,1)S(1)}, bf16[48,72,128]{2,1,0:T(8,128)(2,1)}, u32[]{:S(2)}) copy-start(bf16[48,72,128]{2,1,0:T(8,128)(2,1)} %get-tuple-element.15.inner_ref) | copy-start | bytes 2654212
  14.4 11.3 %copy-start.1 = (bf16[48,72,128]{2,1,0:T(8,128)(2,1)S(1)}, bf16[48,72,128]{2,1,0:T(8,128)(2,1)}, u32[]{:S(2)}) copy-start(bf16[48,72,128]{2,1,0:T(8,128)(2,1)} %get-tuple-element.16.outer_ref) | copy-start | bytes 2654212
  14.4 11.3 %copy-start.4 = (s32[12288]{0:T(1024)S(1)}, s32[12288]{0:T(1024)}, u32[]{:S(2)}) copy-start(s32[12288]{0:T(1024)} %param.8) | copy-start | bytes 147460
  14.4 42.8 %all-to-all-start = ((bf16[128,72,128]{2,1,0:T(8,128)(2,1)}), bf16[128,72,128]{2,1,0:T(8,128)(2,1)}, u32[]{:S(2)}, u32[]{:S(2)}) async-start(bf16[128,72,128]{2,1,0:T(8,128)(2,1)} %messages.2), calls=%async_computation | async-start | bytes 4718592 | tf_op jit(solution)/shard_map/all_to_all | solution.py:587
  24.7 0.9 copy-start.6
  37.1 3.9 %collective-permute-start.2 = (f32[48,128]{1,0:T(8,128)S(1)}, f32[48,128]{1,0:T(8,128)S(1)}, u32[]{:S(2)}, u32[]{:S(2)}) collective-permute-start(f32[48,128]{1,0:T(8,128)S(1)} %get-tuple-element.25), channel_id=1, source_target_pairs={{0,1},{1,0},{2,3},{3,2},{4,5},{5,4},{6,7},{7,6},{8,9},{9,8},{10,11... | collective-permute-start | bytes 73736 | tf_op jit(solution)/shard_map/ppermute | solution.py:582
  38.4 6.7 %collective-permute-start.3 = (f32[48,128]{1,0:T(8,128)S(1)}, f32[48,128]{1,0:T(8,128)S(1)}, u32[]{:S(2)}, u32[]{:S(2)}) collective-permute-start(f32[48,128]{1,0:T(8,128)S(1)} %get-tuple-element.26), channel_id=1, source_target_pairs={{1,2},{2,1},{3,4},{4,3},{5,6},{6,5},{7,8},{8,7},{9,10},{10,9},{11,... | collective-permute-start | bytes 73736 | tf_op jit(solution)/shard_map/ppermute | solution.py:582
  65.3 15.1 %collective-permute-start.4 = (bf16[48,72,128]{2,1,0:T(8,128)(2,1)}, bf16[48,72,128]{2,1,0:T(8,128)(2,1)S(1)}, u32[]{:S(2)}, u32[]{:S(2)}) collective-permute-start(bf16[48,72,128]{2,1,0:T(8,128)(2,1)} %get-tuple-element.20.inner_ref), channel_id=1, source_target_pairs={{0,1},{1,0},{2,3},{3,2},{4,5},{5,4},{6,7},{7,6},{8,9},{9,8},{10,11... | collective-permute-start | bytes 2654216 | tf_op jit(solution)/shard_map/ppermute | solution.py:582
  66.9 14.7 %collective-permute-start.5 = (bf16[48,72,128]{2,1,0:T(8,128)(2,1)}, bf16[48,72,128]{2,1,0:T(8,128)(2,1)}, u32[]{:S(2)}, u32[]{:S(2)}) collective-permute-start(bf16[48,72,128]{2,1,0:T(8,128)(2,1)} %get-tuple-element.21.outer_ref), channel_id=1, source_target_pairs={{1,2},{2,1},{3,4},{4,3},{5,6},{6,5},{7,8},{8,7},{9,10},{10,9},{11,... | collective-permute-start | bytes 2654216 | tf_op jit(solution)/shard_map/ppermute | solution.py:582
  72.6 9.1 %copy-start.2 = (bf16[48,72,128]{2,1,0:T(8,128)(2,1)S(1)}, bf16[48,72,128]{2,1,0:T(8,128)(2,1)}, u32[]{:S(2)}) copy-start(bf16[48,72,128]{2,1,0:T(8,128)(2,1)} %get-tuple-element.20.inner_ref) | copy-start | bytes 2654212
  72.6 9.0 %copy-start.3 = (bf16[48,72,128]{2,1,0:T(8,128)(2,1)S(1)}, bf16[48,72,128]{2,1,0:T(8,128)(2,1)}, u32[]{:S(2)}) copy-start(bf16[48,72,128]{2,1,0:T(8,128)(2,1)} %get-tuple-element.21.outer_ref) | copy-start | bytes 2654212
  72.6 40.5 %all-to-all-start.1 = ((bf16[128,72,128]{2,1,0:T(8,128)(2,1)}), bf16[128,72,128]{2,1,0:T(8,128)(2,1)}, u32[]{:S(2)}, u32[]{:S(2)}) async-start(bf16[128,72,128]{2,1,0:T(8,128)(2,1)} %messages.3), calls=%async_computation.1 | async-start | bytes 4718592 | tf_op jit(solution)/shard_map/all_to_all | solution.py:587
  80.4 1.2 %copy-start.7 = (bf16[48,72,128]{2,1,0:T(8,128)(2,1)}, bf16[48,72,128]{2,1,0:T(8,128)(2,1)S(1)}, u32[]{:S(2)}) copy-start(bf16[48,72,128]{2,1,0:T(8,128)(2,1)S(1)} %collective-permute-done.4.from_inner_ref) | copy-start | bytes 2654212

commit v6 on v5

--- a/solution.py
+++ b/solution.py
@@ -14,6 +14,7 @@
 LOADS = 8
 BAND_LOADS = 12
 PARTS = 4
+MESSAGE_PARTS = 8
 BAND_COST = 10**11
 MESSAGE_COST = 10**6
 VMEM = 60
@@ -138,16 +139,16 @@
     for load in loads:
         load.start()
     top = jnp.zeros((rows - EXTRA, width), F32)
-    part = count // PARTS
+    part = count // MESSAGE_PARTS
     if with_columns:
-        remote_loads = Loads([(remote_ref, remote, 0)], PARTS, sems, 3)
-        for i in range(PARTS):
+        remote_loads = Loads([(remote_ref, remote, 0)], MESSAGE_PARTS, sems, 3)
+        for i in range(MESSAGE_PARTS):
             remote_loads.start(i)
     for load in loads:
         load.wait()
     shared = block[...]
-    stores = Loads([(messages, out_ref, 0)], PARTS, out_sems, 0)
-    for number in range(PARTS):
+    stores = Loads([(messages, out_ref, 0)], MESSAGE_PARTS, out_sems, 0)
+    for number in range(MESSAGE_PARTS):
         if with_columns:
             remote_loads.wait(number)
 
@@ -169,40 +170,47 @@
 
         lax.fori_loop(0, part, step, 0, unroll=8)
         stores.start(number)
-    for number in range(PARTS):
+    for number in range(MESSAGE_PARTS):
         stores.wait(number)
 
 
-def prep_kernel(odd_ref, ts_ref, counts_ref, inner_ref, outer_ref, block_ref, ts, tiles, sems, out_sems):
-    channels, width = ts.shape[0], counts_ref.shape[1]
+def prep_kernel(
+    odd_ref, ts_ref, counts_ref, inner_ref, outer_ref, block_ref, ts, counts, tiles, block, sems, out_sems
+):
+    channels, width = ts.shape[0], counts.shape[1]
     count_tiles = tiles.shape[0]
     half = count_tiles // 2
     here = count_tiles // LOADS
     loads = Loads([(ts_ref, ts, 1)], LOADS, sems, 0)
-    for load in range(2 * AHEAD):
+    count_load = pltpu.make_async_copy(counts_ref, counts, sems.at[LOADS])
+    count_load.start()
+    for load in range(LOADS):
         loads.start(load)
     stores = Halves(odd_ref[0], tiles, half, inner_ref, outer_ref, out_sems, 0, PARTS)
+    count_load.wait()
     part = jnp.zeros((channels, width), F32)
     for load in range(LOADS):
         loads.wait(load)
-        loads.start(load + 2 * AHEAD)
 
         def tile(k, part, load=load):
             t = load * here + k
-            block = ts[:, pl.ds(pl.multiple_of(t * width, width), width)]
-            count = counts_ref[pl.ds(t, 1), :].astype(F32)
+            values = ts[:, pl.ds(pl.multiple_of(t * width, width), width)]
+            count = counts[pl.ds(t, 1), :].astype(F32)
             recip = 1.0 / (count + PRIOR)
             high, low = pieces(recip, 2)
-            tiles[t] = stacked(block * recip, rows8({0: high, 1: low, 2: jnp.ones_like(recip)}))
-            return part + block
+            tiles[t] = stacked(values * recip, rows8({0: high, 1: low, 2: jnp.ones_like(recip)}))
+            return part + values
 
         part = lax.fori_loop(0, here, tile, part, unroll=4)
         if (load + 1) % (LOADS // PARTS) == 0:
             stores.start(load // (LOADS // PARTS))
     row = to_row(jnp.sum(part, axis=1, keepdims=True))
-    row = row + at_lane(total(counts_ref[...].astype(F32)), channels)
+    row = row + at_lane(total(counts[...].astype(F32)), channels)
     one, two, three = pieces(row, 3)
-    block_ref[...] = rows8({3: one, 4: two, 5: three})
+    block[...] = rows8({3: one, 4: two, 5: three})
+    block_store = pltpu.make_async_copy(block, block_ref, sems.at[LOADS])
+    block_store.start()
+    block_store.wait()
     for i in range(PARTS):
         stores.wait(i)
 
@@ -269,19 +277,23 @@
         stores.wait(load)
 
 
-def add_remote(landing_ref, in_ref, weights_ref, band_ref, incoming, weights, band, acc, sems, each=None):
+def add_remote(landing_ref, in_ref, weights_ref, band_ref, incoming, weights, band, acc, sems, each=None, small=()):
     shards, rows, width = incoming.shape
     group = shards // LOADS
     loads = Loads([(in_ref, incoming, 0), (weights_ref, weights, 0)], LOADS, sems, 0)
     band_loads = Loads([(band_ref, band, 0)], PARTS, sems, 2 * LOADS)
     for load in range(AHEAD):
         loads.start(load)
+    for load in small:
+        load.start()
 
     def clear(t, carry):
         acc[t] = jnp.zeros((rows, width), F32)
         return carry
 
     lax.fori_loop(0, acc.shape[0], clear, 0, unroll=8)
+    for load in small:
+        load.wait()
     seen = jnp.zeros((EXTRA, width), F32)
     for load in range(LOADS):
         loads.start(load + AHEAD)
@@ -316,14 +328,12 @@
     count_tiles = acc.shape[0]
     half = count_tiles // 2
     column_load = pltpu.make_async_copy(columns_ref, columns, out_sems.at[0])
-    column_load.start()
-    column_load.wait()
 
     def each(p, tail):
         columns[pl.ds(send_ref[p], 1), :] += tail[6:7] + tail[7:8]
 
     seen, band_loads = add_remote(
-        landing_ref, in_ref, weights_ref, band_ref, incoming, weights, band, acc, sems, each
+        landing_ref, in_ref, weights_ref, band_ref, incoming, weights, band, acc, sems, each, [column_load]
     )
     known = seen[3:4, :] + seen[4:5, :] + seen[5:6, :]
     count_total = pick_lane(known, channels)
@@ -387,13 +397,9 @@
         pltpu.make_async_copy(recip_ref, recips, out_sems.at[0]),
         pltpu.make_async_copy(first_ref, firsts, out_sems.at[1]),
     ]
-    for load in small:
-        load.start()
     seen, band_loads = add_remote(
-        landing_ref, in_ref, weights_ref, band_ref, incoming, weights, band, acc, sems
+        landing_ref, in_ref, weights_ref, band_ref, incoming, weights, band, acc, sems, None, small
     )
-    for load in small:
-        load.wait()
     known = seen[3:4, :] + seen[4:5, :] + seen[5:6, :]
     scalars = seen[2:3, :] + seen[6:7, :] + seen[7:8, :]
     weight_total, spread_total = pick_lane(scalars, 0), pick_lane(scalars, 1)
@@ -470,10 +476,17 @@
     count_tiles, width = counts.shape
     rows = channels + EXTRA
     tile, _ = shapes(count_tiles, rows, shards)
-    scratch = [pltpu.VMEM(ts.shape, F32), pltpu.VMEM((count_tiles, rows, width), BF16), sems(LOADS), sems(PARTS)]
     block = jax.ShapeDtypeStruct((EXTRA, width), F32)
+    scratch = [
+        pltpu.VMEM(ts.shape, F32),
+        pltpu.VMEM(counts.shape, jnp.int32),
+        pltpu.VMEM((count_tiles, rows, width), BF16),
+        pltpu.VMEM(block.shape, F32),
+        sems(LOADS + 1),
+        sems(PARTS),
+    ]
     return call(
-        prep_kernel, 1, [ANY, whole(counts.shape)], [ANY, ANY, whole(block.shape)], [tile, tile, block], scratch,
+        prep_kernel, 1, [ANY] * 2, [ANY] * 3, [tile, tile, block], scratch,
         "prep", cost(10**6, 5 * 10**6),
     )(odd, ts, counts)
 
@@ -486,8 +499,8 @@
         pltpu.VMEM((2 * half, rows, width), BF16),
         pltpu.VMEM(message.shape, BF16),
         pltpu.VMEM(block.shape, F32),
-        sems(3 + PARTS),
-        sems(PARTS),
+        sems(3 + MESSAGE_PARTS),
+        sems(MESSAGE_PARTS),
     ]
     operands = [odd, send, inner, outer, block]
     if remote_weights is not None:

time: 121 us -> 119 us (0.983)
  Pallas kernels: 50.8 us -> 49 us
    pallas_call x1, Pallas kernels: 4.61 us -> 2.83 us  [prep(): call(prep_kernel, 1, [ANY] * 2, [ANY] * 3, [tile, tile, block], scratch,...]
where the time goes in v6:
time: 119 us
  Pallas kernels  49 us (41%)
  waiting for transfers between devices  37 us (31%)
  starting transfers between devices  30.4 us (26%)
    all_to_all x2, waiting for transfers between devices, exchange(): lax.all_to_all(outgoing, 'item', split_axis=0, concat_axis=0, tiled=True)  31.8 us
    pallas_call x2, Pallas kernels, band_product(): call(functools.partial(band_kernel, with_ones), 2, [ANY, whole(counts.sha...  22.7 us
    all_to_all x2, starting transfers between devices, exchange(): lax.all_to_all(outgoing, 'item', split_axis=0, concat_axis=0, tiled=True)  17.9 us
    pallas_call x2, Pallas kernels, fill_messages(): call(functools.partial(message_kernel, remote_weights is not None), 2, [A...  8.22 us
    ppermute x3, starting transfers between devices, swap(): lax.ppermute(outer, 'item', outer_pairs)  8.1 us
    pallas_call x1, Pallas kernels, first_round(): call(first_kernel, 3, [ANY] * 4, [ANY] * 5, [tile, tile, first, recip, fi...  7.76 us
    pallas_call x1, Pallas kernels, last_round(): call(last_kernel, 1, [ANY] * 5, ANY, jax.ShapeDtypeStruct(shape, F32), sc...  7.52 us
    ppermute x3, waiting for transfers between devices, swap(): lax.ppermute(outer, 'item', outer_pairs)  5.16 us
  transfers between devices with their start and end apart: 8, of which 4 were waited for; matrix products, arithmetic and copies ran while one was open for 1% of the time, Pallas kernels for 26%

profile of v6, /device:TPU:1, one launch (start us, length us, event | category | flops | bytes accessed | tf_op | source)
XLA Modules:
  0.0 118.5 jit_solution(238140813350189529)
XLA Ops:
  0.0 2.8 %prep.1 = (bf16[48,72,128]{2,1,0:T(8,128)(2,1)}, bf16[48,72,128]{2,1,0:T(8,128)(2,1)}, f32[8,128]{1,0:T(8,128)}) custom-call(s32[1]{0:T(128)} %bitcast.1.odd_ref, f32[64,12288]{1,0:T(8,128)} %ts_ref.5, s32[96,128]{1,0:T(8,128)} %bitcast.4), custom_call_target="tpu_custom_call" | custom-call | flops 1000000 | bytes 5000000 | tf_op jit(solution)/shard_map/prep/pallas_call | solution.py:488
  2.8 1.5 %collective-permute-start = (bf16[48,72,128]{2,1,0:T(8,128)(2,1)}, bf16[48,72,128]{2,1,0:T(8,128)(2,1)S(1)}, u32[]{:S(2)}, u32[]{:S(2)}) collective-permute-start(bf16[48,72,128]{2,1,0:T(8,128)(2,1)} %get-tuple-element.15.inner_ref), channel_id=1, source_target_pairs={{0,1},{1,0},{2,3},{3,2},{4,5},{5,4},{6,7},{7,6},{8,9},{9,8},{10,11... | collective-permute-start | bytes 2654216 | tf_op jit(solution)/shard_map/ppermute | solution.py:595
  4.4 3.5 %collective-permute-start.1 = (bf16[48,72,128]{2,1,0:T(8,128)(2,1)}, bf16[48,72,128]{2,1,0:T(8,128)(2,1)}, u32[]{:S(2)}, u32[]{:S(2)}) collective-permute-start(bf16[48,72,128]{2,1,0:T(8,128)(2,1)} %get-tuple-element.16.outer_ref), channel_id=1, source_target_pairs={{1,2},{2,1},{3,4},{4,3},{5,6},{6,5},{7,8},{8,7},{9,10},{10,9},{11,... | collective-permute-start | bytes 2654216 | tf_op jit(solution)/shard_map/ppermute | solution.py:595
  7.9 4.5 %messages.2 = bf16[128,72,128]{2,1,0:T(8,128)(2,1)} custom-call(s32[1]{0:T(128)} %bitcast.1.odd_ref, s32[128]{0:T(128)} %bitcast.7, bf16[48,72,128]{2,1,0:T(8,128)(2,1)} %get-tuple-element.15.inner_ref, bf16[48,72,128]{2,1,0:T(8,128)(2,1)} %get-tuple-element.16.outer_ref, f32[8,128]{1,0:T(8,128)} %get-tuple-element.17.block_ref, ...), custom_call_target="tpu_custom_call" | custom-call | flops 1000000 | bytes 5000000 | tf_op jit(solution)/shard_map/messages/pallas_call | solution.py:509
  12.5 0.0 copy-start.4
  12.5 10.1 %all-to-all-start = ((bf16[128,72,128]{2,1,0:T(8,128)(2,1)}), bf16[128,72,128]{2,1,0:T(8,128)(2,1)}, u32[]{:S(2)}, u32[]{:S(2)}) async-start(bf16[128,72,128]{2,1,0:T(8,128)(2,1)} %messages.2), calls=%async_computation | async-start | bytes 4718592 | tf_op jit(solution)/shard_map/all_to_all | solution.py:600
  22.6 0.1 copy.8
  22.7 0.1 reshape.19.offsets_ref
  22.8 0.9 copy-done.6
  23.7 11.4 %band.2 = (f32[96,72,128]{2,1,0:T(8,128)}, f32[192,128]{1,0:T(8,128)S(1)}) custom-call(s32[1]{0:T(128)} %bitcast.1.odd_ref, s32[384]{0:T(512)S(1)} %reshape.19.offsets_ref, f32[64,12288]{1,0:T(8,128)} %ts_ref.5, s32[96,128]{1,0:T(8,128)S(1)} %bitcast.5, bf16[48,72,128]{2,1,0:T(8,128)(2,1)S(1)} %copy-done, bf16[48,72,128]{2,1,0:T(8,128)(2,1)S(1)} %copy-done.1, ...), custom_call_target="tpu_custom_call" | custom-call | flops 99999997952 | bytes 20000000 | tf_op jit(solution)/shard_map/band/pallas_call | solution.py:531
  35.2 1.2 %collective-permute-start.2 = (f32[48,128]{1,0:T(8,128)S(1)}, f32[48,128]{1,0:T(8,128)S(1)}, u32[]{:S(2)}, u32[]{:S(2)}) collective-permute-start(f32[48,128]{1,0:T(8,128)S(1)} %get-tuple-element.25), channel_id=1, source_target_pairs={{0,1},{1,0},{2,3},{3,2},{4,5},{5,4},{6,7},{7,6},{8,9},{9,8},{10,11... | collective-permute-start | bytes 73736 | tf_op jit(solution)/shard_map/ppermute | solution.py:595
  36.4 2.7 %collective-permute-start.3 = (f32[48,128]{1,0:T(8,128)S(1)}, f32[48,128]{1,0:T(8,128)S(1)}, u32[]{:S(2)}, u32[]{:S(2)}) collective-permute-start(f32[48,128]{1,0:T(8,128)S(1)} %get-tuple-element.26), channel_id=1, source_target_pairs={{1,2},{2,1},{3,4},{4,3},{5,6},{6,5},{7,8},{8,7},{9,10},{10,9},{11,... | collective-permute-start | bytes 73736 | tf_op jit(solution)/shard_map/ppermute | solution.py:595
  39.1 4.0 %collective-permute-done.3 = f32[48,128]{1,0:T(8,128)S(1)} collective-permute-done((f32[48,128]{1,0:T(8,128)S(1)}, f32[48,128]{1,0:T(8,128)S(1)}, u32[]{:S(2)}, u32[]{:S(2)}) %collective-permute-start.3) | collective-permute-done | bytes 24608 | tf_op jit(solution)/shard_map/ppermute | solution.py:595
  43.1 0.6 maximum_add_fusion.columns_ref
  43.7 11.6 %all-to-all-done.in_ref = bf16[128,72,128]{2,1,0:T(8,128)(2,1)} async-done(((bf16[128,72,128]{2,1,0:T(8,128)(2,1)}), bf16[128,72,128]{2,1,0:T(8,128)(2,1)}, u32[]{:S(2)}, u32[]{:S(2)}) %all-to-all-start) | async-done | bytes 2359328 | tf_op jit(solution)/shard_map/all_to_all | solution.py:600
  55.3 7.8 %first.1 = (bf16[48,72,128]{2,1,0:T(8,128)(2,1)}, bf16[48,72,128]{2,1,0:T(8,128)(2,1)}, f32[8,128]{1,0:T(8,128)}, f32[96,128]{1,0:T(8,128)}, f32[8,128]{1,0:T(8,128)}) custom-call(s32[1]{0:T(128)} %bitcast.1.odd_ref, s32[128]{0:T(128)} %bitcast.8, s32[128]{0:T(128)} %bitcast.10, bf16[128,72,128]{2,1,0:T(8,128)(2,1)} %all-to-all-done.in_ref, ...), custom_call_target="tpu_custom_call" | custom-call | flops 301989888 | bytes 20000000 | tf_op jit(solution)/shard_map/first/pallas_call | solution.py:561
  63.0 1.7 %collective-permute-start.4 = (bf16[48,72,128]{2,1,0:T(8,128)(2,1)}, bf16[48,72,128]{2,1,0:T(8,128)(2,1)S(1)}, u32[]{:S(2)}, u32[]{:S(2)}) collective-permute-start(bf16[48,72,128]{2,1,0:T(8,128)(2,1)} %get-tuple-element.20.inner_ref), channel_id=1, source_target_pairs={{0,1},{1,0},{2,3},{3,2},{4,5},{5,4},{6,7},{7,6},{8,9},{9,8},{10,11... | collective-permute-start | bytes 2654216 | tf_op jit(solution)/shard_map/ppermute | solution.py:595
  64.7 1.9 %collective-permute-start.5 = (bf16[48,72,128]{2,1,0:T(8,128)(2,1)}, bf16[48,72,128]{2,1,0:T(8,128)(2,1)}, u32[]{:S(2)}, u32[]{:S(2)}) collective-permute-start(bf16[48,72,128]{2,1,0:T(8,128)(2,1)} %get-tuple-element.21.outer_ref), channel_id=1, source_target_pairs={{1,2},{2,1},{3,4},{4,3},{5,6},{6,5},{7,8},{8,7},{9,10},{10,9},{11,... | collective-permute-start | bytes 2654216 | tf_op jit(solution)/shard_map/ppermute | solution.py:595
  66.6 3.7 %messages.3 = bf16[128,72,128]{2,1,0:T(8,128)(2,1)} custom-call(s32[1]{0:T(128)} %bitcast.1.odd_ref, s32[128]{0:T(128)} %bitcast.9, bf16[48,72,128]{2,1,0:T(8,128)(2,1)} %get-tuple-element.20.inner_ref, bf16[48,72,128]{2,1,0:T(8,128)(2,1)} %get-tuple-element.21.outer_ref, f32[8,128]{1,0:T(8,128)} %get-tuple-element.22.block_ref), custom_call_target="tpu_custom_call" | custom-call | flops 1000000 | bytes 5000000 | tf_op jit(solution)/shard_map/messages/pallas_call | solution.py:509
  70.3 7.8 %all-to-all-start.1 = ((bf16[128,72,128]{2,1,0:T(8,128)(2,1)}), bf16[128,72,128]{2,1,0:T(8,128)(2,1)}, u32[]{:S(2)}, u32[]{:S(2)}) async-start(bf16[128,72,128]{2,1,0:T(8,128)(2,1)} %messages.3), calls=%async_computation.1 | async-start | bytes 4718592 | tf_op jit(solution)/shard_map/all_to_all | solution.py:600
  78.1 1.2 %collective-permute-done.5.from_outer_ref = bf16[48,72,128]{2,1,0:T(8,128)(2,1)} collective-permute-done((bf16[48,72,128]{2,1,0:T(8,128)(2,1)}, bf16[48,72,128]{2,1,0:T(8,128)(2,1)}, u32[]{:S(2)}, u32[]{:S(2)}) %collective-permute-start.5) | collective-permute-done | bytes 884768 | tf_op jit(solution)/shard_map/ppermute | solution.py:595
  79.4 11.2 %band.3.band_ref = f32[96,72,128]{2,1,0:T(8,128)} custom-call(s32[1]{0:T(128)} %bitcast.1.odd_ref, s32[384]{0:T(512)S(1)} %reshape.19.offsets_ref, f32[64,12288]{1,0:T(8,128)} %ts_ref.5, s32[96,128]{1,0:T(8,128)S(1)} %bitcast.6, bf16[48,72,128]{2,1,0:T(8,128)(2,1)S(1)} %copy-done.2, bf16[48,72,128]{2,1,0:T(8,128)(2,1)S(1)} %copy-done.3, ...), custom_call_target="tpu_custom_call" | custom-call | flops 99999997952 | bytes 20000000 | tf_op jit(solution)/shard_map/band/pallas_call | solution.py:531
  90.6 20.2 %all-to-all-done.1.in_ref = bf16[128,72,128]{2,1,0:T(8,128)(2,1)} async-done(((bf16[128,72,128]{2,1,0:T(8,128)(2,1)}), bf16[128,72,128]{2,1,0:T(8,128)(2,1)}, u32[]{:S(2)}, u32[]{:S(2)}) %all-to-all-start.1) | async-done | bytes 2359328 | tf_op jit(solution)/shard_map/all_to_all | solution.py:600
  110.8 7.5 %last.1 = f32[64,12288]{1,0:T(8,128)} custom-call(s32[128]{0:T(128)} %bitcast.11, bf16[128,72,128]{2,1,0:T(8,128)(2,1)} %all-to-all-done.1.in_ref, bf16[128,128,128]{2,1,0:T(8,128)(2,1)} %weights_ref.7, f32[96,72,128]{2,1,0:T(8,128)} %band.3.band_ref, f32[96,128]{1,0:T(8,128)} %get-tuple-element.23.recip_ref, f32[8,128]{1,0:T(8,128)} %get-tuple-element.24.first_ref), custom_call_target="tpu_custom_call" | custom-call | flops 301989888 | bytes 20000000 | tf_op jit(solution)/shard_map/last/pallas_call | solution.py:577
  (20 shorter events, 0.1 us)
Async XLA Ops:
  2.8 19.9 %collective-permute-start = (bf16[48,72,128]{2,1,0:T(8,128)(2,1)}, bf16[48,72,128]{2,1,0:T(8,128)(2,1)S(1)}, u32[]{:S(2)}, u32[]{:S(2)}) collective-permute-start(bf16[48,72,128]{2,1,0:T(8,128)(2,1)} %get-tuple-element.15.inner_ref), channel_id=1, source_target_pairs={{0,1},{1,0},{2,3},{3,2},{4,5},{5,4},{6,7},{7,6},{8,9},{9,8},{10,11... | collective-permute-start | bytes 2654216 | tf_op jit(solution)/shard_map/ppermute | solution.py:595
  4.4 18.4 %collective-permute-start.1 = (bf16[48,72,128]{2,1,0:T(8,128)(2,1)}, bf16[48,72,128]{2,1,0:T(8,128)(2,1)}, u32[]{:S(2)}, u32[]{:S(2)}) collective-permute-start(bf16[48,72,128]{2,1,0:T(8,128)(2,1)} %get-tuple-element.16.outer_ref), channel_id=1, source_target_pairs={{1,2},{2,1},{3,4},{4,3},{5,6},{6,5},{7,8},{8,7},{9,10},{10,9},{11,... | collective-permute-start | bytes 2654216 | tf_op jit(solution)/shard_map/ppermute | solution.py:595
  12.4 10.1 %copy-start.5 = (s32[96,4]{0,1:T(4,128)S(1)}, s32[96,4]{0,1:T(4,128)}, u32[]{:S(2)}) copy-start(s32[96,4]{0,1:T(4,128)} %param.9) | copy-start | bytes 4612
  12.4 11.3 %copy-start = (bf16[48,72,128]{2,1,0:T(8,128)(2,1)S(1)}, bf16[48,72,128]{2,1,0:T(8,128)(2,1)}, u32[]{:S(2)}) copy-start(bf16[48,72,128]{2,1,0:T(8,128)(2,1)} %get-tuple-element.15.inner_ref) | copy-start | bytes 2654212
  12.5 11.3 %copy-start.1 = (bf16[48,72,128]{2,1,0:T(8,128)(2,1)S(1)}, bf16[48,72,128]{2,1,0:T(8,128)(2,1)}, u32[]{:S(2)}) copy-start(bf16[48,72,128]{2,1,0:T(8,128)(2,1)} %get-tuple-element.16.outer_ref) | copy-start | bytes 2654212
  12.5 11.3 %copy-start.4 = (s32[12288]{0:T(1024)S(1)}, s32[12288]{0:T(1024)}, u32[]{:S(2)}) copy-start(s32[12288]{0:T(1024)} %param.8) | copy-start | bytes 147460
  12.5 42.8 %all-to-all-start = ((bf16[128,72,128]{2,1,0:T(8,128)(2,1)}), bf16[128,72,128]{2,1,0:T(8,128)(2,1)}, u32[]{:S(2)}, u32[]{:S(2)}) async-start(bf16[128,72,128]{2,1,0:T(8,128)(2,1)} %messages.2), calls=%async_computation | async-start | bytes 4718592 | tf_op jit(solution)/shard_map/all_to_all | solution.py:600
  22.8 0.9 copy-start.6
  35.2 3.9 %collective-permute-start.2 = (f32[48,128]{1,0:T(8,128)S(1)}, f32[48,128]{1,0:T(8,128)S(1)}, u32[]{:S(2)}, u32[]{:S(2)}) collective-permute-start(f32[48,128]{1,0:T(8,128)S(1)} %get-tuple-element.25), channel_id=1, source_target_pairs={{0,1},{1,0},{2,3},{3,2},{4,5},{5,4},{6,7},{7,6},{8,9},{9,8},{10,11... | collective-permute-start | bytes 73736 | tf_op jit(solution)/shard_map/ppermute | solution.py:595
  36.4 6.7 %collective-permute-start.3 = (f32[48,128]{1,0:T(8,128)S(1)}, f32[48,128]{1,0:T(8,128)S(1)}, u32[]{:S(2)}, u32[]{:S(2)}) collective-permute-start(f32[48,128]{1,0:T(8,128)S(1)} %get-tuple-element.26), channel_id=1, source_target_pairs={{1,2},{2,1},{3,4},{4,3},{5,6},{6,5},{7,8},{8,7},{9,10},{10,9},{11,... | collective-permute-start | bytes 73736 | tf_op jit(solution)/shard_map/ppermute | solution.py:595
  63.0 15.1 %collective-permute-start.4 = (bf16[48,72,128]{2,1,0:T(8,128)(2,1)}, bf16[48,72,128]{2,1,0:T(8,128)(2,1)S(1)}, u32[]{:S(2)}, u32[]{:S(2)}) collective-permute-start(bf16[48,72,128]{2,1,0:T(8,128)(2,1)} %get-tuple-element.20.inner_ref), channel_id=1, source_target_pairs={{0,1},{1,0},{2,3},{3,2},{4,5},{5,4},{6,7},{7,6},{8,9},{9,8},{10,11... | collective-permute-start | bytes 2654216 | tf_op jit(solution)/shard_map/ppermute | solution.py:595
  64.7 14.7 %collective-permute-start.5 = (bf16[48,72,128]{2,1,0:T(8,128)(2,1)}, bf16[48,72,128]{2,1,0:T(8,128)(2,1)}, u32[]{:S(2)}, u32[]{:S(2)}) collective-permute-start(bf16[48,72,128]{2,1,0:T(8,128)(2,1)} %get-tuple-element.21.outer_ref), channel_id=1, source_target_pairs={{1,2},{2,1},{3,4},{4,3},{5,6},{6,5},{7,8},{8,7},{9,10},{10,9},{11,... | collective-permute-start | bytes 2654216 | tf_op jit(solution)/shard_map/ppermute | solution.py:595
  70.3 9.0 %copy-start.2 = (bf16[48,72,128]{2,1,0:T(8,128)(2,1)S(1)}, bf16[48,72,128]{2,1,0:T(8,128)(2,1)}, u32[]{:S(2)}) copy-start(bf16[48,72,128]{2,1,0:T(8,128)(2,1)} %get-tuple-element.20.inner_ref) | copy-start | bytes 2654212
  70.3 9.0 %copy-start.3 = (bf16[48,72,128]{2,1,0:T(8,128)(2,1)S(1)}, bf16[48,72,128]{2,1,0:T(8,128)(2,1)}, u32[]{:S(2)}) copy-start(bf16[48,72,128]{2,1,0:T(8,128)(2,1)} %get-tuple-element.21.outer_ref) | copy-start | bytes 2654212
  70.3 40.5 %all-to-all-start.1 = ((bf16[128,72,128]{2,1,0:T(8,128)(2,1)}), bf16[128,72,128]{2,1,0:T(8,128)(2,1)}, u32[]{:S(2)}, u32[]{:S(2)}) async-start(bf16[128,72,128]{2,1,0:T(8,128)(2,1)} %messages.3), calls=%async_computation.1 | async-start | bytes 4718592 | tf_op jit(solution)/shard_map/all_to_all | solution.py:600
  78.1 1.2 %copy-start.7 = (bf16[48,72,128]{2,1,0:T(8,128)(2,1)}, bf16[48,72,128]{2,1,0:T(8,128)(2,1)S(1)}, u32[]{:S(2)}) copy-start(bf16[48,72,128]{2,1,0:T(8,128)(2,1)S(1)} %collective-permute-done.4.from_inner_ref) | copy-start | bytes 2654212

commit v7 on v6

--- a/solution.py
+++ b/solution.py
@@ -16,7 +16,6 @@
 PARTS = 4
 MESSAGE_PARTS = 8
 BAND_COST = 10**11
-MESSAGE_COST = 10**6
 VMEM = 60
 VMEM_ROUND = 60
 VMEM_BAND = 52
@@ -123,59 +122,32 @@
         pl.when(self.odd == 0)(self.copies[i][1].wait)
 
 
-def message_kernel(with_columns, odd_ref, send_ref, inner_ref, outer_ref, block_ref, *rest):
-    if with_columns:
-        remote_ref, out_ref, tiles, messages, block, sems, out_sems, remote, columns = rest
-    else:
-        out_ref, tiles, messages, block, sems, out_sems = rest
+def store_messages(send_ref, tiles, messages, out_ref, sems, first, shared, remote=None, remote_loads=None):
     count, rows, width = messages.shape
-    half = inner_ref.shape[0]
-    odd = odd_ref[0]
-    loads = [
-        pltpu.make_async_copy(inner_ref, tiles.at[pl.ds((1 - odd) * half, half)], sems.at[0]),
-        pltpu.make_async_copy(outer_ref, tiles.at[pl.ds(odd * half, half)], sems.at[1]),
-        pltpu.make_async_copy(block_ref, block, sems.at[2]),
-    ]
-    for load in loads:
-        load.start()
     top = jnp.zeros((rows - EXTRA, width), F32)
     part = count // MESSAGE_PARTS
-    if with_columns:
-        remote_loads = Loads([(remote_ref, remote, 0)], MESSAGE_PARTS, sems, 3)
-        for i in range(MESSAGE_PARTS):
-            remote_loads.start(i)
-    for load in loads:
-        load.wait()
-    shared = block[...]
-    stores = Loads([(messages, out_ref, 0)], MESSAGE_PARTS, out_sems, 0)
+    stores = Loads([(messages, out_ref, 0)], MESSAGE_PARTS, sems, first)
     for number in range(MESSAGE_PARTS):
-        if with_columns:
+        if remote is not None:
             remote_loads.wait(number)
-
-            def column(k, carry, number=number):
-                q = number * part + k
-                columns[pl.ds(q, 1), :] = jnp.sum(remote[q].astype(F32), axis=0, keepdims=True)
-                return carry
-
-            lax.fori_loop(0, part, column, 0, unroll=8)
 
         def step(k, carry, number=number):
             q = number * part + k
             extra = shared
-            if with_columns:
-                high, low = pieces(columns[pl.ds(q, 1), :], 2)
+            if remote is not None:
+                high, low = pieces(jnp.sum(remote[q].astype(F32), axis=0, keepdims=True), 2)
                 extra = rows8({6: high, 7: low}, shared)
             messages[q] = tiles[send_ref[q]] + stacked(top, extra)
             return carry
 
         lax.fori_loop(0, part, step, 0, unroll=8)
         stores.start(number)
-    for number in range(MESSAGE_PARTS):
-        stores.wait(number)
+    return stores
 
 
 def prep_kernel(
-    odd_ref, ts_ref, counts_ref, inner_ref, outer_ref, block_ref, ts, counts, tiles, block, sems, out_sems
+    odd_ref, send_ref, ts_ref, counts_ref, remote_ref, inner_ref, outer_ref, out_ref,
+    ts, counts, remote, tiles, messages, sems, out_sems,
 ):
     channels, width = ts.shape[0], counts.shape[1]
     count_tiles = tiles.shape[0]
@@ -184,6 +156,7 @@
     loads = Loads([(ts_ref, ts, 1)], LOADS, sems, 0)
     count_load = pltpu.make_async_copy(counts_ref, counts, sems.at[LOADS])
     count_load.start()
+    remote_loads = Loads([(remote_ref, remote, 0)], MESSAGE_PARTS, sems, LOADS + 1)
     for load in range(LOADS):
         loads.start(load)
     stores = Halves(odd_ref[0], tiles, half, inner_ref, outer_ref, out_sems, 0, PARTS)
@@ -191,6 +164,9 @@
     part = jnp.zeros((channels, width), F32)
     for load in range(LOADS):
         loads.wait(load)
+        if load >= LOADS // 2:
+            for i in range(2):
+                remote_loads.start(2 * (load - LOADS // 2) + i)
 
         def tile(k, part, load=load):
             t = load * here + k
@@ -207,12 +183,14 @@
     row = to_row(jnp.sum(part, axis=1, keepdims=True))
     row = row + at_lane(total(counts[...].astype(F32)), channels)
     one, two, three = pieces(row, 3)
-    block[...] = rows8({3: one, 4: two, 5: three})
-    block_store = pltpu.make_async_copy(block, block_ref, sems.at[LOADS])
-    block_store.start()
-    block_store.wait()
+    block = rows8({3: one, 4: two, 5: three})
+    messages_out = store_messages(
+        send_ref, tiles, messages, out_ref, out_sems, PARTS, block, remote, remote_loads
+    )
     for i in range(PARTS):
         stores.wait(i)
+    for i in range(MESSAGE_PARTS):
+        messages_out.wait(i)
 
 
 def band_kernel(
@@ -320,8 +298,8 @@
 
 def first_kernel(
     odd_ref, send_ref, landing_ref, in_ref, weights_ref, band_ref, columns_ref,
-    inner_ref, outer_ref, block_ref, recip_ref, first_ref,
-    incoming, weights, band, acc, tiles, columns, recips, firsts, block, sems, out_sems,
+    inner_ref, outer_ref, out_ref, recip_ref, first_ref,
+    incoming, weights, band, acc, tiles, columns, recips, firsts, messages, sems, out_sems,
 ):
     shards, rows, width = incoming.shape
     channels = rows - EXTRA
@@ -376,14 +354,17 @@
     scalars = at_lane(total(all_weights), 0) + at_lane(total(all_recips), 1)
     one, two, three = pieces(row, 3)
     uno, due, tre = pieces(scalars, 3)
-    block[...] = rows8({2: uno, 3: one, 4: two, 5: three, 6: due, 7: tre})
-    for source, ref in ((recips, recip_ref), (firsts, first_ref), (block, block_ref)):
+    block = rows8({2: uno, 3: one, 4: two, 5: three, 6: due, 7: tre})
+    for source, ref in ((recips, recip_ref), (firsts, first_ref)):
         stores.append(pltpu.make_async_copy(source, ref, out_sems.at[len(stores)]))
         stores[-1].start()
+    messages_out = store_messages(send_ref, tiles, messages, out_ref, out_sems, 3 + PARTS, block)
     for store in stores:
         store.wait()
     for number in range(PARTS):
         halves.wait(number)
+    for number in range(MESSAGE_PARTS):
+        messages_out.wait(number)
 
 
 def last_kernel(
@@ -471,45 +452,23 @@
     return pltpu.SemaphoreType.DMA((count,))
 
 
-def prep(odd, ts, counts, shards):
+def prep(odd, send, ts, counts, remote_weights):
     channels, columns = ts.shape
     count_tiles, width = counts.shape
     rows = channels + EXTRA
-    tile, _ = shapes(count_tiles, rows, shards)
-    block = jax.ShapeDtypeStruct((EXTRA, width), F32)
+    tile, message = shapes(count_tiles, rows, send.shape[0])
     scratch = [
         pltpu.VMEM(ts.shape, F32),
         pltpu.VMEM(counts.shape, jnp.int32),
+        pltpu.VMEM(remote_weights.shape, BF16),
         pltpu.VMEM((count_tiles, rows, width), BF16),
-        pltpu.VMEM(block.shape, F32),
-        sems(LOADS + 1),
-        sems(PARTS),
+        pltpu.VMEM(message.shape, BF16),
+        sems(LOADS + 1 + MESSAGE_PARTS),
+        sems(PARTS + MESSAGE_PARTS),
     ]
     return call(
-        prep_kernel, 1, [ANY] * 2, [ANY] * 3, [tile, tile, block], scratch,
-        "prep", cost(10**6, 5 * 10**6),
-    )(odd, ts, counts)
-
-
-def fill_messages(odd, send, inner, outer, block, remote_weights=None):
-    half, rows, width = inner.shape
-    shards = send.shape[0]
-    _, message = shapes(2 * half, rows, shards)
-    scratch = [
-        pltpu.VMEM((2 * half, rows, width), BF16),
-        pltpu.VMEM(message.shape, BF16),
-        pltpu.VMEM(block.shape, F32),
-        sems(3 + MESSAGE_PARTS),
-        sems(MESSAGE_PARTS),
-    ]
-    operands = [odd, send, inner, outer, block]
-    if remote_weights is not None:
-        operands.append(remote_weights)
-        scratch += [pltpu.VMEM(remote_weights.shape, BF16), pltpu.VMEM((shards, width), F32)]
-    return call(
-        functools.partial(message_kernel, remote_weights is not None), 2, [ANY] * (len(operands) - 2), ANY,
-        message, scratch, "messages", cost(MESSAGE_COST, 5 * 10**6),
-    )(*operands)
+        prep_kernel, 2, [ANY] * 3, [ANY] * 3, [tile, tile, message], scratch, "prep", cost(10**6, 5 * 10**6)
+    )(odd, send, ts, counts, remote_weights)
 
 
 def band_product(with_ones, odd, offsets, ts, counts, inner, outer, from_inner, from_outer, band_weights):
@@ -546,7 +505,7 @@
 def first_round(odd, send, landing, incoming, remote_weights, mixed, columns):
     shards, rows, width = incoming.shape
     count_tiles = mixed.shape[0]
-    tile, _ = shapes(count_tiles, rows, shards)
+    tile, message = shapes(count_tiles, rows, shards)
     recip = jax.ShapeDtypeStruct((count_tiles, width), F32)
     first = jax.ShapeDtypeStruct((8, width), F32)
     scratch = round_scratch(incoming, remote_weights, mixed) + [
@@ -554,12 +513,12 @@
         pltpu.VMEM(columns.shape, F32),
         pltpu.VMEM(recip.shape, F32),
         pltpu.VMEM(first.shape, F32),
-        pltpu.VMEM((EXTRA, width), F32),
+        pltpu.VMEM(message.shape, BF16),
         sems(PARTS + 2 * LOADS),
-        sems(3 + PARTS),
+        sems(3 + PARTS + MESSAGE_PARTS),
     ]
     return call(
-        first_kernel, 3, [ANY] * 4, [ANY] * 5, [tile, tile, first, recip, first], scratch, "first",
+        first_kernel, 3, [ANY] * 4, [ANY] * 5, [tile, tile, message, recip, first], scratch, "first",
         cost(2 * 128 * 72 * 128 * 128, 20 * 10**6), VMEM_ROUND,
     )(odd, send, landing, incoming, remote_weights, mixed, columns)
 
@@ -594,14 +553,12 @@
     def swap(inner, outer):
         return lax.ppermute(inner, "item", inner_pairs), lax.ppermute(outer, "item", outer_pairs)
 
-    def exchange(inner, outer, block, *weights):
+    def exchange(inner, outer, outgoing):
         halo = swap(inner, outer)
-        outgoing = fill_messages(odd, send, inner, outer, block, *weights)
-        incoming = lax.all_to_all(outgoing, "item", split_axis=0, concat_axis=0, tiled=True)
-        return halo, incoming
-
-    inner, outer, block = prep(odd, target_sums, counts, shards)
-    halo, incoming = exchange(inner, outer, block, remote_weights)
+        return halo, lax.all_to_all(outgoing, "item", split_axis=0, concat_axis=0, tiled=True)
+
+    inner, outer, outgoing = prep(odd, send, target_sums, counts, remote_weights)
+    halo, incoming = exchange(inner, outer, outgoing)
     mixed, sums = band_product(True, odd, offsets, target_sums, counts, inner, outer, *halo, band_weights)
     below, above = sums[:reach], sums[reach + count_tiles :]
     from_inner, from_outer = swap(
@@ -611,10 +568,10 @@
         jnp.where(parity == 1, from_inner, from_outer), jnp.where(parity == 1, from_outer, from_inner)
     )
     columns = sums[reach : reach + count_tiles] + jnp.concatenate([lower, upper], axis=0)
-    inner, outer, block, recip, first = first_round(
+    inner, outer, outgoing, recip, first = first_round(
         odd, send, landing, incoming, remote_weights, mixed, columns
     )
-    halo, incoming = exchange(inner, outer, block)
+    halo, incoming = exchange(inner, outer, outgoing)
     (mixed,) = band_product(False, odd, offsets, target_sums, counts, inner, outer, *halo, band_weights)
     return last_round(landing, incoming, remote_weights, mixed, recip, first)
 

time: 119 us -> 131 us (1.10); the launches traced: 119 us -> 128 us
  starting transfers between devices: 30.4 us -> 44.3 us
  Pallas kernels: 49 us -> 44.8 us
    all_to_all x2, starting transfers between devices: 17.9 us -> 31.8 us  [exchange(): lax.all_to_all(outgoing, 'item', split_axis=0, concat_axis=0, tiled=True)]
    pallas_call x4 -> x2, Pallas kernels: 18.8 us -> 14.6 us  [the longest x1 8.59 us: first_round(): call(first_kernel, 3, [ANY] * 4, [ANY] * 5, [tile, tile, message, recip,...]
    all_to_all x2, waiting for transfers between devices: 31.8 us -> 27.7 us  [exchange(): lax.all_to_all(outgoing, 'item', split_axis=0, concat_axis=0, tiled=True)]
    ppermute x3, waiting for transfers between devices: 5.16 us -> 8.9 us  [swap(): lax.ppermute(outer, 'item', outer_pairs)]
  transfers between devices with their start and end apart: 8 -> 8, of which waited for: 4 -> 4; matrix products, arithmetic and copies ran while one was open for 1% -> 1% of each run, Pallas kernels for 26% -> 18%
where the time goes in v7:
time: 131 us; the launch traced here: 128 us
  Pallas kernels  44.8 us (34%)
  starting transfers between devices  44.3 us (34%)
  waiting for transfers between devices  36.6 us (28%)
  local copies, waits for them, and re-layouts  1.4 us (1%)
    all_to_all x2, starting transfers between devices, exchange(): lax.all_to_all(outgoing, 'item', split_axis=0, concat_axis=0, tiled=True)  31.8 us
    all_to_all x2, waiting for transfers between devices, exchange(): lax.all_to_all(outgoing, 'item', split_axis=0, concat_axis=0, tiled=True)  27.7 us
    pallas_call x2, Pallas kernels, band_product(): call(functools.partial(band_kernel, with_ones), 2, [ANY, whole(counts.sha...  22.7 us
    ppermute x3, waiting for transfers between devices, swap(): lax.ppermute(outer, 'item', outer_pairs)  8.9 us
    pallas_call x1, Pallas kernels, first_round(): call(first_kernel, 3, [ANY] * 4, [ANY] * 5, [tile, tile, message, recip,...  8.59 us
    ppermute x3, starting transfers between devices, swap(): lax.ppermute(outer, 'item', outer_pairs)  8.41 us
    pallas_call x1, Pallas kernels, last_round(): call(last_kernel, 1, [ANY] * 5, ANY, jax.ShapeDtypeStruct(shape, F32), sc...  7.52 us
    pallas_call x1, Pallas kernels, prep(): call(prep_kernel, 2, [ANY] * 3, [ANY] * 3, [tile, tile, message], scratch...  6.04 us
  transfers between devices with their start and end apart: 8, of which 4 were waited for; matrix products, arithmetic and copies ran while one was open for 1% of the time, Pallas kernels for 18%

profile of v7, /device:TPU:1, one launch (start us, length us, event | category | flops | bytes accessed | tf_op | source)
XLA Modules:
  0.0 128.1 jit_solution(7457024892428342789)
XLA Ops:
  0.0 6.0 %prep.1 = (bf16[48,72,128]{2,1,0:T(8,128)(2,1)}, bf16[48,72,128]{2,1,0:T(8,128)(2,1)}, bf16[128,72,128]{2,1,0:T(8,128)(2,1)}) custom-call(s32[1]{0:T(128)} %bitcast.1.odd_ref, s32[128]{0:T(128)} %bitcast.7, f32[64,12288]{1,0:T(8,128)} %ts_ref.5, s32[96,128]{1,0:T(8,128)} %bitcast.4, bf16[128,128,128]{2,1,0:T(8,128)(2,1)} %weights_ref.7), custom_call_target="tpu_custom_call" | custom-call | flops 1000000 | bytes 5000000 | tf_op jit(solution)/shard_map/prep/pallas_call | solution.py:469
  6.0 0.0 copy-start.5
  6.1 0.0 copy-start
  6.1 1.5 %collective-permute-start = (bf16[48,72,128]{2,1,0:T(8,128)(2,1)}, bf16[48,72,128]{2,1,0:T(8,128)(2,1)S(1)}, u32[]{:S(2)}, u32[]{:S(2)}) collective-permute-start(bf16[48,72,128]{2,1,0:T(8,128)(2,1)} %get-tuple-element.16.inner_ref), channel_id=1, source_target_pairs={{0,1},{1,0},{2,3},{3,2},{4,5},{5,4},{6,7},{7,6},{8,9},{9,8},{10,11... | collective-permute-start | bytes 2654216 | tf_op jit(solution)/shard_map/ppermute | solution.py:554
  7.6 3.6 %collective-permute-start.1 = (bf16[48,72,128]{2,1,0:T(8,128)(2,1)}, bf16[48,72,128]{2,1,0:T(8,128)(2,1)}, u32[]{:S(2)}, u32[]{:S(2)}) collective-permute-start(bf16[48,72,128]{2,1,0:T(8,128)(2,1)} %get-tuple-element.17.outer_ref), channel_id=1, source_target_pairs={{1,2},{2,1},{3,4},{4,3},{5,6},{6,5},{7,8},{8,7},{9,10},{10,9},{11,... | collective-permute-start | bytes 2654216 | tf_op jit(solution)/shard_map/ppermute | solution.py:554
  11.3 10.1 %all-to-all-start = ((bf16[128,72,128]{2,1,0:T(8,128)(2,1)}), bf16[128,72,128]{2,1,0:T(8,128)(2,1)}, u32[]{:S(2)}, u32[]{:S(2)}) async-start(bf16[128,72,128]{2,1,0:T(8,128)(2,1)} %get-tuple-element.15), calls=%async_computation | async-start | bytes 4718592 | tf_op jit(solution)/shard_map/all_to_all | solution.py:558
  21.3 0.1 copy.8
  21.4 0.1 reshape.19.offsets_ref
  21.6 0.7 collective-permute-done.1.from_outer_ref
  22.3 0.3 copy-done.6
  22.6 11.4 %band.2 = (f32[96,72,128]{2,1,0:T(8,128)}, f32[192,128]{1,0:T(8,128)S(1)}) custom-call(s32[1]{0:T(128)} %bitcast.1.odd_ref, s32[384]{0:T(512)S(1)} %reshape.19.offsets_ref, f32[64,12288]{1,0:T(8,128)} %ts_ref.5, s32[96,128]{1,0:T(8,128)S(1)} %bitcast.5, bf16[48,72,128]{2,1,0:T(8,128)(2,1)S(1)} %copy-done.1, bf16[48,72,128]{2,1,0:T(8,128)(2,1)S(1)} %copy-done.2, ...), custom_call_target="tpu_custom_call" | custom-call | flops 99999997952 | bytes 20000000 | tf_op jit(solution)/shard_map/band/pallas_call | solution.py:490
  34.0 1.2 collective-permute-start.2
  35.2 2.8 %collective-permute-start.3 = (f32[48,128]{1,0:T(8,128)S(1)}, f32[48,128]{1,0:T(8,128)S(1)}, u32[]{:S(2)}, u32[]{:S(2)}) collective-permute-start(f32[48,128]{1,0:T(8,128)S(1)} %get-tuple-element.26), channel_id=1, source_target_pairs={{1,2},{2,1},{3,4},{4,3},{5,6},{6,5},{7,8},{8,7},{9,10},{10,9},{11,... | collective-permute-start | bytes 73736 | tf_op jit(solution)/shard_map/ppermute | solution.py:554
  38.1 8.2 %collective-permute-done.3 = f32[48,128]{1,0:T(8,128)S(1)} collective-permute-done((f32[48,128]{1,0:T(8,128)S(1)}, f32[48,128]{1,0:T(8,128)S(1)}, u32[]{:S(2)}, u32[]{:S(2)}) %collective-permute-start.3) | collective-permute-done | bytes 24608 | tf_op jit(solution)/shard_map/ppermute | solution.py:554
  46.3 0.6 maximum_add_fusion.columns_ref
  46.9 7.1 %all-to-all-done.in_ref = bf16[128,72,128]{2,1,0:T(8,128)(2,1)} async-done(((bf16[128,72,128]{2,1,0:T(8,128)(2,1)}), bf16[128,72,128]{2,1,0:T(8,128)(2,1)}, u32[]{:S(2)}, u32[]{:S(2)}) %all-to-all-start) | async-done | bytes 2359328 | tf_op jit(solution)/shard_map/all_to_all | solution.py:558
  54.0 8.6 %first.1 = (bf16[48,72,128]{2,1,0:T(8,128)(2,1)}, bf16[48,72,128]{2,1,0:T(8,128)(2,1)}, bf16[128,72,128]{2,1,0:T(8,128)(2,1)}, f32[96,128]{1,0:T(8,128)}, f32[8,128]{1,0:T(8,128)}) custom-call(s32[1]{0:T(128)} %bitcast.1.odd_ref, s32[128]{0:T(128)} %bitcast.8, s32[128]{0:T(128)} %bitcast.9, bf16[128,72,128]{2,1,0:T(8,128)(2,1)} %all-to-all-done.in_ref, ...), custom_call_target="tpu_custom_call" | custom-call | flops 301989888 | bytes 20000000 | tf_op jit(solution)/shard_map/first/pallas_call | solution.py:520
  62.6 1.4 %collective-permute-start.4 = (bf16[48,72,128]{2,1,0:T(8,128)(2,1)}, bf16[48,72,128]{2,1,0:T(8,128)(2,1)S(1)}, u32[]{:S(2)}, u32[]{:S(2)}) collective-permute-start(bf16[48,72,128]{2,1,0:T(8,128)(2,1)} %get-tuple-element.21.inner_ref), channel_id=1, source_target_pairs={{0,1},{1,0},{2,3},{3,2},{4,5},{5,4},{6,7},{7,6},{8,9},{9,8},{10,11... | collective-permute-start | bytes 2654216 | tf_op jit(solution)/shard_map/ppermute | solution.py:554
  64.0 1.9 %collective-permute-start.5 = (bf16[48,72,128]{2,1,0:T(8,128)(2,1)}, bf16[48,72,128]{2,1,0:T(8,128)(2,1)}, u32[]{:S(2)}, u32[]{:S(2)}) collective-permute-start(bf16[48,72,128]{2,1,0:T(8,128)(2,1)} %get-tuple-element.22.outer_ref), channel_id=1, source_target_pairs={{1,2},{2,1},{3,4},{4,3},{5,6},{6,5},{7,8},{8,7},{9,10},{10,9},{11,... | collective-permute-start | bytes 2654216 | tf_op jit(solution)/shard_map/ppermute | solution.py:554
  65.9 21.8 %all-to-all-start.1 = ((bf16[128,72,128]{2,1,0:T(8,128)(2,1)}), bf16[128,72,128]{2,1,0:T(8,128)(2,1)}, u32[]{:S(2)}, u32[]{:S(2)}) async-start(bf16[128,72,128]{2,1,0:T(8,128)(2,1)} %get-tuple-element.20), calls=%async_computation.1 | async-start | bytes 4718592 | tf_op jit(solution)/shard_map/all_to_all | solution.py:558
  87.8 0.9 copy-done.7
  88.6 11.2 %band.3.band_ref = f32[96,72,128]{2,1,0:T(8,128)} custom-call(s32[1]{0:T(128)} %bitcast.1.odd_ref, s32[384]{0:T(512)S(1)} %reshape.19.offsets_ref, f32[64,12288]{1,0:T(8,128)} %ts_ref.5, s32[96,128]{1,0:T(8,128)S(1)} %bitcast.6, bf16[48,72,128]{2,1,0:T(8,128)(2,1)S(1)} %copy-done.3, bf16[48,72,128]{2,1,0:T(8,128)(2,1)S(1)} %copy-done.4, ...), custom_call_target="tpu_custom_call" | custom-call | flops 99999997952 | bytes 20000000 | tf_op jit(solution)/shard_map/band/pallas_call | solution.py:490
  99.9 20.5 %all-to-all-done.1.in_ref = bf16[128,72,128]{2,1,0:T(8,128)(2,1)} async-done(((bf16[128,72,128]{2,1,0:T(8,128)(2,1)}), bf16[128,72,128]{2,1,0:T(8,128)(2,1)}, u32[]{:S(2)}, u32[]{:S(2)}) %all-to-all-start.1) | async-done | bytes 2359328 | tf_op jit(solution)/shard_map/all_to_all | solution.py:558
  120.4 7.5 %last.1 = f32[64,12288]{1,0:T(8,128)} custom-call(s32[128]{0:T(128)} %bitcast.10, bf16[128,72,128]{2,1,0:T(8,128)(2,1)} %all-to-all-done.1.in_ref, bf16[128,128,128]{2,1,0:T(8,128)(2,1)} %weights_ref.7, f32[96,72,128]{2,1,0:T(8,128)} %band.3.band_ref, f32[96,128]{1,0:T(8,128)} %get-tuple-element.23.recip_ref, f32[8,128]{1,0:T(8,128)} %get-tuple-element.24.first_ref), custom_call_target="tpu_custom_call" | custom-call | flops 301989888 | bytes 20000000 | tf_op jit(solution)/shard_map/last/pallas_call | solution.py:536
  (18 shorter events, 0.1 us)
Async XLA Ops:
  6.0 15.3 %copy-start.5 = (s32[96,4]{0,1:T(4,128)S(1)}, s32[96,4]{0,1:T(4,128)}, u32[]{:S(2)}) copy-start(s32[96,4]{0,1:T(4,128)} %param.9) | copy-start | bytes 4612
  6.1 16.5 %copy-start = (s32[12288]{0:T(1024)S(1)}, s32[12288]{0:T(1024)}, u32[]{:S(2)}) copy-start(s32[12288]{0:T(1024)} %param.8) | copy-start | bytes 147460
  6.1 16.5 %copy-start.1 = (bf16[48,72,128]{2,1,0:T(8,128)(2,1)S(1)}, bf16[48,72,128]{2,1,0:T(8,128)(2,1)}, u32[]{:S(2)}) copy-start(bf16[48,72,128]{2,1,0:T(8,128)(2,1)} %get-tuple-element.16.inner_ref) | copy-start | bytes 2654212
  6.1 16.5 %copy-start.2 = (bf16[48,72,128]{2,1,0:T(8,128)(2,1)S(1)}, bf16[48,72,128]{2,1,0:T(8,128)(2,1)}, u32[]{:S(2)}) copy-start(bf16[48,72,128]{2,1,0:T(8,128)(2,1)} %get-tuple-element.17.outer_ref) | copy-start | bytes 2654212
  6.1 15.5 %collective-permute-start = (bf16[48,72,128]{2,1,0:T(8,128)(2,1)}, bf16[48,72,128]{2,1,0:T(8,128)(2,1)S(1)}, u32[]{:S(2)}, u32[]{:S(2)}) collective-permute-start(bf16[48,72,128]{2,1,0:T(8,128)(2,1)} %get-tuple-element.16.inner_ref), channel_id=1, source_target_pairs={{0,1},{1,0},{2,3},{3,2},{4,5},{5,4},{6,7},{7,6},{8,9},{9,8},{10,11... | collective-permute-start | bytes 2654216 | tf_op jit(solution)/shard_map/ppermute | solution.py:554
  7.6 14.7 %collective-permute-start.1 = (bf16[48,72,128]{2,1,0:T(8,128)(2,1)}, bf16[48,72,128]{2,1,0:T(8,128)(2,1)}, u32[]{:S(2)}, u32[]{:S(2)}) collective-permute-start(bf16[48,72,128]{2,1,0:T(8,128)(2,1)} %get-tuple-element.17.outer_ref), channel_id=1, source_target_pairs={{1,2},{2,1},{3,4},{4,3},{5,6},{6,5},{7,8},{8,7},{9,10},{10,9},{11,... | collective-permute-start | bytes 2654216 | tf_op jit(solution)/shard_map/ppermute | solution.py:554
  11.3 42.8 %all-to-all-start = ((bf16[128,72,128]{2,1,0:T(8,128)(2,1)}), bf16[128,72,128]{2,1,0:T(8,128)(2,1)}, u32[]{:S(2)}, u32[]{:S(2)}) async-start(bf16[128,72,128]{2,1,0:T(8,128)(2,1)} %get-tuple-element.15), calls=%async_computation | async-start | bytes 4718592 | tf_op jit(solution)/shard_map/all_to_all | solution.py:558
  21.6 1.0 copy-start.6
  34.0 4.1 %collective-permute-start.2 = (f32[48,128]{1,0:T(8,128)S(1)}, f32[48,128]{1,0:T(8,128)S(1)}, u32[]{:S(2)}, u32[]{:S(2)}) collective-permute-start(f32[48,128]{1,0:T(8,128)S(1)} %get-tuple-element.25), channel_id=1, source_target_pairs={{0,1},{1,0},{2,3},{3,2},{4,5},{5,4},{6,7},{7,6},{8,9},{9,8},{10,11... | collective-permute-start | bytes 73736 | tf_op jit(solution)/shard_map/ppermute | solution.py:554
  35.2 11.0 %collective-permute-start.3 = (f32[48,128]{1,0:T(8,128)S(1)}, f32[48,128]{1,0:T(8,128)S(1)}, u32[]{:S(2)}, u32[]{:S(2)}) collective-permute-start(f32[48,128]{1,0:T(8,128)S(1)} %get-tuple-element.26), channel_id=1, source_target_pairs={{1,2},{2,1},{3,4},{4,3},{5,6},{6,5},{7,8},{8,7},{9,10},{10,9},{11,... | collective-permute-start | bytes 73736 | tf_op jit(solution)/shard_map/ppermute | solution.py:554
  62.6 26.0 %copy-start.3 = (bf16[48,72,128]{2,1,0:T(8,128)(2,1)S(1)}, bf16[48,72,128]{2,1,0:T(8,128)(2,1)}, u32[]{:S(2)}) copy-start(bf16[48,72,128]{2,1,0:T(8,128)(2,1)} %get-tuple-element.21.inner_ref) | copy-start | bytes 2654212
  62.6 26.0 %copy-start.4 = (bf16[48,72,128]{2,1,0:T(8,128)(2,1)S(1)}, bf16[48,72,128]{2,1,0:T(8,128)(2,1)}, u32[]{:S(2)}) copy-start(bf16[48,72,128]{2,1,0:T(8,128)(2,1)} %get-tuple-element.22.outer_ref) | copy-start | bytes 2654212
  62.6 25.1 %collective-permute-start.4 = (bf16[48,72,128]{2,1,0:T(8,128)(2,1)}, bf16[48,72,128]{2,1,0:T(8,128)(2,1)S(1)}, u32[]{:S(2)}, u32[]{:S(2)}) collective-permute-start(bf16[48,72,128]{2,1,0:T(8,128)(2,1)} %get-tuple-element.21.inner_ref), channel_id=1, source_target_pairs={{0,1},{1,0},{2,3},{3,2},{4,5},{5,4},{6,7},{7,6},{8,9},{9,8},{10,11... | collective-permute-start | bytes 2654216 | tf_op jit(solution)/shard_map/ppermute | solution.py:554
  64.0 23.7 %collective-permute-start.5 = (bf16[48,72,128]{2,1,0:T(8,128)(2,1)}, bf16[48,72,128]{2,1,0:T(8,128)(2,1)}, u32[]{:S(2)}, u32[]{:S(2)}) collective-permute-start(bf16[48,72,128]{2,1,0:T(8,128)(2,1)} %get-tuple-element.22.outer_ref), channel_id=1, source_target_pairs={{1,2},{2,1},{3,4},{4,3},{5,6},{6,5},{7,8},{8,7},{9,10},{10,9},{11,... | collective-permute-start | bytes 2654216 | tf_op jit(solution)/shard_map/ppermute | solution.py:554
  65.9 54.5 %all-to-all-start.1 = ((bf16[128,72,128]{2,1,0:T(8,128)(2,1)}), bf16[128,72,128]{2,1,0:T(8,128)(2,1)}, u32[]{:S(2)}, u32[]{:S(2)}) async-start(bf16[128,72,128]{2,1,0:T(8,128)(2,1)} %get-tuple-element.20), calls=%async_computation.1 | async-start | bytes 4718592 | tf_op jit(solution)/shard_map/all_to_all | solution.py:558
  87.7 0.9 copy-start.7

commit v8 on v6

--- a/solution.py
+++ b/solution.py
@@ -20,7 +20,7 @@
 VMEM = 60
 VMEM_ROUND = 60
 VMEM_BAND = 52
-AHEAD = 3
+AHEAD = 5
 
 
 def pieces(value, count):

time: 119 us -> 119 us (level)
  no operation moved by 1% of the time
where the time goes in v8:
time: 119 us; the launch traced here: 118 us
  Pallas kernels  48.9 us (41%)
  waiting for transfers between devices  37 us (31%)
  starting transfers between devices  30.4 us (26%)
    all_to_all x2, waiting for transfers between devices, exchange(): lax.all_to_all(outgoing, 'item', split_axis=0, concat_axis=0, tiled=True)  31.8 us
    pallas_call x2, Pallas kernels, band_product(): call(functools.partial(band_kernel, with_ones), 2, [ANY, whole(counts.sha...  22.7 us
    all_to_all x2, starting transfers between devices, exchange(): lax.all_to_all(outgoing, 'item', split_axis=0, concat_axis=0, tiled=True)  17.9 us
    pallas_call x2, Pallas kernels, fill_messages(): call(functools.partial(message_kernel, remote_weights is not None), 2, [A...  8.22 us
    ppermute x3, starting transfers between devices, swap(): lax.ppermute(outer, 'item', outer_pairs)  8.12 us
    pallas_call x1, Pallas kernels, first_round(): call(first_kernel, 3, [ANY] * 4, [ANY] * 5, [tile, tile, first, recip, fi...  7.85 us
    pallas_call x1, Pallas kernels, last_round(): call(last_kernel, 1, [ANY] * 5, ANY, jax.ShapeDtypeStruct(shape, F32), sc...  7.3 us
    ppermute x3, waiting for transfers between devices, swap(): lax.ppermute(outer, 'item', outer_pairs)  5.16 us
  transfers between devices with their start and end apart: 8, of which 4 were waited for; matrix products, arithmetic and copies ran while one was open for 1% of the time, Pallas kernels for 26%

profile of v8, /device:TPU:1, one launch (start us, length us, event | category | flops | bytes accessed | tf_op | source)
XLA Modules:
  0.0 118.4 jit_solution(5011728279895071758)
XLA Ops:
  0.0 2.8 %prep.1 = (bf16[48,72,128]{2,1,0:T(8,128)(2,1)}, bf16[48,72,128]{2,1,0:T(8,128)(2,1)}, f32[8,128]{1,0:T(8,128)}) custom-call(s32[1]{0:T(128)} %bitcast.1.odd_ref, f32[64,12288]{1,0:T(8,128)} %ts_ref.5, s32[96,128]{1,0:T(8,128)} %bitcast.4), custom_call_target="tpu_custom_call" | custom-call | flops 1000000 | bytes 5000000 | tf_op jit(solution)/shard_map/prep/pallas_call | solution.py:488
  2.8 1.5 %collective-permute-start = (bf16[48,72,128]{2,1,0:T(8,128)(2,1)}, bf16[48,72,128]{2,1,0:T(8,128)(2,1)S(1)}, u32[]{:S(2)}, u32[]{:S(2)}) collective-permute-start(bf16[48,72,128]{2,1,0:T(8,128)(2,1)} %get-tuple-element.15.inner_ref), channel_id=1, source_target_pairs={{0,1},{1,0},{2,3},{3,2},{4,5},{5,4},{6,7},{7,6},{8,9},{9,8},{10,11... | collective-permute-start | bytes 2654216 | tf_op jit(solution)/shard_map/ppermute | solution.py:595
  4.4 3.5 %collective-permute-start.1 = (bf16[48,72,128]{2,1,0:T(8,128)(2,1)}, bf16[48,72,128]{2,1,0:T(8,128)(2,1)}, u32[]{:S(2)}, u32[]{:S(2)}) collective-permute-start(bf16[48,72,128]{2,1,0:T(8,128)(2,1)} %get-tuple-element.16.outer_ref), channel_id=1, source_target_pairs={{1,2},{2,1},{3,4},{4,3},{5,6},{6,5},{7,8},{8,7},{9,10},{10,9},{11,... | collective-permute-start | bytes 2654216 | tf_op jit(solution)/shard_map/ppermute | solution.py:595
  7.9 4.5 %messages.2 = bf16[128,72,128]{2,1,0:T(8,128)(2,1)} custom-call(s32[1]{0:T(128)} %bitcast.1.odd_ref, s32[128]{0:T(128)} %bitcast.7, bf16[48,72,128]{2,1,0:T(8,128)(2,1)} %get-tuple-element.15.inner_ref, bf16[48,72,128]{2,1,0:T(8,128)(2,1)} %get-tuple-element.16.outer_ref, f32[8,128]{1,0:T(8,128)} %get-tuple-element.17.block_ref, ...), custom_call_target="tpu_custom_call" | custom-call | flops 1000000 | bytes 5000000 | tf_op jit(solution)/shard_map/messages/pallas_call | solution.py:509
  12.5 0.0 copy-start.4
  12.5 10.1 %all-to-all-start = ((bf16[128,72,128]{2,1,0:T(8,128)(2,1)}), bf16[128,72,128]{2,1,0:T(8,128)(2,1)}, u32[]{:S(2)}, u32[]{:S(2)}) async-start(bf16[128,72,128]{2,1,0:T(8,128)(2,1)} %messages.2), calls=%async_computation | async-start | bytes 4718592 | tf_op jit(solution)/shard_map/all_to_all | solution.py:600
  22.6 0.1 copy.8
  22.7 0.1 reshape.19.offsets_ref
  22.8 0.9 copy-done.6
  23.7 11.4 %band.2 = (f32[96,72,128]{2,1,0:T(8,128)}, f32[192,128]{1,0:T(8,128)S(1)}) custom-call(s32[1]{0:T(128)} %bitcast.1.odd_ref, s32[384]{0:T(512)S(1)} %reshape.19.offsets_ref, f32[64,12288]{1,0:T(8,128)} %ts_ref.5, s32[96,128]{1,0:T(8,128)S(1)} %bitcast.5, bf16[48,72,128]{2,1,0:T(8,128)(2,1)S(1)} %copy-done, bf16[48,72,128]{2,1,0:T(8,128)(2,1)S(1)} %copy-done.1, ...), custom_call_target="tpu_custom_call" | custom-call | flops 99999997952 | bytes 20000000 | tf_op jit(solution)/shard_map/band/pallas_call | solution.py:531
  35.2 1.2 %collective-permute-start.2 = (f32[48,128]{1,0:T(8,128)S(1)}, f32[48,128]{1,0:T(8,128)S(1)}, u32[]{:S(2)}, u32[]{:S(2)}) collective-permute-start(f32[48,128]{1,0:T(8,128)S(1)} %get-tuple-element.25), channel_id=1, source_target_pairs={{0,1},{1,0},{2,3},{3,2},{4,5},{5,4},{6,7},{7,6},{8,9},{9,8},{10,11... | collective-permute-start | bytes 73736 | tf_op jit(solution)/shard_map/ppermute | solution.py:595
  36.4 2.7 %collective-permute-start.3 = (f32[48,128]{1,0:T(8,128)S(1)}, f32[48,128]{1,0:T(8,128)S(1)}, u32[]{:S(2)}, u32[]{:S(2)}) collective-permute-start(f32[48,128]{1,0:T(8,128)S(1)} %get-tuple-element.26), channel_id=1, source_target_pairs={{1,2},{2,1},{3,4},{4,3},{5,6},{6,5},{7,8},{8,7},{9,10},{10,9},{11,... | collective-permute-start | bytes 73736 | tf_op jit(solution)/shard_map/ppermute | solution.py:595
  39.1 4.0 %collective-permute-done.3 = f32[48,128]{1,0:T(8,128)S(1)} collective-permute-done((f32[48,128]{1,0:T(8,128)S(1)}, f32[48,128]{1,0:T(8,128)S(1)}, u32[]{:S(2)}, u32[]{:S(2)}) %collective-permute-start.3) | collective-permute-done | bytes 24608 | tf_op jit(solution)/shard_map/ppermute | solution.py:595
  43.1 0.6 maximum_add_fusion.columns_ref
  43.7 11.6 %all-to-all-done.in_ref = bf16[128,72,128]{2,1,0:T(8,128)(2,1)} async-done(((bf16[128,72,128]{2,1,0:T(8,128)(2,1)}), bf16[128,72,128]{2,1,0:T(8,128)(2,1)}, u32[]{:S(2)}, u32[]{:S(2)}) %all-to-all-start) | async-done | bytes 2359328 | tf_op jit(solution)/shard_map/all_to_all | solution.py:600
  55.3 7.9 %first.1 = (bf16[48,72,128]{2,1,0:T(8,128)(2,1)}, bf16[48,72,128]{2,1,0:T(8,128)(2,1)}, f32[8,128]{1,0:T(8,128)}, f32[96,128]{1,0:T(8,128)}, f32[8,128]{1,0:T(8,128)}) custom-call(s32[1]{0:T(128)} %bitcast.1.odd_ref, s32[128]{0:T(128)} %bitcast.8, s32[128]{0:T(128)} %bitcast.10, bf16[128,72,128]{2,1,0:T(8,128)(2,1)} %all-to-all-done.in_ref, ...), custom_call_target="tpu_custom_call" | custom-call | flops 301989888 | bytes 20000000 | tf_op jit(solution)/shard_map/first/pallas_call | solution.py:561
  63.1 1.6 %collective-permute-start.4 = (bf16[48,72,128]{2,1,0:T(8,128)(2,1)}, bf16[48,72,128]{2,1,0:T(8,128)(2,1)S(1)}, u32[]{:S(2)}, u32[]{:S(2)}) collective-permute-start(bf16[48,72,128]{2,1,0:T(8,128)(2,1)} %get-tuple-element.20.inner_ref), channel_id=1, source_target_pairs={{0,1},{1,0},{2,3},{3,2},{4,5},{5,4},{6,7},{7,6},{8,9},{9,8},{10,11... | collective-permute-start | bytes 2654216 | tf_op jit(solution)/shard_map/ppermute | solution.py:595
  64.8 1.9 %collective-permute-start.5 = (bf16[48,72,128]{2,1,0:T(8,128)(2,1)}, bf16[48,72,128]{2,1,0:T(8,128)(2,1)}, u32[]{:S(2)}, u32[]{:S(2)}) collective-permute-start(bf16[48,72,128]{2,1,0:T(8,128)(2,1)} %get-tuple-element.21.outer_ref), channel_id=1, source_target_pairs={{1,2},{2,1},{3,4},{4,3},{5,6},{6,5},{7,8},{8,7},{9,10},{10,9},{11,... | collective-permute-start | bytes 2654216 | tf_op jit(solution)/shard_map/ppermute | solution.py:595
  66.7 3.7 %messages.3 = bf16[128,72,128]{2,1,0:T(8,128)(2,1)} custom-call(s32[1]{0:T(128)} %bitcast.1.odd_ref, s32[128]{0:T(128)} %bitcast.9, bf16[48,72,128]{2,1,0:T(8,128)(2,1)} %get-tuple-element.20.inner_ref, bf16[48,72,128]{2,1,0:T(8,128)(2,1)} %get-tuple-element.21.outer_ref, f32[8,128]{1,0:T(8,128)} %get-tuple-element.22.block_ref), custom_call_target="tpu_custom_call" | custom-call | flops 1000000 | bytes 5000000 | tf_op jit(solution)/shard_map/messages/pallas_call | solution.py:509
  70.4 7.8 %all-to-all-start.1 = ((bf16[128,72,128]{2,1,0:T(8,128)(2,1)}), bf16[128,72,128]{2,1,0:T(8,128)(2,1)}, u32[]{:S(2)}, u32[]{:S(2)}) async-start(bf16[128,72,128]{2,1,0:T(8,128)(2,1)} %messages.3), calls=%async_computation.1 | async-start | bytes 4718592 | tf_op jit(solution)/shard_map/all_to_all | solution.py:600
  78.2 1.2 %collective-permute-done.5.from_outer_ref = bf16[48,72,128]{2,1,0:T(8,128)(2,1)} collective-permute-done((bf16[48,72,128]{2,1,0:T(8,128)(2,1)}, bf16[48,72,128]{2,1,0:T(8,128)(2,1)}, u32[]{:S(2)}, u32[]{:S(2)}) %collective-permute-start.5) | collective-permute-done | bytes 884768 | tf_op jit(solution)/shard_map/ppermute | solution.py:595
  79.4 11.2 %band.3.band_ref = f32[96,72,128]{2,1,0:T(8,128)} custom-call(s32[1]{0:T(128)} %bitcast.1.odd_ref, s32[384]{0:T(512)S(1)} %reshape.19.offsets_ref, f32[64,12288]{1,0:T(8,128)} %ts_ref.5, s32[96,128]{1,0:T(8,128)S(1)} %bitcast.6, bf16[48,72,128]{2,1,0:T(8,128)(2,1)S(1)} %copy-done.2, bf16[48,72,128]{2,1,0:T(8,128)(2,1)S(1)} %copy-done.3, ...), custom_call_target="tpu_custom_call" | custom-call | flops 99999997952 | bytes 20000000 | tf_op jit(solution)/shard_map/band/pallas_call | solution.py:531
  90.7 20.2 %all-to-all-done.1.in_ref = bf16[128,72,128]{2,1,0:T(8,128)(2,1)} async-done(((bf16[128,72,128]{2,1,0:T(8,128)(2,1)}), bf16[128,72,128]{2,1,0:T(8,128)(2,1)}, u32[]{:S(2)}, u32[]{:S(2)}) %all-to-all-start.1) | async-done | bytes 2359328 | tf_op jit(solution)/shard_map/all_to_all | solution.py:600
  110.9 7.3 %last.1 = f32[64,12288]{1,0:T(8,128)} custom-call(s32[128]{0:T(128)} %bitcast.11, bf16[128,72,128]{2,1,0:T(8,128)(2,1)} %all-to-all-done.1.in_ref, bf16[128,128,128]{2,1,0:T(8,128)(2,1)} %weights_ref.7, f32[96,72,128]{2,1,0:T(8,128)} %band.3.band_ref, f32[96,128]{1,0:T(8,128)} %get-tuple-element.23.recip_ref, f32[8,128]{1,0:T(8,128)} %get-tuple-element.24.first_ref), custom_call_target="tpu_custom_call" | custom-call | flops 301989888 | bytes 20000000 | tf_op jit(solution)/shard_map/last/pallas_call | solution.py:577
  (20 shorter events, 0.1 us)
Async XLA Ops:
  2.8 19.9 %collective-permute-start = (bf16[48,72,128]{2,1,0:T(8,128)(2,1)}, bf16[48,72,128]{2,1,0:T(8,128)(2,1)S(1)}, u32[]{:S(2)}, u32[]{:S(2)}) collective-permute-start(bf16[48,72,128]{2,1,0:T(8,128)(2,1)} %get-tuple-element.15.inner_ref), channel_id=1, source_target_pairs={{0,1},{1,0},{2,3},{3,2},{4,5},{5,4},{6,7},{7,6},{8,9},{9,8},{10,11... | collective-permute-start | bytes 2654216 | tf_op jit(solution)/shard_map/ppermute | solution.py:595
  4.4 18.4 %collective-permute-start.1 = (bf16[48,72,128]{2,1,0:T(8,128)(2,1)}, bf16[48,72,128]{2,1,0:T(8,128)(2,1)}, u32[]{:S(2)}, u32[]{:S(2)}) collective-permute-start(bf16[48,72,128]{2,1,0:T(8,128)(2,1)} %get-tuple-element.16.outer_ref), channel_id=1, source_target_pairs={{1,2},{2,1},{3,4},{4,3},{5,6},{6,5},{7,8},{8,7},{9,10},{10,9},{11,... | collective-permute-start | bytes 2654216 | tf_op jit(solution)/shard_map/ppermute | solution.py:595
  12.4 10.1 %copy-start.5 = (s32[96,4]{0,1:T(4,128)S(1)}, s32[96,4]{0,1:T(4,128)}, u32[]{:S(2)}) copy-start(s32[96,4]{0,1:T(4,128)} %param.9) | copy-start | bytes 4612
  12.4 11.3 %copy-start = (bf16[48,72,128]{2,1,0:T(8,128)(2,1)S(1)}, bf16[48,72,128]{2,1,0:T(8,128)(2,1)}, u32[]{:S(2)}) copy-start(bf16[48,72,128]{2,1,0:T(8,128)(2,1)} %get-tuple-element.15.inner_ref) | copy-start | bytes 2654212
  12.5 11.3 %copy-start.1 = (bf16[48,72,128]{2,1,0:T(8,128)(2,1)S(1)}, bf16[48,72,128]{2,1,0:T(8,128)(2,1)}, u32[]{:S(2)}) copy-start(bf16[48,72,128]{2,1,0:T(8,128)(2,1)} %get-tuple-element.16.outer_ref) | copy-start | bytes 2654212
  12.5 11.3 %copy-start.4 = (s32[12288]{0:T(1024)S(1)}, s32[12288]{0:T(1024)}, u32[]{:S(2)}) copy-start(s32[12288]{0:T(1024)} %param.8) | copy-start | bytes 147460
  12.5 42.8 %all-to-all-start = ((bf16[128,72,128]{2,1,0:T(8,128)(2,1)}), bf16[128,72,128]{2,1,0:T(8,128)(2,1)}, u32[]{:S(2)}, u32[]{:S(2)}) async-start(bf16[128,72,128]{2,1,0:T(8,128)(2,1)} %messages.2), calls=%async_computation | async-start | bytes 4718592 | tf_op jit(solution)/shard_map/all_to_all | solution.py:600
  22.8 0.9 copy-start.6
  35.2 3.9 %collective-permute-start.2 = (f32[48,128]{1,0:T(8,128)S(1)}, f32[48,128]{1,0:T(8,128)S(1)}, u32[]{:S(2)}, u32[]{:S(2)}) collective-permute-start(f32[48,128]{1,0:T(8,128)S(1)} %get-tuple-element.25), channel_id=1, source_target_pairs={{0,1},{1,0},{2,3},{3,2},{4,5},{5,4},{6,7},{7,6},{8,9},{9,8},{10,11... | collective-permute-start | bytes 73736 | tf_op jit(solution)/shard_map/ppermute | solution.py:595
  36.4 6.7 %collective-permute-start.3 = (f32[48,128]{1,0:T(8,128)S(1)}, f32[48,128]{1,0:T(8,128)S(1)}, u32[]{:S(2)}, u32[]{:S(2)}) collective-permute-start(f32[48,128]{1,0:T(8,128)S(1)} %get-tuple-element.26), channel_id=1, source_target_pairs={{1,2},{2,1},{3,4},{4,3},{5,6},{6,5},{7,8},{8,7},{9,10},{10,9},{11,... | collective-permute-start | bytes 73736 | tf_op jit(solution)/shard_map/ppermute | solution.py:595
  63.1 15.1 %collective-permute-start.4 = (bf16[48,72,128]{2,1,0:T(8,128)(2,1)}, bf16[48,72,128]{2,1,0:T(8,128)(2,1)S(1)}, u32[]{:S(2)}, u32[]{:S(2)}) collective-permute-start(bf16[48,72,128]{2,1,0:T(8,128)(2,1)} %get-tuple-element.20.inner_ref), channel_id=1, source_target_pairs={{0,1},{1,0},{2,3},{3,2},{4,5},{5,4},{6,7},{7,6},{8,9},{9,8},{10,11... | collective-permute-start | bytes 2654216 | tf_op jit(solution)/shard_map/ppermute | solution.py:595
  64.8 14.7 %collective-permute-start.5 = (bf16[48,72,128]{2,1,0:T(8,128)(2,1)}, bf16[48,72,128]{2,1,0:T(8,128)(2,1)}, u32[]{:S(2)}, u32[]{:S(2)}) collective-permute-start(bf16[48,72,128]{2,1,0:T(8,128)(2,1)} %get-tuple-element.21.outer_ref), channel_id=1, source_target_pairs={{1,2},{2,1},{3,4},{4,3},{5,6},{6,5},{7,8},{8,7},{9,10},{10,9},{11,... | collective-permute-start | bytes 2654216 | tf_op jit(solution)/shard_map/ppermute | solution.py:595
  70.4 9.0 %copy-start.2 = (bf16[48,72,128]{2,1,0:T(8,128)(2,1)S(1)}, bf16[48,72,128]{2,1,0:T(8,128)(2,1)}, u32[]{:S(2)}) copy-start(bf16[48,72,128]{2,1,0:T(8,128)(2,1)} %get-tuple-element.20.inner_ref) | copy-start | bytes 2654212
  70.4 9.0 %copy-start.3 = (bf16[48,72,128]{2,1,0:T(8,128)(2,1)S(1)}, bf16[48,72,128]{2,1,0:T(8,128)(2,1)}, u32[]{:S(2)}) copy-start(bf16[48,72,128]{2,1,0:T(8,128)(2,1)} %get-tuple-element.21.outer_ref) | copy-start | bytes 2654212
  70.4 40.5 %all-to-all-start.1 = ((bf16[128,72,128]{2,1,0:T(8,128)(2,1)}), bf16[128,72,128]{2,1,0:T(8,128)(2,1)}, u32[]{:S(2)}, u32[]{:S(2)}) async-start(bf16[128,72,128]{2,1,0:T(8,128)(2,1)} %messages.3), calls=%async_computation.1 | async-start | bytes 4718592 | tf_op jit(solution)/shard_map/all_to_all | solution.py:600
  78.2 1.2 %copy-start.7 = (bf16[48,72,128]{2,1,0:T(8,128)(2,1)}, bf16[48,72,128]{2,1,0:T(8,128)(2,1)S(1)}, u32[]{:S(2)}) copy-start(bf16[48,72,128]{2,1,0:T(8,128)(2,1)S(1)} %collective-permute-done.4.from_inner_ref) | copy-start | bytes 2654212
